TPU v7x, 32 devices: a whole 2x2x4 slice. The times are simulated.
32 devices in a mesh: seq: 8 (over y, x, core), batch: 4 (over z).
Axes of the slice: x: 2, y: 2, z: 4, core: 2. Of those that a mesh axis runs over, the one named last changes fastest.
Arguments:
- tokens: bfloat16 [16, 2048, 512], P('batch', 'seq'), may hold values from -33 to 33
- lengths: int32 [16], P('batch'), may hold values from 512 to 2048, as said below
- cotangent: bfloat16 [16, 2048, 512], P('batch', 'seq'), may hold values from -6 to 6
- norm_gain: float32 [2, 512], replicated, may hold values from 0.5 to 1.5
- norm_shift: float32 [2, 512], replicated, may hold values from -1.75 to 1.75
- lift_weight: bfloat16 [2, 512, 512], replicated, may hold values from -0.25 to 0.25
- decay_log: float32 [2, 256], replicated, may hold values from -9.5 to -3.4
- phase_log: float32 [2, 256], replicated, may hold values from -7 to 1
- skip_gain: float32 [2, 512], replicated, may hold values from -3 to 3
- mix_weight: bfloat16 [2, 512, 512], replicated, may hold values from -0.25 to 0.25
- glu_weight: bfloat16 [2, 512, 1024], replicated, may hold values from -0.25 to 0.25
- glu_bias: float32 [2, 1024], replicated, may hold values from -1.75 to 1.75
Outputs:
- produced: bfloat16 [16, 2048, 512], P('batch', 'seq')
- input_grad: bfloat16 [16, 2048, 512], P('batch', 'seq')
- grad_norm_gain: float32 [2, 512], replicated
- grad_norm_shift: float32 [2, 512], replicated
- grad_lift: float32 [2, 512, 512], replicated
- grad_decay: float32 [2, 256], replicated
- grad_phase: float32 [2, 256], replicated
- grad_skip: float32 [2, 512], replicated
- grad_mix: float32 [2, 512, 512], replicated
- grad_glu: float32 [2, 512, 1024], replicated
- grad_glu_bias: float32 [2, 1024], replicated
Inputs may be any that keep to these rules, and one draw needn't show every extreme that they name: `lengths`: each group of 4 sequences on one index of batch holds one of length 2048, which one drawn from the seed.
All inputs are finite; a program needn't handle non-finite values.
Results may differ from a plain program's by a relative error of at most 0.015.
Values may be sent and summed in bfloat16 or wider, within the bound.
No kernel may reach another device: no remote copies, remote signals or barrier semaphores. Data moves between devices by JAX's collectives and lax.ppermute only.
A program may use at most 192 MiB of HBM per device.

v0:
```python
from functools import partial
import math

import jax
import jax.numpy as jnp
from jax import lax
from jax.sharding import PartitionSpec as P

norm_eps = 1e-05


def complex_step(earlier, later):
    carry_real, carry_imaginary, state_real, state_imaginary = earlier
    factor_real, factor_imaginary, input_real, input_imaginary = later
    return (
        factor_real * carry_real - factor_imaginary * carry_imaginary,
        factor_real * carry_imaginary + factor_imaginary * carry_real,
        factor_real * state_real - factor_imaginary * state_imaginary + input_real,
        factor_real * state_imaginary + factor_imaginary * state_real + input_imaginary,
    )


def rotation_decay(decay_log, phase_log):
    decay_rate = jnp.exp(decay_log)
    magnitude = jnp.exp(-decay_rate)
    phase_angle = jnp.exp(phase_log)
    return (
        magnitude * jnp.cos(phase_angle),
        magnitude * jnp.sin(phase_angle),
        jnp.sqrt(1.0 - jnp.exp(-2.0 * decay_rate)),
    )


def valid_at(lengths, time_start, time_span):
    places = time_start + jnp.arange(time_span, dtype=jnp.int32)
    return (places[None, :] < lengths[:, None]).astype(jnp.float32)


def linear_chain(
    decay_rate, phase_angle, step_mask, input_real, input_imaginary, backwards, adjoint
):
    span, seq_count, share = input_real.shape
    stride = math.gcd(64, span)
    tracts = span // stride
    tracted_shape = (tracts, stride, seq_count, share)
    mask_blocks = step_mask.reshape(tracts, stride, seq_count, 1)
    counts = lax.cumsum(mask_blocks, axis=1, reverse=backwards)
    rotation_rate = -phase_angle if adjoint else phase_angle
    magnitude = jnp.exp(-decay_rate * counts)
    growth = jnp.exp(decay_rate * counts)
    phase_now = rotation_rate * counts
    cosine = jnp.cos(phase_now)
    sine = jnp.sin(phase_now)
    power_real = magnitude * cosine
    power_imaginary = magnitude * sine
    drive_real = input_real.reshape(tracted_shape)
    drive_imaginary = input_imaginary.reshape(tracted_shape)
    weighted_real = growth * (cosine * drive_real + sine * drive_imaginary)
    weighted_imaginary = growth * (cosine * drive_imaginary - sine * drive_real)
    running_real = lax.cumsum(weighted_real, axis=1, reverse=backwards)
    running_imaginary = lax.cumsum(weighted_imaginary, axis=1, reverse=backwards)
    local_real = power_real * running_real - power_imaginary * running_imaginary
    local_imaginary = power_real * running_imaginary + power_imaginary * running_real
    edge_index = 0 if backwards else stride - 1
    summary = (
        power_real[:, edge_index],
        power_imaginary[:, edge_index],
        local_real[:, edge_index],
        local_imaginary[:, edge_index],
    )
    inclusive = lax.associative_scan(complex_step, summary, reverse=backwards, axis=0)
    unit_row = jnp.ones_like(summary[2][:1])
    zero_row = jnp.zeros_like(summary[2][:1])
    identity_rows = (unit_row, zero_row, zero_row, zero_row)
    if backwards:
        exclusive = tuple(
            (
                jnp.concatenate([member[1:], start_row], axis=0)
                for member, start_row in zip(inclusive, identity_rows)
            )
        )
    else:
        exclusive = tuple(
            (
                jnp.concatenate([start_row, member[:-1]], axis=0)
                for member, start_row in zip(inclusive, identity_rows)
            )
        )
    zero_edge = jnp.zeros((seq_count, share), jnp.float32)
    start_real = exclusive[2] + exclusive[0] * zero_edge[None] - exclusive[1] * zero_edge[None]
    start_imaginary = exclusive[3] + exclusive[0] * zero_edge[None] + exclusive[1] * zero_edge[None]
    fixed_real = (
        local_real + power_real * start_real[:, None] - power_imaginary * start_imaginary[:, None]
    )
    fixed_imaginary = (
        local_imaginary
        + power_real * start_imaginary[:, None]
        + power_imaginary * start_real[:, None]
    )
    return (
        fixed_real.reshape(span, seq_count, share),
        fixed_imaginary.reshape(span, seq_count, share),
        zero_edge,
        zero_edge,
    )


def local(
    tokens,
    lengths,
    cotangent,
    norm_gain,
    norm_shift,
    lift_weight,
    decay_log,
    phase_log,
    skip_gain,
    mix_weight,
    glu_weight,
    glu_bias,
):
    seq_devices = lax.axis_size("seq")
    seq_place = lax.axis_index("seq")
    seq_count, stretch_size, model_width = tokens.shape
    state_count = decay_log.shape[1]
    valid = valid_at(lengths, seq_place * stretch_size, stretch_size)
    valid_col = valid[..., None]
    state_share = state_count // seq_devices
    state_start = seq_place * state_share
    time_start = 0
    time_span = stretch_size * seq_devices
    scan_valid = valid_at(lengths, time_start, time_span).T[:, :, None]
    after_valid = valid_at(lengths, time_start + 1, time_span).T[:, :, None]
    before_valid = valid_at(lengths, time_start - 1, time_span).T[:, :, None]
    stored = []
    current = tokens.astype(jnp.float32)
    for block_index in range(2):
        moments = lax.psum(
            (
                jnp.sum(current * valid_col, axis=(0, 1)),
                jnp.sum(current * current * valid_col, axis=(0, 1)),
                jnp.sum(valid),
            ),
            ("seq", "batch"),
        )
        count = moments[2]
        average = moments[0] / count
        inverse_root = lax.rsqrt(moments[1] / count - average * average + norm_eps)
        centered = (current - average) * inverse_root
        normed = (centered * norm_gain[block_index] + norm_shift[block_index]).astype(jnp.bfloat16)
        lift_matrix = lift_weight[block_index].reshape(model_width, 2, state_count)
        lifted = jnp.einsum(
            "sth,hkn->tskn", normed, lift_matrix, preferred_element_type=jnp.float32
        ).astype(jnp.bfloat16)
        lifted = lax.all_to_all(lifted, "seq", split_axis=3, concat_axis=0, tiled=True)
        decay_part = lax.dynamic_slice_in_dim(decay_log[block_index], state_start, state_share)
        phase_part = lax.dynamic_slice_in_dim(phase_log[block_index], state_start, state_share)
        decay_real, decay_imaginary, input_scale = rotation_decay(decay_part, phase_part)
        decay_rate = jnp.exp(decay_part)
        phase_angle = jnp.exp(phase_part)
        drive = input_scale * scan_valid
        lifted_real = lifted[:, :, 0].astype(jnp.float32)
        lifted_imaginary = lifted[:, :, 1].astype(jnp.float32)
        state_real, state_imaginary, entry_real, entry_imaginary = linear_chain(
            decay_rate,
            phase_angle,
            scan_valid,
            drive * lifted_real,
            drive * lifted_imaginary,
            block_index == 1,
            False,
        )
        state_low = jnp.stack([state_real, state_imaginary], axis=2).astype(jnp.bfloat16)
        state_low = lax.all_to_all(state_low, "seq", split_axis=0, concat_axis=3, tiled=True)
        mix_matrix = mix_weight[block_index].reshape(2, state_count, model_width)
        mixed = jnp.einsum(
            "tskn,knh->sth", state_low, mix_matrix, preferred_element_type=jnp.float32
        ) + skip_gain[block_index] * normed.astype(jnp.float32)
        activated = jax.nn.gelu(mixed, approximate=True).astype(jnp.bfloat16)
        projected = (
            jnp.einsum(
                "sth,hj->stj",
                activated,
                glu_weight[block_index],
                preferred_element_type=jnp.float32,
            )
            + glu_bias[block_index]
        )
        current = current + projected[..., :model_width] * jax.nn.sigmoid(
            projected[..., model_width:]
        )
        stored.append(
            (
                count,
                inverse_root,
                centered,
                normed,
                lift_matrix,
                lifted_real,
                lifted_imaginary,
                decay_part,
                phase_part,
                decay_rate,
                phase_angle,
                drive,
                state_real,
                state_imaginary,
                entry_real,
                entry_imaginary,
                state_low,
                mix_matrix,
                mixed,
                activated,
                projected,
            )
        )
    produced = (current * valid_col).astype(jnp.bfloat16)
    back_current = cotangent.astype(jnp.float32) * valid_col
    gain_grads = [None, None]
    shift_grads = [None, None]
    weight_grads = [None, None]
    for block_index in (1, 0):
        (
            count,
            inverse_root,
            centered,
            normed,
            lift_matrix,
            lifted_real,
            lifted_imaginary,
            decay_part,
            phase_part,
            decay_rate,
            phase_angle,
            drive,
            state_real,
            state_imaginary,
            entry_real,
            entry_imaginary,
            state_low,
            mix_matrix,
            mixed,
            activated,
            projected,
        ) = stored[block_index]
        linear_half = projected[..., :model_width]
        gate_sigmoid = jax.nn.sigmoid(projected[..., model_width:])
        back_projected = jnp.concatenate(
            [
                back_current * gate_sigmoid,
                back_current * linear_half * gate_sigmoid * (1.0 - gate_sigmoid),
            ],
            axis=-1,
        ).astype(jnp.bfloat16)
        grad_glu = jnp.einsum(
            "sth,stj->hj", activated, back_projected, preferred_element_type=jnp.float32
        )
        grad_glu_bias = jnp.sum(back_projected.astype(jnp.float32), axis=(0, 1))
        back_activated = jnp.einsum(
            "stj,hj->sth",
            back_projected,
            glu_weight[block_index],
            preferred_element_type=jnp.float32,
        )
        gelu_pullback = jax.vjp(partial(jax.nn.gelu, approximate=True), mixed)[1]
        back_mixed = gelu_pullback(back_activated)[0].astype(jnp.bfloat16)
        back_mixed_wide = back_mixed.astype(jnp.float32)
        grad_skip = jnp.sum(back_mixed_wide * normed.astype(jnp.float32), axis=(0, 1))
        grad_mix = jnp.einsum(
            "tskn,sth->knh", state_low, back_mixed, preferred_element_type=jnp.float32
        ).reshape(2 * state_count, model_width)
        back_state = jnp.einsum(
            "sth,knh->tskn", back_mixed, mix_matrix, preferred_element_type=jnp.float32
        ).astype(jnp.bfloat16)
        back_state = lax.all_to_all(back_state, "seq", split_axis=3, concat_axis=0, tiled=True)
        shift_valid = after_valid if block_index == 0 else before_valid
        adjoint_real, adjoint_imaginary, unused_real, unused_imaginary = linear_chain(
            decay_rate,
            phase_angle,
            shift_valid,
            back_state[:, :, 0].astype(jnp.float32),
            back_state[:, :, 1].astype(jnp.float32),
            block_index == 0,
            True,
        )
        if block_index == 0:
            prior_real = jnp.concatenate([entry_real[None], state_real[:-1]], axis=0)
            prior_imaginary = jnp.concatenate([entry_imaginary[None], state_imaginary[:-1]], axis=0)
        else:
            prior_real = jnp.concatenate([state_real[1:], entry_real[None]], axis=0)
            prior_imaginary = jnp.concatenate([state_imaginary[1:], entry_imaginary[None]], axis=0)
        back_decay_real = jnp.sum(
            scan_valid * (adjoint_real * prior_real + adjoint_imaginary * prior_imaginary),
            axis=(0, 1),
        )
        back_decay_imaginary = jnp.sum(
            scan_valid * (adjoint_imaginary * prior_real - adjoint_real * prior_imaginary),
            axis=(0, 1),
        )
        back_scale = jnp.sum(
            scan_valid * (adjoint_real * lifted_real + adjoint_imaginary * lifted_imaginary),
            axis=(0, 1),
        )
        decay_pullback = jax.vjp(rotation_decay, decay_part, phase_part)[1]
        decay_part_grad, phase_part_grad = decay_pullback(
            (back_decay_real, back_decay_imaginary, back_scale)
        )
        grad_decay = lax.dynamic_update_slice_in_dim(
            jnp.zeros((state_count,), jnp.float32), decay_part_grad, state_start, 0
        )
        grad_phase = lax.dynamic_update_slice_in_dim(
            jnp.zeros((state_count,), jnp.float32), phase_part_grad, state_start, 0
        )
        back_lifted = (
            jnp.stack([adjoint_real, adjoint_imaginary], axis=2) * drive[:, :, None, :]
        ).astype(jnp.bfloat16)
        back_lifted = lax.all_to_all(back_lifted, "seq", split_axis=0, concat_axis=3, tiled=True)
        grad_lift = jnp.einsum(
            "sth,tskn->hkn", normed, back_lifted, preferred_element_type=jnp.float32
        ).reshape(model_width, 2 * state_count)
        back_normed = (
            jnp.einsum(
                "tskn,hkn->sth", back_lifted, lift_matrix, preferred_element_type=jnp.float32
            )
            + skip_gain[block_index] * back_mixed_wide
        )
        norm_terms = lax.psum(
            (jnp.sum(back_normed * centered, axis=(0, 1)), jnp.sum(back_normed, axis=(0, 1))),
            ("seq", "batch"),
        )
        gain_grads[block_index] = norm_terms[0]
        shift_grads[block_index] = norm_terms[1]
        gain_now = norm_gain[block_index]
        back_current = back_current + inverse_root * (
            gain_now * back_normed
            - valid_col * gain_now * (norm_terms[1] + centered * norm_terms[0]) / count
        )
        weight_grads[block_index] = (
            grad_lift,
            grad_decay,
            grad_phase,
            grad_skip,
            grad_mix,
            grad_glu,
            grad_glu_bias,
        )
    reduced = lax.psum(
        (
            weight_grads[0][0],
            weight_grads[0][1],
            weight_grads[0][2],
            weight_grads[0][3],
            weight_grads[0][4],
            weight_grads[0][5],
            weight_grads[0][6],
            weight_grads[1][0],
            weight_grads[1][1],
            weight_grads[1][2],
            weight_grads[1][3],
            weight_grads[1][4],
            weight_grads[1][5],
            weight_grads[1][6],
        ),
        ("seq", "batch"),
    )
    weight_grads = [reduced[0:7], reduced[7:14]]
    stacked = tuple(
        (jnp.stack([weight_grads[0][member], weight_grads[1][member]]) for member in range(7))
    )
    return (
        produced,
        back_current.astype(jnp.bfloat16),
        jnp.stack(gain_grads),
        jnp.stack(shift_grads),
        stacked[0],
        stacked[1],
        stacked[2],
        stacked[3],
        stacked[4],
        stacked[5],
        stacked[6],
    )


def solution(mesh):
    placed = (
        P("batch", "seq", None),
        P("batch"),
        P("batch", "seq", None),
        P(),
        P(),
        P(),
        P(),
        P(),
        P(),
        P(),
        P(),
        P(),
    )
    return jax.shard_map(
        local,
        mesh=mesh,
        in_specs=placed,
        out_specs=(
            P("batch", "seq", None),
            P("batch", "seq", None),
            P(),
            P(),
            P(),
            P(),
            P(),
            P(),
            P(),
            P(),
            P(),
        ),
        check_vma=False,
    )
```

profile of v0, /device:TPU:0, one launch (start us, length us, event | category | flops | bytes accessed | tf_op | source)
XLA Modules:
  0.0 1215.5 jit_solution(8116405871813268584)
XLA Ops:
  14.8 42.3 %all-reduce.183 = (f32[512]{0:T(512)S(1)}, f32[]{:T(128)}, f32[512]{0:T(512)S(1)}) all-reduce(f32[512]{0:T(512)S(1)} %get-tuple-element.23, f32[]{:T(128)} %fusion.200, f32[512]{0:T(512)S(1)} %get-tuple-element.22), channel_id=1, replica_groups=mesh['seq'=8,'batch'=4] {'seq','batch'}, use_global_device_ids=true, to_apply=%region_6.0 | all-reduce | flops 1025 | bytes 8200 | tf_op jit(solution)/shard_map/psum | solution.py:138
  86.0 10.9 fusion.43
  136.1 9.9 multiply_add_fusion.4
  226.5 11.0 all-to-all-done.1
  242.0 9.0 copy.3234
  256.8 39.2 %all-reduce.182 = (f32[512]{0:T(512)S(1)}, f32[512]{0:T(512)S(1)}) all-reduce(f32[512]{0:T(512)S(1)} %get-tuple-element.16, f32[512]{0:T(512)S(1)} %get-tuple-element.15), channel_id=1, replica_groups=mesh['seq'=8,'batch'=4] {'seq','batch'}, use_global_device_ids=true, to_apply=%region_13.14 | all-reduce | flops 1024 | bytes 8192 | tf_op jit(solution)/shard_map/psum | solution.py:138
  328.8 11.3 fusion.54
  388.5 11.5 multiply_add_fusion.3
  518.8 10.8 copy.3237
  548.7 14.2 %all-to-all-done.4 = bf16[256,4,2,256]{0,2,1,3:T(2,128)(2,1)S(1)} async-done(((bf16[256,4,2,256]{0,2,1,3:T(2,128)(2,1)}), bf16[256,4,2,256]{0,2,1,3:T(2,128)(2,1)S(1)}, u32[]{:S(2)}, u32[]{:S(2)}) %all-to-all-start.4) | async-done | bytes 1048608 | tf_op jit(solution)/shard_map/all_to_all | solution.py:275
  569.6 11.2 fusion.65
  620.9 10.0 multiply_add_fusion.2
  677.6 10.3 copy.3157
  749.8 10.4 copy.3239
  764.2 39.7 %all-reduce.181 = (f32[512]{0:T(512)S(1)}, f32[512]{0:T(512)S(1)}) all-reduce(f32[512]{0:T(512)S(1)} %get-tuple-element.20, f32[512]{0:T(512)S(1)} %get-tuple-element.19), channel_id=1, replica_groups=mesh['seq'=8,'batch'=4] {'seq','batch'}, use_global_device_ids=true, to_apply=%region_22.23 | all-reduce | flops 1024 | bytes 8192 | tf_op jit(solution)/shard_map/psum | solution.py:327
  825.1 10.8 multiply_subtract_fusion.4
  846.6 10.7 fusion.71
  862.0 8.5 fusion.232
  888.7 8.5 fusion.231
  909.5 11.2 multiply_subtract_fusion
  950.3 10.3 fusion.119
  1008.8 9.0 copy.3242
  1028.6 42.0 %all-reduce.180 = (f32[512]{0:T(512)S(1)}, f32[512]{0:T(512)S(1)}, f32[1,256]{1,0:T(1,128)S(1)}, f32[1,256]{1,0:T(1,128)S(1)}, f32[1,256]{1,0:T(1,128)S(1)}, /*i...) all-reduce(f32[512]{0:T(512)S(1)} %get-tuple-element.18, ...), channel_id=1, replica_groups=mesh['seq'=8,'batch'=4] {'seq','batch'}, use_global_device_ids=true, to_apply=%region_29.30 | all-reduce | flops 5120 | bytes 40960 | tf_op jit(solution)/shard_map/psum | solution.py:327
  1078.3 121.7 %all-reduce.187.cloned.1.call-done = (f32[1,512,512]{2,1,0:T(8,128)}, f32[1,512,512]{2,1,0:T(8,128)}, f32[1,512,512]{2,1,0:T(8,128)}, f32[1,512,512]{2,1,0:T(8,1...) async-done(((f32[1,512,512]{2,1,0:T(8,128)}, f32[1,512,512]{2,1,0:T(8,128)}, f32[1,512,512]{2,1,0:T(8,128)}, f32[1,512,512]{2,1,0:T(8,128)}, ...) | async-done | bytes 8388624 | tf_op jit(solution)/shard_map/psum | solution.py:347
  (1181 shorter events, 712.3 us)
Async XLA Ops:
  9.3 245.4 %copy-start.66 = (f32[4,256]{1,0:T(4,128)}, f32[4,256]{1,0:T(4,128)S(1)}, u32[]{:S(2)}) copy-start(f32[4,256]{1,0:T(4,128)S(1)} %compare_convert_fusion.2) | copy-start | bytes 12292
  10.7 47.1 %copy-start.105 = (f32[1,512]{1,0:T(1,128)}, f32[1,512]{1,0:T(1,128)S(1)}, u32[]{:S(2)}) copy-start(f32[1,512]{1,0:T(1,128)S(1)} %get-tuple-element.331) | copy-start | bytes 6148
  12.0 45.8 %copy-start.146 = (f32[1,512]{1,0:T(1,128)}, f32[1,512]{1,0:T(1,128)S(1)}, u32[]{:S(2)}) copy-start(f32[1,512]{1,0:T(1,128)S(1)} %get-tuple-element.333) | copy-start | bytes 6148
  14.4 44.2 %copy-start.61 = (bf16[1,512,512]{1,2,0:T(8,128)(2,1)}, bf16[1,512,512]{1,2,0:T(8,128)(2,1)S(1)}, u32[]{:S(2)}) copy-start(bf16[1,512,512]{1,2,0:T(8,128)(2,1)S(1)} %copy.3244) | copy-start | bytes 1572868
  60.7 19.4 %all-to-all-start = ((bf16[256,4,2,256]{0,2,1,3:T(2,128)(2,1)}), bf16[256,4,2,256]{0,2,1,3:T(2,128)(2,1)S(1)}, u32[]{:S(2)}, u32[]{:S(2)}) async-start(bf16[256,4,2,256]{0,2,1,3:T(2,128)(2,1)} %copy.3057), calls=%async_computation | async-start | bytes 2097152 | tf_op jit(solution)/shard_map/all_to_all | solution.py:155
  75.0 122.2 %copy-start.64 = (f32[2048,4]{0,1:T(4,128)}, f32[2048,4]{0,1:T(4,128)S(1)}, u32[]{:S(2)}) copy-start(f32[2048,4]{0,1:T(4,128)S(1)} %mul.2622) | copy-start | bytes 98308
  75.7 121.5 %copy-start.77 = (f32[32]{0:T(128)}, f32[32]{0:T(128)S(1)}, u32[]{:S(2)}) copy-start(f32[32]{0:T(128)S(1)} %get-tuple-element.360) | copy-start | bytes 388
  76.4 120.8 %copy-start.83 = (f32[32]{0:T(128)}, f32[32]{0:T(128)S(1)}, u32[]{:S(2)}) copy-start(f32[32]{0:T(128)S(1)} %get-tuple-element.52) | copy-start | bytes 388
  110.5 72.3 %copy-start.2 = (f32[32,64,4,32]{1,0,3,2:T(8,128)}, f32[32,64,4,32]{1,0,3,2:T(8,128)S(1)}, u32[]{:S(2)}) copy-start(f32[32,64,4,32]{1,0,3,2:T(8,128)S(1)} %copy.3063) | copy-start | bytes 3145732
  218.4 19.0 %all-to-all-start.1 = ((bf16[8,2,32768]{2,1,0:T(2,128)(2,1)}), bf16[8,2,32768]{2,1,0:T(2,128)(2,1)S(1)}, u32[]{:S(2)}, u32[]{:S(2)}) async-start(bf16[8,2,32768]{2,1,0:T(2,128)(2,1)} %reshape.1022), calls=%async_computation.1 | async-start | bytes 2097152 | tf_op jit(solution)/shard_map/all_to_all | solution.py:174
  254.8 41.9 %copy-start.87 = (f32[1,512]{1,0:T(1,128)S(1)}, f32[1,512]{1,0:T(1,128)}, u32[]{:S(2)}) copy-start(f32[1,512]{1,0:T(1,128)} %get-tuple-element.330) | copy-start | bytes 6148
  254.8 41.9 %copy-start.112 = (f32[1,512]{1,0:T(1,128)S(1)}, f32[1,512]{1,0:T(1,128)}, u32[]{:S(2)}) copy-start(f32[1,512]{1,0:T(1,128)} %get-tuple-element.332) | copy-start | bytes 6148
  301.9 19.2 %all-to-all-start.2 = ((bf16[256,4,2,256]{0,2,1,3:T(2,128)(2,1)}), bf16[256,4,2,256]{0,2,1,3:T(2,128)(2,1)S(1)}, u32[]{:S(2)}, u32[]{:S(2)}) async-start(bf16[256,4,2,256]{0,2,1,3:T(2,128)(2,1)} %copy.3093), calls=%async_computation.2 | async-start | bytes 2097152 | tf_op jit(solution)/shard_map/all_to_all | solution.py:155
  485.4 28.9 %all-to-all-start.3 = ((bf16[8,2,32768]{2,1,0:T(2,128)(2,1)}), bf16[8,2,32768]{2,1,0:T(2,128)(2,1)S(1)}, u32[]{:S(2)}, u32[]{:S(2)}) async-start(bf16[8,2,32768]{2,1,0:T(2,128)(2,1)} %reshape.1024), calls=%async_computation.3 | async-start | bytes 2097152 | tf_op jit(solution)/shard_map/all_to_all | solution.py:174
  543.2 19.6 %all-to-all-start.4 = ((bf16[256,4,2,256]{0,2,1,3:T(2,128)(2,1)}), bf16[256,4,2,256]{0,2,1,3:T(2,128)(2,1)S(1)}, u32[]{:S(2)}, u32[]{:S(2)}) async-start(bf16[256,4,2,256]{0,2,1,3:T(2,128)(2,1)} %copy.3128), calls=%async_computation.4 | async-start | bytes 2097152 | tf_op jit(solution)/shard_map/all_to_all | solution.py:275
  696.1 46.6 %all-to-all-start.5 = ((bf16[8,2,32768]{2,1,0:T(2,128)(2,1)}), bf16[8,2,32768]{2,1,0:T(2,128)(2,1)}, u32[]{:S(2)}, u32[]{:S(2)}) async-start(bf16[8,2,32768]{2,1,0:T(2,128)(2,1)} %reshape.1026), calls=%async_computation.5 | async-start | bytes 2097152 | tf_op jit(solution)/shard_map/all_to_all | solution.py:317
  701.1 208.4 %copy-start.91 = (f32[32]{0:T(128)}, f32[32]{0:T(128)S(1)}, u32[]{:S(2)}) copy-start(f32[32]{0:T(128)S(1)} %get-tuple-element.347) | copy-start | bytes 388
  760.2 43.7 %copy-start.88 = (f32[1,512]{1,0:T(1,128)S(1)}, f32[1,512]{1,0:T(1,128)}, u32[]{:S(2)}) copy-start(f32[1,512]{1,0:T(1,128)} %get-tuple-element.330) | copy-start | bytes 6148
  820.8 19.7 %all-to-all-start.6 = ((bf16[256,4,2,256]{0,2,1,3:T(2,128)(2,1)}), bf16[256,4,2,256]{0,2,1,3:T(2,128)(2,1)}, u32[]{:S(2)}, u32[]{:S(2)}) async-start(bf16[256,4,2,256]{0,2,1,3:T(2,128)(2,1)} %copy.3166), calls=%async_computation.6 | async-start | bytes 2097152 | tf_op jit(solution)/shard_map/all_to_all | solution.py:275
  985.3 19.0 %all-to-all-start.7 = ((bf16[8,2,32768]{2,1,0:T(2,128)(2,1)}), bf16[8,2,32768]{2,1,0:T(2,128)(2,1)S(1)}, u32[]{:S(2)}, u32[]{:S(2)}) async-start(bf16[8,2,32768]{2,1,0:T(2,128)(2,1)} %reshape.1028), calls=%async_computation.7 | async-start | bytes 2097152 | tf_op jit(solution)/shard_map/all_to_all | solution.py:317
  989.0 210.9 %all-reduce.187.cloned.1.call-start = ((), (), s32[]{:S(2)}) async-start(), calls=%async_computation.8 | async-start | bytes 16777216 | tf_op jit(solution)/shard_map/psum | solution.py:347
  1023.9 47.8 %copy-start.111 = (f32[512]{0:T(512)S(1)}, f32[512]{0:T(512)}, u32[]{:S(2)}) copy-start(f32[512]{0:T(512)} %copy-done.110) | copy-start | bytes 6148
  1024.0 48.4 %copy-start.109 = (f32[512]{0:T(512)S(1)}, f32[512]{0:T(512)}, u32[]{:S(2)}) copy-start(f32[512]{0:T(512)} %copy-done.108) | copy-start | bytes 6148
  1024.0 50.2 %copy-start.5 = (f32[4,256,512]{2,1,0:T(8,128)S(1)}, f32[4,256,512]{2,1,0:T(8,128)}, u32[]{:S(2)}) copy-start(f32[4,256,512]{2,1,0:T(8,128)} %copy-done.4) | copy-start | bytes 6291460
  (147 other events, 709.2 us)
Sparse Core Ops, SparseCore 0:
  1019.8 180.0 all-reduce.186
where the time goes:
time: 1230 us; the launch traced here: 1220 us
  local copies, waits for them, and re-layouts  535 us (43%)
  other arithmetic  264 us (21%)
  blocking collectives  163 us (13%)
  waiting for transfers between devices  160 us (13%)
  matrix products  42.5 us (3%)
  starting transfers between devices  31.9 us (3%)
  between operations  18.7 us (2%)
    psum x1, waiting for transfers between devices, local(): lax.psum((weight_grads[0][0], weight_grads[0][1], weight_grads[0][2], wei...  122 us
    another operation x32, local copies, waits for them, and re-layouts, linear_chain(): running_real = lax.cumsum(weighted_real, axis=1, reverse=backwards)  116 us
    psum x2, blocking collectives, local(): lax.psum((jnp.sum(back_normed * centered, axis=(0, 1)), jnp.sum(back_norm...  81.7 us
    psum x2, blocking collectives, local(): lax.psum((jnp.sum(current * valid_col, axis=(0, 1)), jnp.sum(current * cu...  81.5 us
    unnamed x350, local copies, waits for them, and re-layouts  76 us
    another operation x8, other arithmetic, linear_chain(): running_real = lax.cumsum(weighted_real, axis=1, reverse=backwards)  52.9 us
    slice x260, local copies, waits for them, and re-layouts, linear_chain(): lax.associative_scan(complex_step, summary, reverse=backwards, axis=0)  42.6 us
    mul x3, other arithmetic, linear_chain(): weighted_real = growth * (cosine * drive_real + sine * drive_imaginary)  33.4 us
  transfers between devices with their start and end apart: 9, of which 7 were waited for; matrix products, arithmetic and copies ran while one was open for 11% of the time, Pallas kernels for 0%

commit v1 on v0

v1 whole, which is shorter than its diff:
```python
from functools import partial

import jax
import jax.numpy as jnp
from jax import lax
from jax.experimental import pallas as pl
from jax.experimental.pallas import tpu as pltpu
from jax.sharding import PartitionSpec as P

norm_eps = 1e-05
f32 = jnp.float32
bf16 = jnp.bfloat16

CHUNKS = 8
BLOCKS = 4
LANES = 128
VMEM_LIMIT = 24 * 1024 * 1024

in_vmem = pl.BlockSpec(memory_space=pltpu.VMEM)
in_smem = pl.BlockSpec(memory_space=pltpu.SMEM)
in_hbm = pl.BlockSpec(memory_space=pltpu.HBM)


def near(shape, dtype):
    return in_vmem, pltpu.VMEM(shape, dtype)


def far(shape, dtype):
    return in_hbm, pltpu.HBM(shape, dtype)


def moved(shape, dtype):
    return in_vmem, jax.ShapeDtypeStruct(shape, dtype)


def call(kernel, info, inputs, arrays, away, outs, scratch, name):
    arrays = [pltpu.with_memory_space_constraint(a, pltpu.VMEM) for a in arrays]
    away = [pltpu.with_memory_space_constraint(a, pltpu.HBM) for a in away]
    return pl.pallas_call(
        kernel,
        in_specs=[in_smem] + [in_vmem] * (len(inputs) + len(arrays)) + [in_hbm] * len(away),
        out_specs=[spec for spec, _ in outs],
        out_shape=[shape for _, shape in outs],
        scratch_shapes=scratch,
        compiler_params=pltpu.CompilerParams(vmem_limit_bytes=VMEM_LIMIT),
        name=name,
    )(info, *inputs, *arrays, *away)


class Copies:
    def __init__(self, sources, targets, sems):
        self.sources, self.targets, self.sems = sources, targets, sems
        self.size = sources[0].shape[0] // BLOCKS

    def copy(self, n, block):
        here = pl.ds(block * self.size, self.size)
        return pltpu.make_async_copy(self.sources[n].at[here, :], self.targets[n].at[here, :], self.sems.at[n, block])

    def start(self, block):
        for n in range(len(self.sources)):
            self.copy(n, block).start()

    def wait(self, block):
        for n in range(len(self.sources)):
            self.copy(n, block).wait()


def staged(shapes):
    return [pltpu.VMEM(shape, dtype) for shape, dtype in shapes] + [pltpu.SemaphoreType.DMA((len(shapes), BLOCKS))]


def wide(mask, width):
    return jnp.concatenate([mask] * (width // LANES), axis=1)


def dot(a, b):
    return lax.dot_general(a, b, (((1,), (0,)), ((), ())), preferred_element_type=f32)


def dot_t(a, b):
    return lax.dot_general(a, b, (((1,), (1,)), ((), ())), preferred_element_type=f32)


def t_dot(a, b):
    return lax.dot_general(a, b, (((0,), (0,)), ((), ())), preferred_element_type=f32)


def cmul(ar, ai, br, bi):
    return ar * br - ai * bi, ar * bi + ai * br


def order(steps, reverse):
    return range(steps - 1, -1, -1) if reverse else range(steps)


def shuffle_matrix(span, back):
    chunk = span // CHUNKS
    place = lax.broadcasted_iota(jnp.int32, (span, span), 0)
    source = lax.broadcasted_iota(jnp.int32, (span, span), 1)
    if back:
        wanted = (place % chunk) * CHUNKS + place // chunk
    else:
        wanted = (place % CHUNKS) * chunk + place // CHUNKS
    return (source == wanted).astype(f32).astype(bf16)


class Where:
    def __init__(self, info_ref, seqs, span):
        self.seq, self.batch = info_ref[0], info_ref[1]
        self.seqs, self.span = seqs, span
        self.lengths = [info_ref[2 + s] for s in range(seqs)]
        self.lefts = [length - self.seq * span for length in self.lengths]

    def steps_left(self):
        before = (self.span // CHUNKS) * lax.broadcasted_iota(jnp.int32, (CHUNKS, LANES), 0)
        return jnp.concatenate([left - before for left in self.lefts], axis=0)


def valid_rows(left, first, steps):
    return jnp.concatenate([(left > first + t).astype(f32) for t in range(steps)], axis=0)


def shuffle_rows(wide_ref, source_ref):
    steps, seqs, chunks, width = wide_ref.shape
    shuffle = shuffle_matrix(steps * chunks, False)
    for s in range(seqs):
        wide_ref[:, s] = dot(shuffle, source_ref[s]).reshape(steps, chunks, width)


def enter_kernel(info_ref, tokens_ref, rows_ref, sums_ref, wide_ref, acc_ref):
    seqs, span, width = tokens_ref.shape
    where = Where(info_ref, seqs, span)
    step = lax.broadcasted_iota(jnp.int32, (span, 1), 0)
    total = jnp.zeros((1, width), f32)
    squares = jnp.zeros((1, width), f32)
    count = jnp.zeros((1, 1), f32)
    for s in range(seqs):
        valid = (step < where.lefts[s]).astype(f32)
        x = tokens_ref[s].astype(f32)
        masked = x * valid
        total += jnp.sum(masked, axis=0, keepdims=True)
        squares += jnp.sum(masked * x, axis=0, keepdims=True)
        count += jnp.sum(valid, axis=0, keepdims=True)
    tail = jnp.broadcast_to(count, (1, LANES))
    acc_ref[0:1, :] = jnp.concatenate([total, tail], axis=1)
    acc_ref[1:2, :] = jnp.concatenate([squares, tail], axis=1)
    for j in range(sums_ref.shape[0]):
        sums_ref[j] = acc_ref[...]
    shuffle_rows(wide_ref, tokens_ref)
    rows_ref[...] = wide_ref[...].reshape(seqs * span, width).astype(bf16)


def enter(info, tokens, devices):
    seqs, span, width = tokens.shape
    return call(
        enter_kernel,
        info,
        (tokens,),
        (),
        (),
        [near((seqs * span, width), bf16), moved((devices, 2, width + LANES), f32)],
        [pltpu.VMEM((span // CHUNKS, seqs, CHUNKS, width), f32), pltpu.VMEM((2, width + LANES), f32)],
        "enter",
    )


def power_kernel(span, seqs, info_ref, decay_ref, phase_ref, lam_ref, scale_ref, *outs):
    blocks, states = decay_ref.shape
    groups = states // LANES
    group = outs[0].shape[1]
    total, limit = outs[1].shape[0], span // CHUNKS
    where = Where(info_ref, seqs, span)
    rate = jnp.exp(decay_ref[...])
    size, angle = jnp.exp(-rate), jnp.exp(phase_ref[...])
    lam_ref[:, :states] = size * jnp.cos(angle)
    lam_ref[:, states:] = size * jnp.sin(angle)
    scale_ref[...] = jnp.sqrt(1.0 - jnp.exp(-2.0 * rate))
    chunk_left = where.steps_left()
    line = lax.broadcasted_iota(jnp.int32, (total, LANES), 0)
    span_left = jnp.zeros((total, LANES), jnp.int32)
    for s, length in enumerate(where.lengths):
        span_left = jnp.where(line % seqs == s, length - span * (line // seqs), span_left)
    for k in range(blocks):
        for back in (0, 1):
            table_ref, leap_ref = outs[4 * k + 2 * back : 4 * k + 2 * back + 2]
            shift = 0 if not back else (-1 if k == 0 else 1)
            chunk_count = jnp.clip(chunk_left + shift, 0, limit)
            span_count = jnp.clip(span_left + shift, 0, span)
            for low in range(groups):
                real_lanes = slice(low * LANES, (low + 1) * LANES)
                imag_lanes = slice((groups + low) * LANES, (groups + low + 1) * LANES)
                br, bi = lam_ref[k : k + 1, real_lanes], lam_ref[k : k + 1, imag_lanes]
                if back:
                    bi = -bi
                cr = jnp.ones((group, LANES), f32)
                ci = jnp.zeros((group, LANES), f32)
                pr = jnp.ones((total, LANES), f32)
                pi = jnp.zeros((total, LANES), f32)
                for bit in range(span.bit_length()):
                    if (1 << bit) <= limit:
                        nr, ni = cmul(cr, ci, br, bi)
                        odd = (chunk_count & (1 << bit)) != 0
                        cr, ci = jnp.where(odd, nr, cr), jnp.where(odd, ni, ci)
                    nr, ni = cmul(pr, pi, br, bi)
                    odd = (span_count & (1 << bit)) != 0
                    pr, pi = jnp.where(odd, nr, pr), jnp.where(odd, ni, pi)
                    br, bi = cmul(br, bi, br, bi)
                table_ref[low] = cr
                table_ref[groups + low] = ci
                leap_ref[:, real_lanes] = pr
                leap_ref[:, imag_lanes] = pi


def power_tables(info, decay_log, phase_log, seqs, seq_devices, span):
    blocks, states = decay_log.shape
    outs = [near((blocks, 2 * states), f32), near((blocks, states), f32)]
    for _ in range(2 * blocks):
        outs.append(near((2 * states // LANES, seqs * CHUNKS, LANES), f32))
        outs.append(near((seq_devices * seqs, 2 * states), f32))
    return call(partial(power_kernel, span, seqs), info, (), (decay_log, phase_log), (), outs, [], "powers")


def stretch_part(ends_ref, power_ref, reverse, seqs):
    groups = ends_ref.shape[0] // 2
    reals, imags = [], []
    for low in range(groups):
        real = jnp.zeros((seqs, LANES), f32)
        imag = jnp.zeros((seqs, LANES), f32)
        for c in order(CHUNKS, reverse):
            here = pl.ds(c, seqs, stride=CHUNKS)
            real, imag = cmul(power_ref[low, here, :], power_ref[groups + low, here, :], real, imag)
            real += ends_ref[low, here, :]
            imag += ends_ref[groups + low, here, :]
        reals.append(real)
        imags.append(imag)
    return jnp.concatenate(reals + imags, axis=1)


def chunk_starts(start_ref, place, parts_ref, leaps_ref, ends_ref, power_ref, reverse):
    devices, seqs, width = parts_ref.shape
    states = width // 2
    groups = states // LANES
    real = jnp.zeros((seqs, states), f32)
    imag = jnp.zeros((seqs, states), f32)
    for j in order(devices, reverse):
        ahead = (j > place) if reverse else (j < place)
        leap, part = leaps_ref[seqs * j : seqs * (j + 1), :], parts_ref[j]
        next_real, next_imag = cmul(leap[:, :states], leap[:, states:], real, imag)
        real = jnp.where(ahead, next_real + part[:, :states], real)
        imag = jnp.where(ahead, next_imag + part[:, states:], imag)
    for low in range(groups):
        hr = real[:, low * LANES : (low + 1) * LANES]
        hi = imag[:, low * LANES : (low + 1) * LANES]
        for c in order(CHUNKS, reverse):
            here = pl.ds(c, seqs, stride=CHUNKS)
            start_ref[low, here, :] = hr
            start_ref[groups + low, here, :] = hi
            hr, hi = cmul(power_ref[low, here, :], power_ref[groups + low, here, :], hr, hi)
            hr += ends_ref[low, here, :]
            hi += ends_ref[groups + low, here, :]


def scan_block(h_ref, drive, left, lam, conjugate, shift, first, steps, reverse, out_ref=None):
    groups, group, _ = h_ref.shape
    groups = groups // 2
    masks = [left > first + t + shift for t in range(steps)]
    for low in range(groups):
        real_lanes = slice(low * LANES, (low + 1) * LANES)
        imag_lanes = slice((groups + low) * LANES, (groups + low + 1) * LANES)
        hr, hi = h_ref[low], h_ref[groups + low]
        lr, li = lam[:, real_lanes], lam[:, imag_lanes]
        if conjugate:
            li = -li
        for t in order(steps, reverse):
            ur, ui = drive(t, real_lanes, imag_lanes)
            nr, ni = cmul(lr, li, hr, hi)
            hr = jnp.where(masks[t], nr, hr) + ur
            hi = jnp.where(masks[t], ni, hi) + ui
            if out_ref is not None:
                out_ref[t * group : (t + 1) * group, real_lanes] = hr
                out_ref[t * group : (t + 1) * group, imag_lanes] = hi
        h_ref[low] = hr
        h_ref[groups + low] = hi


def input_drive(lifted, scale, left, first, steps):
    group = left.shape[0]
    masks = [left > first + t for t in range(steps)]

    def drive(t, real_lanes, imag_lanes):
        here = slice(t * group, (t + 1) * group)
        factor = jnp.where(masks[t], scale[:, real_lanes], 0.0)
        return factor * lifted[here, real_lanes], factor * lifted[here, imag_lanes]

    return drive


def blocks_of(rows, group, reverse):
    size = rows // BLOCKS
    for block in order(BLOCKS, reverse):
        yield block, block * (size // group), slice(block * size, (block + 1) * size)


def lift_kernel(k, seqs, info_ref, sums_ref, *refs):
    reverse = k == 1
    if k == 0:
        x_ref, refs = refs[0], refs[1:]
    else:
        count_ref, x_ref = refs[:2]
        refs = refs[2:]
    gain_ref, shift_ref, weight_ref, lam_ref, scale_ref, power_ref = refs[:6]
    normed_ref, lifted_ref, ends_ref, part_ref, stats_ref = refs[6:11]
    rows, width = x_ref.shape
    group = ends_ref.shape[1]
    steps = rows // BLOCKS // group
    where = Where(info_ref, seqs, rows // seqs)
    sums = jnp.sum(sums_ref[...], axis=0)
    if k == 0:
        kept_count_ref = refs[11]
        kept_count_ref[...] = jnp.broadcast_to(sums[0:1, width:], kept_count_ref.shape)
        count = sums[0:1, width : width + 1]
    else:
        count = count_ref[0:1, 0:1]
    average = sums[0:1, :width] / count
    root = lax.rsqrt(sums[1:2, :width] / count - average * average + norm_eps)
    stats_ref[0:1, :] = average
    stats_ref[1:2, :] = root
    gain, shift = gain_ref[k : k + 1, :], shift_ref[k : k + 1, :]
    lam, scale = lam_ref[k : k + 1, :], scale_ref[k : k + 1, :]
    left = where.steps_left()
    ends_ref[...] = jnp.zeros_like(ends_ref)
    for _, first, now in blocks_of(rows, group, reverse):
        normed = ((x_ref[now, :].astype(f32) - average) * root * gain + shift).astype(bf16)
        normed_ref[now, :] = normed
        lifted = dot(normed, weight_ref[k]).astype(bf16)
        lifted_ref[now, :] = lifted
        drive = input_drive(lifted.astype(f32), scale, left, first, steps)
        scan_block(ends_ref, drive, left, lam, False, 0, first, steps, reverse)
    part = stretch_part(ends_ref, power_ref, reverse, seqs)
    for j in range(part_ref.shape[0]):
        part_ref[j] = part


def lift(k, seqs, seq_devices, info, sums, arrays):
    rows, width = arrays[0 if k == 0 else 1].shape
    table = arrays[-1].shape
    states = table[0] * LANES
    outs = [
        near((rows, width), bf16),
        near((rows, states), bf16),
        near(table, f32),
        moved((seq_devices, seqs, states), f32),
        near((2, width), f32),
    ]
    if k == 0:
        outs.append(near((8, LANES), f32))
    return call(partial(lift_kernel, k, seqs), info, (sums,), arrays, (), outs, [], "lift")


def mix_kernel(k, info_ref, parts_ref, *refs):
    reverse = k == 1
    (leaps_ref, ends_ref, power_ref, lifted_ref, normed_ref, x_ref) = refs[:6]
    (mix_ref, skip_ref, glu_ref, bias_ref, lam_ref, scale_ref) = refs[6:12]
    refs = refs[12:]
    if reverse:
        state_ref, activated_ref, slope_ref, gate_ref, gate_slope_ref, masked_out = refs[:6]
        h_ref, states_ref, masked_ref, sems = refs[6:]
        copies = Copies([masked_ref], [masked_out], sems)
    else:
        next_ref, sums_ref = refs[:2]
        away, refs = refs[2:8], refs[8:]
        h_ref, states_ref, acc_ref = refs[:3]
        here = refs[3:9]
        state_ref, activated_ref, slope_ref, gate_ref, gate_slope_ref, low_next_ref = here
        copies = Copies(here, away, refs[9])
    seqs = parts_ref.shape[1]
    rows, width = x_ref.shape
    group = ends_ref.shape[1]
    steps = rows // BLOCKS // group
    where = Where(info_ref, seqs, rows // seqs)
    chunk_starts(h_ref, where.seq, parts_ref, leaps_ref, ends_ref, power_ref, reverse)
    left = where.steps_left()
    skip, bias = skip_ref[k : k + 1, :], bias_ref[k : k + 1, :]
    lam, scale = lam_ref[k : k + 1, :], scale_ref[k : k + 1, :]
    total = jnp.zeros((1, width), f32)
    squares = jnp.zeros((1, width), f32)
    for block, first, now in blocks_of(rows, group, reverse):
        drive = input_drive(lifted_ref[now, :].astype(f32), scale, left, first, steps)
        scan_block(h_ref, drive, left, lam, False, 0, first, steps, reverse, states_ref)
        state = states_ref[...].astype(bf16)
        state_ref[now, :] = state
        mixed = dot(state, mix_ref[k]) + skip * normed_ref[now, :].astype(f32)
        base, cube = 0.7978845608028654, 0.044715
        square = mixed * mixed
        bend = jnp.tanh(mixed * (base + (base * cube) * square))
        half = 0.5 + 0.5 * bend
        activated = (mixed * half).astype(bf16)
        activated_ref[now, :] = activated
        slope_ref[now, :] = (
            half + mixed * (half - half * half) * (2.0 * base + (6.0 * base * cube) * square)
        ).astype(bf16)
        projected = dot(activated, glu_ref[k]) + bias
        gate = 0.5 + 0.5 * jnp.tanh(0.5 * projected[:, width:])
        gated = projected[:, :width] * gate
        gate_ref[now, :] = gate.astype(bf16)
        gate_slope_ref[now, :] = (gated - gated * gate).astype(bf16)
        after = x_ref[now, :].astype(f32) + gated
        masked = after * wide(valid_rows(left, first, steps), width)
        if reverse:
            masked_ref[now, :] = masked.astype(bf16)
        else:
            next_ref[now, :] = after
            low_next_ref[now, :] = after.astype(bf16)
            total += jnp.sum(masked, axis=0, keepdims=True)
            squares += jnp.sum(masked * after, axis=0, keepdims=True)
        copies.start(block)
    if not reverse:
        acc_ref[0:1, :] = total
        acc_ref[1:2, :] = squares
        for j in range(sums_ref.shape[0]):
            sums_ref[j] = acc_ref[...]
    for block in range(BLOCKS):
        copies.wait(block)


def mix(k, info, parts, arrays, devices):
    rows, width = arrays[5].shape
    states = arrays[3].shape[1]
    wide_shape, state_shape = ((rows, width), bf16), ((rows, states), bf16)
    scratch = [pltpu.VMEM(arrays[2].shape, f32), pltpu.VMEM((rows // BLOCKS, states), f32)]
    if k == 1:
        outs = [near(*state_shape)] + [near(*wide_shape)] * 4 + [far(*wide_shape)]
        scratch += staged([wide_shape])
    else:
        outs = [near((rows, width), f32), moved((devices, 2, width), f32), far(*state_shape)] + [far(*wide_shape)] * 5
        scratch += [pltpu.VMEM((2, width), f32)] + staged([state_shape] + [wide_shape] * 5)
    return call(partial(mix_kernel, k), info, (parts,), arrays, (), outs, scratch, "mix")


def glu_back_kernel(k, seqs, info_ref, *refs):
    reverse = k == 0
    if k == 1:
        cot_ref, normed_ref, slope_ref, gate_ref, gate_slope_ref = refs[:5]
        refs = refs[5:]
    else:
        sums_ref, back_normed_ref, stats_ref, gain_ref, count_ref = refs[:5]
        refs = refs[5:]
    glu_ref, mix_ref, lam_ref, power_ref = refs[:4]
    refs = refs[4:]
    if k == 0:
        away, refs = refs[:6], refs[6:]
    (projected_ref, mixed_ref, dh_ref, bias_grad_ref, skip_grad_ref, ends_ref, part_ref) = refs[:7]
    refs = refs[7:]
    rows, width = mixed_ref.shape
    group = ends_ref.shape[1]
    size = rows // BLOCKS
    steps = size // group
    where = Where(info_ref, seqs, rows // seqs)
    if k == 1:
        back_out, wide_ref, back_ref, sems = refs
        copies = Copies([back_ref], [back_out], sems)
        shuffle_rows(wide_ref, cot_ref)
    else:
        back_ref, total_ref = refs[:2]
        here = refs[2:8]
        x_ref, before_ref, normed_ref, slope_ref, gate_ref, gate_slope_ref = here
        copies = Copies(away, here, refs[8])
        for block in order(BLOCKS, reverse):
            copies.start(block)
        sums = jnp.sum(sums_ref[...], axis=0)
        total_ref[...] = sums
        count = count_ref[0:1, 0:1]
        gain_sum, shift_sum = sums[0:1], sums[1:2]
        average, root = stats_ref[0:1, :], stats_ref[1:2, :]
        gain = gain_ref[1:2, :]
    left = where.steps_left()
    lam = lam_ref[k : k + 1, :]
    ends_ref[...] = jnp.zeros_like(ends_ref)
    bias_grad = jnp.zeros((1, 2 * width), f32)
    skip_grad = jnp.zeros((1, width), f32)
    for block, first, now in blocks_of(rows, group, reverse):
        valid = wide(valid_rows(left, first, steps), width)
        if k == 1:
            back = wide_ref[first : first + steps].reshape(size, width) * valid
        else:
            copies.wait(block)
            centered = (x_ref[now, :].astype(f32) - average) * root
            back_normed = back_normed_ref[now, :].astype(f32)
            back = before_ref[now, :].astype(f32) + (root * gain) * (
                back_normed - valid * ((shift_sum + centered * gain_sum) / count)
            )
        back_ref[now, :] = back.astype(bf16)
        if k == 1:
            copies.start(block)
        value_back = (back * gate_ref[now, :].astype(f32)).astype(bf16)
        gate_back = (back * gate_slope_ref[now, :].astype(f32)).astype(bf16)
        back_projected = jnp.concatenate([value_back, gate_back], axis=1)
        projected_ref[now, :] = back_projected
        bias_grad += jnp.sum(back_projected.astype(f32), axis=0, keepdims=True)
        back_activated = dot_t(back_projected, glu_ref[k])
        back_mixed = (slope_ref[now, :].astype(f32) * back_activated).astype(bf16)
        mixed_ref[now, :] = back_mixed
        skip_grad += jnp.sum(back_mixed.astype(f32) * normed_ref[now, :].astype(f32), axis=0, keepdims=True)
        back_state = dot_t(back_mixed, mix_ref[k]).astype(bf16)
        dh_ref[now, :] = back_state
        wide_state = back_state.astype(f32)

        def drive(t, real_lanes, imag_lanes):
            at = slice(t * group, (t + 1) * group)
            return wide_state[at, real_lanes], wide_state[at, imag_lanes]

        shift = 1 if reverse else -1
        scan_block(ends_ref, drive, left, lam, True, shift, first, steps, reverse)
    bias_grad_ref[...] = bias_grad
    skip_grad_ref[...] = skip_grad
    part = stretch_part(ends_ref, power_ref, reverse, seqs)
    for j in range(part_ref.shape[0]):
        part_ref[j] = part
    if k == 1:
        for block in range(BLOCKS):
            copies.wait(block)


def glu_back(k, seqs, seq_devices, info, inputs, arrays, away):
    table = arrays[-1].shape
    states = table[0] * LANES
    width = arrays[-4].shape[1]
    rows = arrays[1 if k == 1 else 0].shape[0]
    outs = [
        near((rows, 2 * width), bf16),
        near((rows, width), bf16),
        near((rows, states), bf16),
        near((1, 2 * width), f32),
        near((1, width), f32),
        near(table, f32),
        moved((seq_devices, seqs, states), f32),
    ]
    if k == 1:
        outs.append(far((rows, width), bf16))
        scratch = [pltpu.VMEM((rows // seqs // CHUNKS, seqs, CHUNKS, width), f32)] + staged([((rows, width), bf16)])
    else:
        outs += [near((rows, width), bf16), near((2, width), f32)]
        scratch = staged([(a.shape, a.dtype) for a in away])
    return call(partial(glu_back_kernel, k, seqs), info, inputs, arrays, away, outs, scratch, "glu_back")


def lift_back_kernel(k, info_ref, parts_ref, *refs):
    reverse = last = k == 0
    (leaps_ref, ends_ref, power_ref, dh_ref, mixed_ref) = refs[:5]
    (stats_ref, weight_ref, skip_ref, lam_ref, scale_ref) = refs[5:10]
    refs = refs[10:]
    if last:
        back_ref, gain_ref = refs[:2]
        small_refs, away, refs = refs[2:8], refs[8:11], refs[11:]
        back_lifted_ref, sums_ref, ahead_ref = refs[:3]
        refs = refs[3:]
        lifted_ref, state_ref, x_ref, sems = refs[-4:]
        copies = Copies(away, refs[-4:-1], sems)
        refs = refs[:-4]
        for block in order(BLOCKS, reverse):
            copies.start(block)
    else:
        lifted_ref, state_ref, x_ref = refs[:3]
        back_lifted_ref, sums_ref, back_normed_ref, lam_grad_ref, scale_grad_ref = refs[3:8]
        refs = refs[8:]
    h_ref, low_ref, acc_ref, lam_acc_ref, scale_acc_ref = refs
    rows, width = x_ref.shape
    group = ends_ref.shape[1]
    seqs = parts_ref.shape[1]
    steps = rows // BLOCKS // group
    states = scale_ref.shape[1]
    where = Where(info_ref, seqs, rows // seqs)
    chunk_starts(h_ref, where.seq, parts_ref, leaps_ref, ends_ref, power_ref, reverse)
    lam_acc_ref[...] = jnp.zeros_like(lam_acc_ref)
    scale_acc_ref[...] = jnp.zeros_like(scale_acc_ref)
    left = where.steps_left()
    lam, scale = lam_ref[k : k + 1, :], scale_ref[k : k + 1, :]
    average, root = stats_ref[0:1, :], stats_ref[1:2, :]
    skip = skip_ref[k : k + 1, :]
    gain_sum = jnp.zeros((1, width), f32)
    shift_sum = jnp.zeros((1, width), f32)
    shift = 1 if reverse else -1
    for block, first, now in blocks_of(rows, group, reverse):
        moving = [left > first + t + shift for t in range(steps)]
        valid = [left > first + t for t in range(steps)]
        if last:
            copies.wait(block)
        dh = dh_ref[now, :].astype(f32)
        lifted = lifted_ref[now, :].astype(f32)
        state = state_ref[now, :].astype(f32)
        for low in range(0, states, LANES):
            real_lanes = slice(low, low + LANES)
            imag_lanes = slice(states + low, states + low + LANES)
            gr, gi = h_ref[low // LANES], h_ref[(states + low) // LANES]
            lr, li = lam[:, real_lanes], -lam[:, imag_lanes]
            part = scale[:, real_lanes]
            sum_r, sum_i = lam_acc_ref[:, real_lanes], lam_acc_ref[:, imag_lanes]
            sum_s = scale_acc_ref[:, real_lanes]
            for t in order(steps, reverse):
                at = slice(t * group, (t + 1) * group)
                hr, hi = state[at, real_lanes], state[at, imag_lanes]
                ur, ui = lifted[at, real_lanes], lifted[at, imag_lanes]
                mr, mi = jnp.where(moving[t], gr, 0.0), jnp.where(moving[t], gi, 0.0)
                sum_r += mr * hr + mi * hi
                sum_i += mi * hr - mr * hi
                nr, ni = cmul(lr, li, gr, gi)
                gr = jnp.where(moving[t], nr, gr) + dh[at, real_lanes]
                gi = jnp.where(moving[t], ni, gi) + dh[at, imag_lanes]
                vr, vi = jnp.where(valid[t], gr, 0.0), jnp.where(valid[t], gi, 0.0)
                sum_s += vr * ur + vi * ui
                low_ref[at, real_lanes] = part * vr
                low_ref[at, imag_lanes] = part * vi
            h_ref[low // LANES] = gr
            h_ref[(states + low) // LANES] = gi
            lam_acc_ref[:, real_lanes] = sum_r
            lam_acc_ref[:, imag_lanes] = sum_i
            scale_acc_ref[:, real_lanes] = sum_s
        back_lifted = low_ref[...].astype(bf16)
        back_lifted_ref[now, :] = back_lifted
        back_normed = dot_t(back_lifted, weight_ref[k]) + skip * mixed_ref[now, :].astype(f32)
        centered = (x_ref[now, :].astype(f32) - average) * root
        gain_sum += jnp.sum(back_normed * centered, axis=0, keepdims=True)
        shift_sum += jnp.sum(back_normed, axis=0, keepdims=True)
        if last:
            ahead_ref[now, :] = (back_ref[now, :].astype(f32) + (root * gain_ref[0:1, :]) * back_normed).astype(bf16)
        else:
            back_normed_ref[now, :] = back_normed.astype(bf16)
    lam_grad = jnp.sum(lam_acc_ref[...], axis=0, keepdims=True)
    scale_grad = jnp.sum(scale_acc_ref[...], axis=0, keepdims=True)
    acc_ref[0:1, :width] = gain_sum
    acc_ref[1:2, :width] = shift_sum
    if last:
        skip0_ref, bias0_ref, skip1_ref, bias1_ref, lam1_ref, scale1_ref = small_refs
        acc_ref[2:3, :width] = skip0_ref[...]
        acc_ref[3:4, :width] = skip1_ref[...]
        acc_ref[4:5, :width] = bias0_ref[:, :width]
        acc_ref[5:6, :width] = bias0_ref[:, width:]
        acc_ref[6:7, :width] = bias1_ref[:, :width]
        acc_ref[7:8, :width] = bias1_ref[:, width:]
        acc_ref[0:1, width:] = lam_grad[:, :states]
        acc_ref[1:2, width:] = lam_grad[:, states:]
        acc_ref[2:3, width:] = lam1_ref[:, :states]
        acc_ref[3:4, width:] = lam1_ref[:, states:]
        acc_ref[4:5, width:] = scale_grad
        acc_ref[5:6, width:] = scale1_ref[...]
        acc_ref[6:8, width:] = jnp.zeros((2, states), f32)
    else:
        lam_grad_ref[...] = lam_grad
        scale_grad_ref[...] = scale_grad
    for j in range(sums_ref.shape[0]):
        sums_ref[j] = acc_ref[...]


def lift_back(k, info, parts, arrays, away, devices):
    table = arrays[2].shape
    rows, states = arrays[3].shape
    width = arrays[4].shape[1]
    scratch = [pltpu.VMEM(table, f32), pltpu.VMEM((rows // BLOCKS, states), f32)]
    if k == 0:
        acc = (8, width + states // 2)
        outs = [near((rows, states), bf16), moved((devices,) + acc, f32), near((rows, width), bf16)]
    else:
        acc = (2, width)
        outs = [near((rows, states), bf16), moved((devices,) + acc, f32), near((rows, width), bf16)]
        outs += [near((1, states), f32), near((1, states // 2), f32)]
    scratch += [
        pltpu.VMEM(acc, f32),
        pltpu.VMEM((table[1], states), f32),
        pltpu.VMEM((table[1], states // 2), f32),
    ]
    if k == 0:
        scratch += staged([(a.shape, a.dtype) for a in away])
    return call(partial(lift_back_kernel, k), info, (parts,), arrays, away, outs, scratch, "lift_back")


def halves_kernel(parts, info_ref, *refs):
    pairs = (len(refs) - 2) // 2
    keep_ref, send_ref = refs[-2:]
    width = keep_ref.shape[1]
    even = info_ref[0] % 2 == 0
    products = [t_dot(refs[2 * n][...], refs[2 * n + 1][...]) for n in range(pairs)]
    first = 0
    for own, other in parts:
        (m, r, rows, c), (n, q, _, d) = own, other
        a = products[m][r : r + rows, c : c + width].astype(bf16)
        b = products[n][q : q + rows, d : d + width].astype(bf16)
        keep_ref[first : first + rows, :] = jnp.where(even, a, b)
        send_ref[first : first + rows, :] = jnp.where(even, b, a)
        first += rows


def halves(info, parts, arrays, rows, width, name):
    outs = [moved((rows, width), bf16)] * 2
    return call(partial(halves_kernel, parts), info, (), arrays, (), outs, [], name)


def split_kernel(shift, slot, info_ref, *refs):
    n = refs[0].shape[0]
    ins, outs = refs[: len(refs) - n], refs[len(refs) - n :]
    place = info_ref[slot] >> shift
    for m in range(n):
        total = ins[0][place ^ m].astype(f32)
        for ref in ins[1:]:
            total += ref[place ^ m].astype(f32)
        outs[m][...] = total.astype(outs[m].dtype)


def split(info, arrays, shift, slot):
    n = arrays[0].shape[0]
    shape = arrays[0].shape[1:]
    outs = [moved(shape, f32)] + [moved(shape, bf16)] * (n - 1)
    return call(partial(split_kernel, shift, slot), info, arrays, (), (), outs, [], "split")


def sum_kernel(info_ref, *refs):
    total = refs[0][...].astype(f32)
    for ref in refs[1:-1]:
        total += ref[...].astype(f32)
    refs[-1][...] = total.astype(bf16)


def join_kernel(shift, slot, info_ref, *refs):
    place = info_ref[slot] >> shift
    for m, ref in enumerate(refs[:-1]):
        refs[-1][place ^ m] = ref[...]


def join(info, arrays, shift, slot):
    outs = [moved((len(arrays),) + arrays[0].shape, bf16)]
    return call(partial(join_kernel, shift, slot), info, arrays, (), (), outs, [], "join")[0]


def trade(x, axis, mask):
    size = lax.axis_size(axis)
    return lax.ppermute(x, axis, [(i, i ^ mask) for i in range(size)])


def sum_along(info, own, sent, batches):
    arrays = [own] + [trade(x, "batch", m + 1) for m, x in enumerate(sent)]
    total = call(sum_kernel, info, arrays, (), (), [moved(own.shape, bf16)], [], "total")[0]
    return join(info, [total] + [trade(total, "batch", m) for m in range(1, batches)], 0, 1)


def all_sum(info, keep, send):
    rows, width = keep.shape
    chips, batches = lax.axis_size("seq") // 2, lax.axis_size("batch")
    shape = (chips, batches, rows // (chips * batches), width)
    own = split(info, [keep.reshape(shape), trade(send, "seq", 1).reshape(shape)], 1, 0)
    own = split(info, [own[0]] + [trade(x, "seq", 2 * m) for m, x in enumerate(own) if m], 0, 1)
    total = sum_along(info, own[0], own[1:], batches)
    total = join(info, [total] + [trade(total, "seq", 2 * m) for m in range(1, chips)], 1, 0).reshape(rows, width)
    return total, trade(total, "seq", 1)


def all_sum_slowly(info, keep, send):
    rows, width = keep.shape
    chips, batches = lax.axis_size("seq") // 2, lax.axis_size("batch")
    groups = [[2 * chip + core for chip in range(chips)] for core in range(2)]
    whole = call(sum_kernel, info, [keep, trade(send, "seq", 1)], (), (), [moved(keep.shape, bf16)], [], "total")[0]
    own = lax.psum_scatter(whole, "seq", axis_index_groups=groups, tiled=True)

    def finish(own, after):
        own, _ = lax.optimization_barrier((own, after))
        own = split(info, [own.reshape(batches, rows // (chips * batches), width)], 0, 1)
        total = sum_along(info, own[0], own[1:], batches).reshape(rows // chips, width)
        total = lax.all_gather(total, "seq", axis_index_groups=groups, tiled=True)
        return total, trade(total, "seq", 1)

    return partial(finish, own)


def results_kernel(k, parts, info_ref, *refs):
    pairs = len(parts)
    halves_refs = refs[: 2 * pairs]
    outs, wide_ref, sems = refs[-5:-2], refs[-2], refs[-1]
    even = info_ref[0] % 2 == 0
    width = wide_ref.shape[2]
    copies = []
    slot = 0
    for n, pieces in enumerate(parts):
        mine_ref, other_ref = halves_refs[2 * n : 2 * n + 2]
        first = 0
        for rows, low, high in pieces:
            mine = mine_ref[first : first + rows, :width].astype(f32)
            other = other_ref[first : first + rows, :width].astype(f32)
            for value, (out, row, column) in (
                (jnp.where(even, mine, other), low),
                (jnp.where(even, other, mine), high),
            ):
                wide_ref[slot, :rows, :] = value
                copy = pltpu.make_async_copy(
                    wide_ref.at[slot, pl.ds(0, rows), :],
                    outs[out].at[k, pl.ds(row, rows), pl.ds(column, width)],
                    sems.at[slot],
                )
                copy.start()
                copies.append(copy)
                slot += 1
            first += rows
    for copy in copies:
        copy.wait()


def results(k, info, parts, pairs, width, into):
    arrays = [half for pair in pairs for half in pair]
    slots = 2 * sum(len(p) for p in parts)
    shapes = [(2, width, 2 * width), (2, width, width), (2, width, width)]
    anywhere = pl.BlockSpec(memory_space=pl.ANY)
    into = list(into)
    return pl.pallas_call(
        partial(results_kernel, k, parts),
        in_specs=[in_smem] + [in_vmem] * len(arrays) + [anywhere] * len(into),
        out_specs=[anywhere] * 3,
        out_shape=[jax.ShapeDtypeStruct(shape, f32) for shape in shapes],
        scratch_shapes=[pltpu.VMEM((slots, width, width), f32), pltpu.SemaphoreType.DMA((slots,))],
        input_output_aliases={1 + len(arrays) + i: i for i in range(len(into))},
        compiler_params=pltpu.CompilerParams(vmem_limit_bytes=VMEM_LIMIT),
        name="results",
    )(info, *arrays, *into)


def leave_kernel(seqs, info_ref, rows_ref, out_ref, wide_ref):
    _, span, width = out_ref.shape
    wide_ref[...] = rows_ref[...].astype(f32).reshape(wide_ref.shape)
    shuffle = shuffle_matrix(span, True)
    for s in range(seqs):
        out_ref[s] = dot(shuffle, wide_ref[:, s].reshape(span, width).astype(bf16)).astype(bf16)


def leave(info, rows, seqs):
    span, width = rows.shape[0] // seqs, rows.shape[1]
    scratch = [pltpu.VMEM((span // CHUNKS, seqs, CHUNKS, width), f32)]
    outs = [moved((seqs, span, width), bf16)]
    return call(partial(leave_kernel, seqs), info, (rows,), (), (), outs, scratch, "leave")[0]


def input_grad_kernel(
    info_ref, sums_ref, tokens_ref, ahead_ref, stats_ref, gain_ref, count_ref, grad_ref, total_ref, wide_ref
):
    seqs, span, width = tokens_ref.shape
    where = Where(info_ref, seqs, span)
    wide_ref[...] = ahead_ref[...].astype(f32).reshape(wide_ref.shape)
    shuffle = shuffle_matrix(span, True)
    sums = jnp.sum(sums_ref[...], axis=0)
    total_ref[...] = sums
    average, root = stats_ref[0:1, :], stats_ref[1:2, :]
    factor = root * gain_ref[0:1, :] / count_ref[0:1, 0:1]
    by_gain = factor * sums[0:1, :width] * root
    fixed = factor * sums[1:2, :width] - by_gain * average
    step = lax.broadcasted_iota(jnp.int32, (span, 1), 0)
    for s in range(seqs):
        valid = (step < where.lefts[s]).astype(f32)
        ahead = dot(shuffle, wide_ref[:, s].reshape(span, width).astype(bf16))
        grad_ref[s] = (ahead - valid * (fixed + by_gain * tokens_ref[s].astype(f32))).astype(bf16)


def input_grads(info, sums, tokens, ahead, stats, gain, count):
    seqs, span, width = tokens.shape
    outs = [moved(tokens.shape, bf16), moved(sums.shape[1:], f32)]
    scratch = [pltpu.VMEM((span // CHUNKS, seqs, CHUNKS, width), f32)]
    return call(
        input_grad_kernel, info, (sums, tokens), (ahead, stats, gain, count), (), outs, scratch, "input_grad"
    )


def rotation_decay(decay_log, phase_log):
    decay_rate = jnp.exp(decay_log)
    magnitude = jnp.exp(-decay_rate)
    phase_angle = jnp.exp(phase_log)
    return (
        magnitude * jnp.cos(phase_angle),
        magnitude * jnp.sin(phase_angle),
        jnp.sqrt(1.0 - jnp.exp(-2.0 * decay_rate)),
    )


def to_all(x, axes):
    return lax.all_to_all(x, axes, split_axis=0, concat_axis=0, tiled=True)


def local(
    tokens,
    lengths,
    cotangent,
    norm_gain,
    norm_shift,
    lift_weight,
    decay_log,
    phase_log,
    skip_gain,
    mix_weight,
    glu_weight,
    glu_bias,
):
    both = ("seq", "batch")
    seq_devices = lax.axis_size("seq")
    devices = seq_devices * lax.axis_size("batch")
    seqs, span, width = tokens.shape
    rows = seqs * span
    states = decay_log.shape[1]
    info = jnp.concatenate(
        [jnp.stack([lax.axis_index("seq"), lax.axis_index("batch")]).astype(jnp.int32), lengths]
    )

    x0, sums = enter(info, tokens, devices)
    sums = to_all(sums, both)
    lam, scale, *tables = power_tables(info, decay_log, phase_log, seqs, seq_devices, span)

    power, leaps = tables[0:2]
    normed0, lifted0, ends, part, stats0, count = lift(
        0, seqs, seq_devices, info, sums, (x0, norm_gain, norm_shift, lift_weight, lam, scale, power)
    )
    weights = (mix_weight, skip_gain, glu_weight, glu_bias, lam, scale)
    x1, sums, state0, activated0, slope0, gate0, gate_slope0, low_x1 = mix(
        0, info, to_all(part, "seq"), (leaps, ends, power, lifted0, normed0, x0, *weights), devices
    )
    sums = to_all(sums, both)

    power, leaps = tables[4:6]
    normed1, lifted1, ends, part, stats1 = lift(
        1, seqs, seq_devices, info, sums, (count, x1, norm_gain, norm_shift, lift_weight, lam, scale, power)
    )
    state1, activated1, slope1, gate1, gate_slope1, masked = mix(
        1, info, to_all(part, "seq"), (leaps, ends, power, lifted1, normed1, x1, *weights), devices
    )

    power, leaps = tables[6:8]
    projected1, mixed1, dh, bias_grad1, skip_grad1, ends, part, back = glu_back(
        1, seqs, seq_devices, info, (),
        (cotangent, normed1, slope1, gate1, gate_slope1, glu_weight, mix_weight, lam, power), (),
    )
    back_lifted1, sums, back_normed, lam_grad1, scale_grad1 = lift_back(
        1, info, to_all(part, "seq"),
        (leaps, ends, power, dh, mixed1, stats1, lift_weight, skip_gain, lam, scale, lifted1, state1, x1), (), devices,
    )
    sums = to_all(sums, both)
    pieces = (((0, 0, width, 0), (1, 0, width, 0)), ((0, 0, width, width), (2, 0, width, 0)))
    keep, send = halves(
        info, pieces, (activated1, projected1, state1, mixed1, normed1, back_lifted1), 2 * width, width, "halves1"
    )
    finish1 = all_sum_slowly(info, keep, send)

    power, leaps = tables[2:4]
    projected0, mixed0, dh, bias_grad0, skip_grad0, ends, part, back, norm_sums1 = glu_back(
        0, seqs, seq_devices, info, (sums,),
        (back_normed, stats1, norm_gain, count, glu_weight, mix_weight, lam, power),
        (low_x1, back, normed0, slope0, gate0, gate_slope0),
    )
    small = (skip_grad0, bias_grad0, skip_grad1, bias_grad1, lam_grad1, scale_grad1)
    back_lifted0, sums, ahead = lift_back(
        0, info, to_all(part, "seq"),
        (leaps, ends, power, dh, mixed0, stats0, lift_weight, skip_gain, lam, scale, back, norm_gain, *small),
        (lifted0, state0, x0), devices,
    )
    sums = to_all(sums, both)
    half = width // 2
    pieces = (
        ((0, 0, width, 0), (0, 0, width, width)),
        ((1, 0, half, 0), (1, half, half, 0)),
        ((2, 0, half, 0), (2, half, half, 0)),
    )
    keep, send = halves(
        info, pieces, (activated0, projected0, state0, mixed0, normed0, back_lifted0), 2 * width, width, "halves0"
    )
    total0 = all_sum(info, keep, send)
    total1 = finish1(keep)
    input_grad, sums = input_grads(info, sums, tokens, ahead, stats0, norm_gain, count)
    produced = leave(info, masked, seqs)

    grads = results(1, info, (((width, (0, 0, 0), (1, 0, 0)), (width, (0, 0, width), (2, 0, 0))),), [total1], width, ())
    parts = ((width, (0, 0, 0), (0, 0, width)), (half, (1, 0, 0), (1, half, 0)), (half, (2, 0, 0), (2, half, 0)))
    grad_glu, grad_mix, grad_lift = results(0, info, (parts,), [total0], width, grads)

    inner, outer = sums[:, :width], sums[:, width:]
    lam_grad = outer[0:4].reshape(2, 2, states)
    grad_decay, grad_phase = jax.vjp(rotation_decay, decay_log, phase_log)[1](
        (lam_grad[:, 0], lam_grad[:, 1], outer[4:6])
    )
    return (
        produced,
        input_grad,
        jnp.stack([inner[0], norm_sums1[0]]),
        jnp.stack([inner[1], norm_sums1[1]]),
        grad_lift,
        grad_decay,
        grad_phase,
        inner[2:4],
        grad_mix,
        grad_glu,
        inner[4:8].reshape(2, 2 * width),
    )


def solution(mesh):
    split = P("batch", "seq", None)
    placed = (split, P("batch"), split) + (P(),) * 9
    return jax.shard_map(
        local,
        mesh=mesh,
        in_specs=placed,
        out_specs=(split, split) + (P(),) * 9,
        check_vma=False,
    )
```

time: 1230 us -> 243 us (0.20); the launches traced: 1220 us -> 242 us
  local copies, waits for them, and re-layouts: 535 us -> 23.7 us
  other arithmetic: 264 us -> 2.13 us
  blocking collectives: 163 us -> 49.9 us
  waiting for transfers between devices: 160 us -> 54.2 us
  Pallas kernels: 0 us -> 61.4 us
  matrix products: 42.5 us -> 0 us
    psum x4 -> x0, blocking collectives: 163 us -> none  [the longest x2 81.7 us: local(): lax.psum((jnp.sum(back_normed * centered, axis=(0, 1)), jnp.sum(back_norm...]
    another operation x46 -> x0, local copies, waits for them, and re-layouts: 160 us -> none  [the longest x32 116 us: linear_chain(): running_real = lax.cumsum(weighted_real, axis=1, reverse=backwards)]
    psum x1 -> x0, waiting for transfers between devices: 122 us -> none  [local(): lax.psum((weight_grads[0][0], weight_grads[0][1], weight_grads[0][2], wei...]
    slice x316 -> x6, local copies, waits for them, and re-layouts: 105 us -> 0.62 us  [the longest x1 0.6 us: local(): inner[2:4]]
    another operation x30 -> x1, other arithmetic: 103 us -> 0.61 us  [local(): jnp.stack([inner[0], norm_sums1[0]])]
    mul x40 -> x0, local copies, waits for them, and re-layouts: 94.8 us -> none  [the longest x12 26.7 us: linear_chain(): power_imaginary * start_imaginary[:, None]]
    pallas_call x0 -> x25, Pallas kernels: none -> 61.4 us  [the longest x23 54.2 us: call(): pl.pallas_call(kernel, in_specs=[in_smem] + [in_vmem] * (len(inputs) + le...]
    mul x6 -> x1, other arithmetic: 55.6 us -> 0.64 us  [rotation_decay(): phase_angle = jnp.exp(phase_log)]
  transfers between devices with their start and end apart: 9 -> 26, of which waited for: 7 -> 15; matrix products, arithmetic and copies ran while one was open for 11% -> 1% of each run, Pallas kernels for 0% -> 13%
where the time goes in v1:
time: 243 us; the launch traced here: 242 us
  Pallas kernels  61.4 us (25%)
  waiting for transfers between devices  54.2 us (22%)
  blocking collectives  49.9 us (21%)
  starting transfers between devices  36.6 us (15%)
  local copies, waits for them, and re-layouts  23.7 us (10%)
  between operations  14.5 us (6%)
    pallas_call x23, Pallas kernels, call(): pl.pallas_call(kernel, in_specs=[in_smem] + [in_vmem] * (len(inputs) + le...  54.2 us
    ppermute x22, waiting for transfers between devices, trade(): return lax.ppermute(x, axis, [(i, i ^ mask) for i in range(size)])  51.1 us
    all_to_all x6, blocking collectives, to_all(): return lax.all_to_all(x, axes, split_axis=0, concat_axis=0, tiled=True)  49.9 us
    ppermute x22, starting transfers between devices, trade(): return lax.ppermute(x, axis, [(i, i ^ mask) for i in range(size)])  25.5 us
    unnamed x94, local copies, waits for them, and re-layouts  22.4 us
    all_to_all x2, starting transfers between devices, to_all(): return lax.all_to_all(x, axes, split_axis=0, concat_axis=0, tiled=True)  11 us
    pallas_call x2, Pallas kernels, results(): pl.pallas_call(partial(results_kernel, k, parts), in_specs=[in_smem] + [i...  7.2 us
  transfers between devices with their start and end apart: 26, of which 15 were waited for; matrix products, arithmetic and copies ran while one was open for 1% of the time, Pallas kernels for 13%

profile of v1, /device:TPU:0, one launch (start us, length us, event | category | flops | bytes accessed | tf_op | source)
XLA Modules:
  0.0 242.5 jit_solution(14762522649463867543)
XLA Ops:
  12.3 7.3 %all-to-all-start = ((f32[32,2,640]{2,1,0:T(2,128)}), f32[32,2,640]{2,1,0:T(2,128)S(1)}, u32[]{:S(2)}, u32[]{:S(2)}) async-start(f32[32,2,640]{2,1,0:T(2,128)} %get-tuple-element.98), calls=%async_computation | async-start | bytes 327680 | tf_op jit(solution)/shard_map/all_to_all | solution.py:878
  25.4 3.1 %all-to-all-done.sums_ref = f32[32,2,640]{2,1,0:T(2,128)S(1)} async-done(((f32[32,2,640]{2,1,0:T(2,128)}), f32[32,2,640]{2,1,0:T(2,128)S(1)}, u32[]{:S(2)}, u32[]{:S(2)}) %all-to-all-start) | async-done | bytes 163872 | tf_op jit(solution)/shard_map/all_to_all | solution.py:878
  33.8 7.4 %all_to_all.40.parts_ref = f32[8,4,512]{2,1,0:T(4,128)S(1)} all-to-all(f32[8,4,512]{2,1,0:T(4,128)S(1)} %get-tuple-element.103), channel_id=1, replica_groups=mesh['seq'=8,'batch'=4] {'seq'}, dimensions={0} | all-to-all | bytes 131072 | tf_op jit(solution)/shard_map/all_to_all | solution.py:878
  42.4 5.9 %mix.2 = (f32[1024,512]{1,0:T(8,128)S(1)}, f32[32,2,512]{2,1,0:T(2,128)S(1)}, bf16[1024,512]{1,0:T(8,128)(2,1)}, bf16[1024,512]{1,0:T(8,128)(2,1)}, bf16[1024,51...) custom-call(s32[6]{0:T(128)S(1)} %pad_add_fusion.info_ref, ...), custom_call_target="tpu_custom_call" | custom-call | tf_op jit(solution)/shard_map/mix/pallas_call | solution.py:39
  49.3 10.2 %all_to_all.41.sums_ref = f32[32,2,512]{2,1,0:T(2,128)S(1)} all-to-all(f32[32,2,512]{2,1,0:T(2,128)S(1)} %get-tuple-element.108), channel_id=1, replica_groups=mesh['seq'=8,'batch'=4] {'seq','batch'}, dimensions={0} | all-to-all | bytes 262144 | tf_op jit(solution)/shard_map/all_to_all | solution.py:878
  61.4 7.4 %all_to_all.42.parts_ref = f32[8,4,512]{2,1,0:T(4,128)S(1)} all-to-all(f32[8,4,512]{2,1,0:T(4,128)S(1)} %get-tuple-element.112), channel_id=1, replica_groups=mesh['seq'=8,'batch'=4] {'seq'}, dimensions={0} | all-to-all | bytes 131072 | tf_op jit(solution)/shard_map/all_to_all | solution.py:878
  68.8 5.4 %mix.3 = (bf16[1024,512]{1,0:T(8,128)(2,1)S(1)}, bf16[1024,512]{1,0:T(8,128)(2,1)S(1)}, bf16[1024,512]{1,0:T(8,128)(2,1)S(1)}, bf16[1024,512]{1,0:T(8,128)(2,1)S...) custom-call(s32[6]{0:T(128)S(1)} %pad_add_fusion.info_ref, f32[8,4,512]{2,1,0:T(4,128)S(1)} %all_to_all.42.parts_ref, ...), custom_call_target="tpu_custom_call" | custom-call | tf_op jit(solution)/shard_map/mix/pallas_call | solution.py:39
  74.2 3.9 %glu_back.2 = (bf16[1024,1024]{1,0:T(8,128)(2,1)S(1)}, bf16[1024,512]{1,0:T(8,128)(2,1)S(1)}, bf16[1024,512]{1,0:T(8,128)(2,1)S(1)}, f32[1,1024]{1,0:T(1,128)S(1...) custom-call(s32[6]{0:T(128)S(1)} %pad_add_fusion.info_ref, ...), custom_call_target="tpu_custom_call" | custom-call | tf_op jit(solution)/shard_map/glu_back/pallas_call | solution.py:39
  78.1 7.4 %all_to_all.43.parts_ref = f32[8,4,512]{2,1,0:T(4,128)S(1)} all-to-all(f32[8,4,512]{2,1,0:T(4,128)S(1)} %get-tuple-element.122), channel_id=1, replica_groups=mesh['seq'=8,'batch'=4] {'seq'}, dimensions={0} | all-to-all | bytes 131072 | tf_op jit(solution)/shard_map/all_to_all | solution.py:878
  88.2 2.9 %halves1.1 = (bf16[1024,512]{1,0:T(8,128)(2,1)S(1)}, bf16[1024,512]{1,0:T(8,128)(2,1)S(1)}) custom-call(s32[6]{0:T(128)S(1)} %pad_add_fusion.info_ref, bf16[1024,512]{1,0:T(8,128)(2,1)S(1)} %get-tuple-element.169.refs_0_, bf16[1024,1024]{1,0:T(8,128)(2,1)S(1)} %get-tuple-element.170.refs_1_, bf16[1024,512]{1,0:T(8,128)(2,1)S(1)} %get-tuple-element.128.refs_11_.refs_2_, ...), custom_call_target="tpu_custom_call" | custom-call | tf_op jit(solution)/shard_map/halves1/pallas_call | solution.py:39
  95.6 10.1 %all_to_all.44.refs_0_ = f32[32,2,512]{2,1,0:T(2,128)S(1)} all-to-all(f32[32,2,512]{2,1,0:T(2,128)S(1)} %get-tuple-element.129), channel_id=1, replica_groups=mesh['seq'=8,'batch'=4] {'seq','batch'}, dimensions={0} | all-to-all | bytes 262144 | tf_op jit(solution)/shard_map/all_to_all | solution.py:878
  108.2 6.1 %glu_back.3 = (bf16[1024,1024]{1,0:T(8,128)(2,1)S(1)}, bf16[1024,512]{1,0:T(8,128)(2,1)S(1)}, bf16[1024,512]{1,0:T(8,128)(2,1)S(1)}, f32[1,1024]{1,0:T(1,128)S(1...) custom-call(s32[6]{0:T(128)S(1)} %pad_add_fusion.info_ref, ...), custom_call_target="tpu_custom_call" | custom-call | tf_op jit(solution)/shard_map/glu_back/pallas_call | solution.py:39
  114.4 7.4 %all_to_all.45.parts_ref = f32[8,4,512]{2,1,0:T(4,128)S(1)} all-to-all(f32[8,4,512]{2,1,0:T(4,128)S(1)} %get-tuple-element.137), channel_id=1, replica_groups=mesh['seq'=8,'batch'=4] {'seq'}, dimensions={0} | all-to-all | bytes 131072 | tf_op jit(solution)/shard_map/all_to_all | solution.py:878
  121.8 4.6 %lift_back.3 = (bf16[1024,512]{1,0:T(8,128)(2,1)S(1)}, f32[32,8,768]{2,1,0:T(8,128)S(1)}, bf16[1024,512]{1,0:T(8,128)(2,1)S(1)}) custom-call(s32[6]{0:T(128)S(1)} %pad_add_fusion.info_ref, f32[8,4,512]{2,1,0:T(4,128)S(1)} %all_to_all.45.parts_ref, f32[32,512]{1,0:T(8,128)S(1)} %copy-done.32, f32[4,32,128]{2,1,0:T(8,128)S(1)} %get-tuple-element.139.refs_1_, ...), custom_call_target="tpu_custom_call" | custom-call | tf_op jit(solution)/shard_map/lift_back/pallas_call | solution.py:39
  127.4 3.9 %halves0.1 = (bf16[1024,512]{1,0:T(8,128)(2,1)S(1)}, bf16[1024,512]{1,0:T(8,128)(2,1)}) custom-call(s32[6]{0:T(128)S(1)} %pad_add_fusion.info_ref, bf16[1024,512]{1,0:T(8,128)(2,1)S(1)} %copy-done.21, bf16[1024,1024]{1,0:T(8,128)(2,1)S(1)} %get-tuple-element.157.refs_1_, bf16[1024,512]{1,0:T(8,128)(2,1)S(1)} %copy-done.13, ...), custom_call_target="tpu_custom_call" | custom-call | tf_op jit(solution)/shard_map/halves0/pallas_call | solution.py:39
  139.5 3.2 %collective-permute-done.16.refs_2_ = bf16[64,512]{1,0:T(8,128)(2,1)S(1)} collective-permute-done((bf16[64,512]{1,0:T(8,128)(2,1)S(1)}, bf16[64,512]{1,0:T(8,128)(2,1)S(1)}, u32[]{:S(2)}, u32[]{:S(2)}) %collective-permute-start.16) | collective-permute-done | bytes 65568 | tf_op jit(solution)/shard_map/ppermute | solution.py:735
  153.0 3.7 %all-to-all-start.7 = ((f32[32,8,768]{2,1,0:T(8,128)}), f32[32,8,768]{2,1,0:T(8,128)}, u32[]{:S(2)}, u32[]{:S(2)}) async-start(f32[32,8,768]{2,1,0:T(8,128)} %copy-done.24), calls=%async_computation.7 | async-start | bytes 1572864 | tf_op jit(solution)/shard_map/all_to_all | solution.py:878
  161.2 15.1 %collective-permute-done.1.refs_1_ = bf16[4,64,512]{2,1,0:T(8,128)(2,1)S(1)} collective-permute-done((bf16[4,64,512]{2,1,0:T(8,128)(2,1)S(1)}, bf16[4,64,512]{2,1,0:T(8,128)(2,1)S(1)}, u32[]{:S(2)}, u32[]{:S(2)}) %collective-permute-start.1) | collective-permute-done | bytes 262176 | tf_op jit(solution)/shard_map/ppermute | solution.py:735
  176.2 8.6 %collective-permute-done.3.refs_3_ = bf16[4,64,512]{2,1,0:T(8,128)(2,1)S(1)} collective-permute-done((bf16[4,64,512]{2,1,0:T(8,128)(2,1)S(1)}, bf16[4,64,512]{2,1,0:T(8,128)(2,1)S(1)}, u32[]{:S(2)}, u32[]{:S(2)}) %collective-permute-start.3) | collective-permute-done | bytes 262176 | tf_op jit(solution)/shard_map/ppermute | solution.py:735
  190.3 3.4 %collective-permute-done.5.refs_2_ = bf16[64,512]{1,0:T(8,128)(2,1)S(1)} collective-permute-done((bf16[64,512]{1,0:T(8,128)(2,1)S(1)}, bf16[64,512]{1,0:T(8,128)(2,1)S(1)}, u32[]{:S(2)}, u32[]{:S(2)}) %collective-permute-start.5) | collective-permute-done | bytes 65568 | tf_op jit(solution)/shard_map/ppermute | solution.py:735
  197.5 3.1 %collective-permute-start.7 = (bf16[64,512]{1,0:T(8,128)(2,1)S(1)}, bf16[64,512]{1,0:T(8,128)(2,1)S(1)}, u32[]{:S(2)}, u32[]{:S(2)}) collective-permute-start(bf16[64,512]{1,0:T(8,128)(2,1)S(1)} %total.3.refs_0_), channel_id=1, source_target_pairs={{0,1},{1,0},{2,3},{3,2},{4,5},{5,4},{6,7},{7,6},{8,9},{9,8},{10,11... | collective-permute-start | bytes 196616 | tf_op jit(solution)/shard_map/ppermute | solution.py:735
  207.8 5.7 %collective-permute-done.12.refs_3_ = bf16[4,64,512]{2,1,0:T(8,128)(2,1)S(1)} collective-permute-done((bf16[4,64,512]{2,1,0:T(8,128)(2,1)S(1)}, bf16[4,64,512]{2,1,0:T(8,128)(2,1)S(1)}, u32[]{:S(2)}, u32[]{:S(2)}) %collective-permute-start.12) | collective-permute-done | bytes 262176 | tf_op jit(solution)/shard_map/ppermute | solution.py:735
  228.4 3.4 %results.2 = (f32[2,512,1024]{2,1,0:T(8,128)}, f32[2,512,512]{2,1,0:T(8,128)}, f32[2,512,512]{2,1,0:T(8,128)}) custom-call(s32[6]{0:T(128)S(1)} %pad_add_fusion.info_ref, bf16[1024,512]{1,0:T(8,128)(2,1)S(1)} %copy-done.15, bf16[1024,512]{1,0:T(8,128)(2,1)} %collective-permute-done.21.refs_1_), custom_call_target="tpu_custom_call" | custom-call | tf_op jit(solution)/shard_map/results/pallas_call | solution.py:810
  231.9 3.8 %results.3 = (f32[2,512,1024]{2,1,0:T(8,128)}, f32[2,512,512]{2,1,0:T(8,128)}, f32[2,512,512]{2,1,0:T(8,128)}) custom-call(s32[6]{0:T(128)S(1)} %pad_add_fusion.info_ref, bf16[1024,512]{1,0:T(8,128)(2,1)} %bitcast.4.refs_0_, bf16[1024,512]{1,0:T(8,128)(2,1)} %collective-permute-done.13.refs_1_, ...), custom_call_target="tpu_custom_call", output_to_operand_aliasing={{0}: (3, {}), {1}: (4, {}), {2}: (5, {})} | custom-call | tf_op jit(solution)/shard_map/results/pallas_call | solution.py:810
  (166 shorter events, 84.9 us)
Async XLA Ops:
  12.3 16.2 %all-to-all-start = ((f32[32,2,640]{2,1,0:T(2,128)}), f32[32,2,640]{2,1,0:T(2,128)S(1)}, u32[]{:S(2)}, u32[]{:S(2)}) async-start(f32[32,2,640]{2,1,0:T(2,128)} %get-tuple-element.98), calls=%async_computation | async-start | bytes 327680 | tf_op jit(solution)/shard_map/all_to_all | solution.py:878
  19.6 112.7 %reduce-scatter.2.cloned.1.call-start = ((), (), s32[]{:S(2)}) async-start(), calls=%async_computation.9 | async-start | bytes 1310720 | tf_op jit(solution)/shard_map/reduce_scatter | solution.py:760
  95.6 121.5 %all-gather.2.cloned.1.call-start = ((), (), s32[]{:S(2)}) async-start(), calls=%async_computation.10 | async-start | bytes 1310720 | tf_op jit(solution)/shard_map/all_gather | solution.py:766
  132.3 24.5 %collective-permute-start = (bf16[1024,512]{1,0:T(8,128)(2,1)}, bf16[1024,512]{1,0:T(8,128)(2,1)S(1)}, u32[]{:S(2)}, u32[]{:S(2)}) collective-permute-start(bf16[1024,512]{1,0:T(8,128)(2,1)} %get-tuple-element.160), channel_id=1, source_target_pairs={{0,4},{4,0},{8,12},{12,8},{16,20},{20,16},{24,28},{28,24},{1,5},{5... | collective-permute-start | bytes 3145736 | tf_op jit(solution)/shard_map/ppermute | solution.py:735
  133.8 5.6 %collective-permute-start.15 = (bf16[64,512]{1,0:T(8,128)(2,1)S(1)}, bf16[64,512]{1,0:T(8,128)(2,1)S(1)}, u32[]{:S(2)}, u32[]{:S(2)}) collective-permute-start(bf16[64,512]{1,0:T(8,128)(2,1)S(1)} %get-tuple-element.176), channel_id=1, source_target_pairs={{0,1},{1,0},{2,3},{3,2},{4,5},{5,4},{6,7},{7,6},{8,9},{9,8},{10,11... | collective-permute-start | bytes 196616 | tf_op jit(solution)/shard_map/ppermute | solution.py:735
  134.2 8.5 %collective-permute-start.16 = (bf16[64,512]{1,0:T(8,128)(2,1)S(1)}, bf16[64,512]{1,0:T(8,128)(2,1)S(1)}, u32[]{:S(2)}, u32[]{:S(2)}) collective-permute-start(bf16[64,512]{1,0:T(8,128)(2,1)S(1)} %get-tuple-element.177), channel_id=1, source_target_pairs={{0,2},{1,3},{2,0},{3,1},{4,6},{5,7},{6,4},{7,5},{8,10},{9,11},{10,... | collective-permute-start | bytes 196616 | tf_op jit(solution)/shard_map/ppermute | solution.py:735
  136.2 6.4 %collective-permute-start.17 = (bf16[64,512]{1,0:T(8,128)(2,1)S(1)}, bf16[64,512]{1,0:T(8,128)(2,1)S(1)}, u32[]{:S(2)}, u32[]{:S(2)}) collective-permute-start(bf16[64,512]{1,0:T(8,128)(2,1)S(1)} %get-tuple-element.178), channel_id=1, source_target_pairs={{0,3},{1,2},{2,1},{3,0},{4,7},{5,6},{6,5},{7,4},{8,11},{9,10},{10,... | collective-permute-start | bytes 196616 | tf_op jit(solution)/shard_map/ppermute | solution.py:735
  143.2 6.8 %collective-permute-start.20 = (bf16[64,512]{1,0:T(8,128)(2,1)S(1)}, bf16[64,512]{1,0:T(8,128)(2,1)S(1)}, u32[]{:S(2)}, u32[]{:S(2)}) collective-permute-start(bf16[64,512]{1,0:T(8,128)(2,1)S(1)} %total.5.refs_0_), channel_id=1, source_target_pairs={{0,3},{1,2},{2,1},{3,0},{4,7},{5,6},{6,5},{7,4},{8,11},{9,10},{10,... | collective-permute-start | bytes 196616 | tf_op jit(solution)/shard_map/ppermute | solution.py:735
  145.7 6.1 %collective-permute-start.19 = (bf16[64,512]{1,0:T(8,128)(2,1)S(1)}, bf16[64,512]{1,0:T(8,128)(2,1)S(1)}, u32[]{:S(2)}, u32[]{:S(2)}) collective-permute-start(bf16[64,512]{1,0:T(8,128)(2,1)S(1)} %total.5.refs_0_), channel_id=1, source_target_pairs={{0,2},{1,3},{2,0},{3,1},{4,6},{5,7},{6,4},{7,5},{8,10},{9,11},{10,... | collective-permute-start | bytes 196616 | tf_op jit(solution)/shard_map/ppermute | solution.py:735
  146.3 5.5 %collective-permute-start.18 = (bf16[64,512]{1,0:T(8,128)(2,1)S(1)}, bf16[64,512]{1,0:T(8,128)(2,1)S(1)}, u32[]{:S(2)}, u32[]{:S(2)}) collective-permute-start(bf16[64,512]{1,0:T(8,128)(2,1)S(1)} %total.5.refs_0_), channel_id=1, source_target_pairs={{0,1},{1,0},{2,3},{3,2},{4,5},{5,4},{6,7},{7,6},{8,9},{9,8},{10,11... | collective-permute-start | bytes 196616 | tf_op jit(solution)/shard_map/ppermute | solution.py:735
  153.0 67.7 %all-to-all-start.7 = ((f32[32,8,768]{2,1,0:T(8,128)}), f32[32,8,768]{2,1,0:T(8,128)}, u32[]{:S(2)}, u32[]{:S(2)}) async-start(f32[32,8,768]{2,1,0:T(8,128)} %copy-done.24), calls=%async_computation.7 | async-start | bytes 1572864 | tf_op jit(solution)/shard_map/all_to_all | solution.py:878
  157.6 18.6 %collective-permute-start.1 = (bf16[4,64,512]{2,1,0:T(8,128)(2,1)S(1)}, bf16[4,64,512]{2,1,0:T(8,128)(2,1)S(1)}, u32[]{:S(2)}, u32[]{:S(2)}) collective-permute-start(bf16[4,64,512]{2,1,0:T(8,128)(2,1)S(1)} %get-tuple-element.162), channel_id=1, source_target_pairs={{0,8},{4,12},{8,0},{12,4},{16,24},{20,28},{24,16},{28,20},{1,9},{5... | collective-permute-start | bytes 786440 | tf_op jit(solution)/shard_map/ppermute | solution.py:735
  159.0 17.2 %collective-permute-start.2 = (bf16[4,64,512]{2,1,0:T(8,128)(2,1)S(1)}, bf16[4,64,512]{2,1,0:T(8,128)(2,1)S(1)}, u32[]{:S(2)}, u32[]{:S(2)}) collective-permute-start(bf16[4,64,512]{2,1,0:T(8,128)(2,1)S(1)} %get-tuple-element.163), channel_id=1, source_target_pairs={{0,16},{4,20},{8,24},{12,28},{16,0},{20,4},{24,8},{28,12},{1,17},{... | collective-permute-start | bytes 786440 | tf_op jit(solution)/shard_map/ppermute | solution.py:735
  160.5 24.3 %collective-permute-start.3 = (bf16[4,64,512]{2,1,0:T(8,128)(2,1)S(1)}, bf16[4,64,512]{2,1,0:T(8,128)(2,1)S(1)}, u32[]{:S(2)}, u32[]{:S(2)}) collective-permute-start(bf16[4,64,512]{2,1,0:T(8,128)(2,1)S(1)} %get-tuple-element.164), channel_id=1, source_target_pairs={{0,24},{4,28},{8,16},{12,20},{16,8},{20,12},{24,0},{28,4},{1,25},{... | collective-permute-start | bytes 786440 | tf_op jit(solution)/shard_map/ppermute | solution.py:735
  187.1 6.6 %collective-permute-start.5 = (bf16[64,512]{1,0:T(8,128)(2,1)S(1)}, bf16[64,512]{1,0:T(8,128)(2,1)S(1)}, u32[]{:S(2)}, u32[]{:S(2)}) collective-permute-start(bf16[64,512]{1,0:T(8,128)(2,1)S(1)} %get-tuple-element.167), channel_id=1, source_target_pairs={{0,2},{1,3},{2,0},{3,1},{4,6},{5,7},{6,4},{7,5},{8,10},{9,11},{10,... | collective-permute-start | bytes 196616 | tf_op jit(solution)/shard_map/ppermute | solution.py:735
  189.4 6.1 %collective-permute-start.6 = (bf16[64,512]{1,0:T(8,128)(2,1)S(1)}, bf16[64,512]{1,0:T(8,128)(2,1)S(1)}, u32[]{:S(2)}, u32[]{:S(2)}) collective-permute-start(bf16[64,512]{1,0:T(8,128)(2,1)S(1)} %get-tuple-element.168), channel_id=1, source_target_pairs={{0,3},{1,2},{2,1},{3,0},{4,7},{5,6},{6,5},{7,4},{8,11},{9,10},{10,... | collective-permute-start | bytes 196616 | tf_op jit(solution)/shard_map/ppermute | solution.py:735
  196.1 6.2 %collective-permute-start.9 = (bf16[64,512]{1,0:T(8,128)(2,1)S(1)}, bf16[64,512]{1,0:T(8,128)(2,1)S(1)}, u32[]{:S(2)}, u32[]{:S(2)}) collective-permute-start(bf16[64,512]{1,0:T(8,128)(2,1)S(1)} %total.3.refs_0_), channel_id=1, source_target_pairs={{0,3},{1,2},{2,1},{3,0},{4,7},{5,6},{6,5},{7,4},{8,11},{9,10},{10,... | collective-permute-start | bytes 196616 | tf_op jit(solution)/shard_map/ppermute | solution.py:735
  197.5 6.1 %collective-permute-start.8 = (bf16[64,512]{1,0:T(8,128)(2,1)S(1)}, bf16[64,512]{1,0:T(8,128)(2,1)S(1)}, u32[]{:S(2)}, u32[]{:S(2)}) collective-permute-start(bf16[64,512]{1,0:T(8,128)(2,1)S(1)} %total.3.refs_0_), channel_id=1, source_target_pairs={{0,2},{1,3},{2,0},{3,1},{4,6},{5,7},{6,4},{7,5},{8,10},{9,11},{10,... | collective-permute-start | bytes 196616 | tf_op jit(solution)/shard_map/ppermute | solution.py:735
  197.5 6.1 %collective-permute-start.7 = (bf16[64,512]{1,0:T(8,128)(2,1)S(1)}, bf16[64,512]{1,0:T(8,128)(2,1)S(1)}, u32[]{:S(2)}, u32[]{:S(2)}) collective-permute-start(bf16[64,512]{1,0:T(8,128)(2,1)S(1)} %total.3.refs_0_), channel_id=1, source_target_pairs={{0,1},{1,0},{2,3},{3,2},{4,5},{5,4},{6,7},{7,6},{8,9},{9,8},{10,11... | collective-permute-start | bytes 196616 | tf_op jit(solution)/shard_map/ppermute | solution.py:735
  204.2 9.3 %collective-permute-start.12 = (bf16[4,64,512]{2,1,0:T(8,128)(2,1)S(1)}, bf16[4,64,512]{2,1,0:T(8,128)(2,1)S(1)}, u32[]{:S(2)}, u32[]{:S(2)}) collective-permute-start(bf16[4,64,512]{2,1,0:T(8,128)(2,1)S(1)} %join.3.refs_0_), channel_id=1, source_target_pairs={{0,24},{4,28},{8,16},{12,20},{16,8},{20,12},{24,0},{28,4},{1,25},{... | collective-permute-start | bytes 786440 | tf_op jit(solution)/shard_map/ppermute | solution.py:735
  204.9 10.6 %collective-permute-start.11 = (bf16[4,64,512]{2,1,0:T(8,128)(2,1)S(1)}, bf16[4,64,512]{2,1,0:T(8,128)(2,1)S(1)}, u32[]{:S(2)}, u32[]{:S(2)}) collective-permute-start(bf16[4,64,512]{2,1,0:T(8,128)(2,1)S(1)} %join.3.refs_0_), channel_id=1, source_target_pairs={{0,16},{4,20},{8,24},{12,28},{16,0},{20,4},{24,8},{28,12},{1,17},{... | collective-permute-start | bytes 786440 | tf_op jit(solution)/shard_map/ppermute | solution.py:735
  206.3 9.1 %collective-permute-start.10 = (bf16[4,64,512]{2,1,0:T(8,128)(2,1)S(1)}, bf16[4,64,512]{2,1,0:T(8,128)(2,1)S(1)}, u32[]{:S(2)}, u32[]{:S(2)}) collective-permute-start(bf16[4,64,512]{2,1,0:T(8,128)(2,1)S(1)} %join.3.refs_0_), channel_id=1, source_target_pairs={{0,8},{4,12},{8,0},{12,4},{16,24},{20,28},{24,16},{28,20},{1,9},{5... | collective-permute-start | bytes 786440 | tf_op jit(solution)/shard_map/ppermute | solution.py:735
  217.0 10.1 %collective-permute-start.21 = (bf16[1024,512]{1,0:T(8,128)(2,1)}, bf16[1024,512]{1,0:T(8,128)(2,1)}, u32[]{:S(2)}, u32[]{:S(2)}) collective-permute-start(bf16[1024,512]{1,0:T(8,128)(2,1)} %all-gather.2.cloned.1.call-done.refs_0_), channel_id=1, source_target_pairs={{0,4},{4,0},{8,12},{12,8},{16,20},{20,16},{24,28},{28,24},{1,5},{5... | collective-permute-start | bytes 3145736 | tf_op jit(solution)/shard_map/ppermute | solution.py:735
  217.0 14.8 %collective-permute-start.13 = (bf16[1024,512]{1,0:T(8,128)(2,1)}, bf16[1024,512]{1,0:T(8,128)(2,1)}, u32[]{:S(2)}, u32[]{:S(2)}) collective-permute-start(bf16[1024,512]{1,0:T(8,128)(2,1)} %bitcast.4.refs_0_), channel_id=1, source_target_pairs={{0,4},{4,0},{8,12},{12,8},{16,20},{20,16},{24,28},{28,24},{1,5},{5... | collective-permute-start | bytes 3145736 | tf_op jit(solution)/shard_map/ppermute | solution.py:735
  (49 other events, 299.9 us)
Sparse Core Ops, SparseCore 0:
  95.7 25.0 reduce-scatter.1
  153.2 35.3 all-gather.1

commit v2 on v1

v2 whole, which is shorter than its diff:
```python
from functools import partial

import jax
import jax.numpy as jnp
from jax import lax
from jax.experimental import pallas as pl
from jax.experimental.pallas import tpu as pltpu
from jax.sharding import PartitionSpec as P

norm_eps = 1e-05
f32 = jnp.float32
bf16 = jnp.bfloat16

CHUNKS = 8
BLOCKS = 4
PARTS = 1
EXTRA = 16
LANES = 128
VMEM_LIMIT = 24 * 1024 * 1024

in_vmem = pl.BlockSpec(memory_space=pltpu.VMEM)
in_smem = pl.BlockSpec(memory_space=pltpu.SMEM)
in_hbm = pl.BlockSpec(memory_space=pltpu.HBM)


def near(shape, dtype):
    return in_vmem, pltpu.VMEM(shape, dtype)


def moved(shape, dtype):
    return in_vmem, jax.ShapeDtypeStruct(shape, dtype)


def copy_parts(source, target, sems):
    size = source.shape[0] // sems.shape[0]
    cuts = [pl.ds(i * size, size) for i in range(sems.shape[0])]
    return [pltpu.make_async_copy(source.at[cut], target.at[cut], sems.at[i]) for i, cut in enumerate(cuts)]


def begin(copies):
    for copy in copies:
        copy.start()


def finished(copies):
    for copy in copies:
        copy.wait()


class Outs(list):
    tick = None


def run(body, info, given, specs, outs, scratch, name, after, aliases=(), us=None):
    cost = None
    if us is not None:
        cost = pl.CostEstimate(flops=int(us * 1.1e9), bytes_accessed=int(us * 3e6), transcendentals=0)
    after = [pltpu.with_memory_space_constraint(t, pltpu.HBM) for t in after]
    n_in, n_out = 1 + len(given), len(outs)

    def ticking(*refs):
        body(*refs[:n_in], *refs[n_in + len(after) : n_in + len(after) + n_out], *refs[n_in + len(after) + n_out + 1 :])

    out = pl.pallas_call(
        ticking,
        in_specs=[in_smem] + specs + [in_hbm] * len(after),
        out_specs=[spec for spec, _ in outs] + [in_hbm],
        out_shape=[shape for _, shape in outs] + [pltpu.HBM((8, LANES), f32)],
        scratch_shapes=scratch,
        input_output_aliases=dict(aliases),
        compiler_params=pltpu.CompilerParams(vmem_limit_bytes=VMEM_LIMIT),
        cost_estimate=cost,
        name=name,
    )(info, *given, *after)
    result = Outs(out[:n_out])
    result.tick = out[n_out]
    return result


def here(x):
    return pltpu.with_memory_space_constraint(x, pltpu.VMEM)


def there(x):
    return pltpu.with_memory_space_constraint(x, pltpu.HBM)


def call(kernel, info, inputs, arrays, away, outs, scratch, name, after=(), fetch=(), spill=(), us=None):
    first = 1 + len(inputs) + len(arrays) + len(away)
    n_copies = len(fetch) + len(spill)
    fetched = [jax.eval_shape(lambda x, at=at: x if at is None else x[at], a) for a, at in fetch]
    outs = list(outs)
    n_outs = len(outs)
    outs += [near(a.shape, a.dtype) for a in fetched] + [(in_hbm, pltpu.HBM(a.shape, a.dtype)) for a in spill]

    def body(*refs):
        ins, rest = refs[: first + n_copies], refs[first + n_copies :]
        sources = list(ins[first:])
        for i, (_, at) in enumerate(fetch):
            if at is not None:
                sources[i] = sources[i].at[at]
        targets = rest[n_outs : n_outs + n_copies]
        rest = rest[:n_outs] + rest[n_outs + n_copies :]
        copies = []
        for i, (x, y) in enumerate(zip(sources, targets)):
            copies += copy_parts(x, y, rest[-1].at[i])
        begin(copies)
        kernel(*ins[:first], *(rest[:-1] if copies else rest))
        finished(copies)

    given = [*inputs, *map(here, arrays), *map(there, away), *(there(a) for a, _ in fetch), *map(here, spill)]
    specs = [in_vmem] * (len(inputs) + len(arrays)) + [in_hbm] * (len(away) + len(fetch)) + [in_vmem] * len(spill)
    scratch = list(scratch) + [pltpu.SemaphoreType.DMA((n_copies, PARTS))] * bool(n_copies)
    return run(body, info, given, specs, outs, scratch, name, after, us=us)


class Pack:
    def __init__(self, *fields):
        self.lanes, self.width = {}, 0
        for name, width in fields:
            self.lanes[name] = slice(self.width, self.width + width)
            self.width += width

    def views(self, ref, *names):
        return [ref.at[:, self.lanes[n]] for n in names]


def kept_pack(width, states):
    return Pack(*((n, width) for n in ("slope", "gate", "gate_slope", "activated")), ("state", states))


def glu_pack(width, states):
    return Pack(("projected", 2 * width), ("mixed", width), ("dh", states), ("back", width))


def lift_pack(width, states):
    return Pack(("lifted", states), ("back_normed", width), ("back", width), ("normed", width))


def wide(mask, width):
    return jnp.concatenate([mask] * (width // LANES), axis=1)


def dot(a, b):
    return lax.dot_general(a, b, (((1,), (0,)), ((), ())), preferred_element_type=f32)


def dot_t(a, b):
    return lax.dot_general(a, b, (((1,), (1,)), ((), ())), preferred_element_type=f32)


def t_dot(a, b):
    return lax.dot_general(a, b, (((0,), (0,)), ((), ())), preferred_element_type=f32)


def cmul(ar, ai, br, bi):
    return ar * br - ai * bi, ar * bi + ai * br


def order(steps, reverse):
    return range(steps - 1, -1, -1) if reverse else range(steps)


def shuffle_matrix(span, back):
    chunk = span // CHUNKS
    place = lax.broadcasted_iota(jnp.int32, (span, span), 0)
    source = lax.broadcasted_iota(jnp.int32, (span, span), 1)
    if back:
        wanted = (place % chunk) * CHUNKS + place // chunk
    else:
        wanted = (place % CHUNKS) * chunk + place // CHUNKS
    return (source == wanted).astype(f32).astype(bf16)


class Where:
    def __init__(self, info_ref, seqs, span):
        self.seq = lax.axis_index("seq")
        self.seqs, self.span = seqs, span
        self.lengths = [info_ref[s] for s in range(seqs)]
        self.lefts = [length - self.seq * span for length in self.lengths]

    def steps_left(self):
        before = (self.span // CHUNKS) * lax.broadcasted_iota(jnp.int32, (CHUNKS, LANES), 0)
        return jnp.concatenate([left - before for left in self.lefts], axis=0)


def valid_rows(left, first, steps):
    return jnp.concatenate([(left > first + t).astype(f32) for t in range(steps)], axis=0)


def shuffle_rows(wide_ref, source_ref):
    steps, seqs, chunks, width = wide_ref.shape
    shuffle = shuffle_matrix(steps * chunks, False)
    for s in range(seqs):
        wide_ref[:, s] = dot(shuffle, source_ref[s]).reshape(steps, chunks, width)


def enter_kernel(info_ref, tokens_ref, sums_ref, here_ref, acc_ref, sems):
    seqs, span, width = tokens_ref.shape
    copies = [copy_parts(tokens_ref.at[s], here_ref.at[s], sems.at[s]) for s in range(seqs)]
    for parts in copies:
        begin(parts)
    where = Where(info_ref, seqs, span)
    step = lax.broadcasted_iota(jnp.int32, (span, 1), 0)
    total = jnp.zeros((1, width), f32)
    squares = jnp.zeros((1, width), f32)
    count = jnp.zeros((1, 1), f32)
    for s in range(seqs):
        valid = (step < where.lefts[s]).astype(f32)
        finished(copies[s])
        x = here_ref[s].astype(f32)
        masked = x * valid
        total += jnp.sum(masked, axis=0, keepdims=True)
        squares += jnp.sum(masked * x, axis=0, keepdims=True)
        count += jnp.sum(valid, axis=0, keepdims=True)
    tail = jnp.broadcast_to(count, (1, LANES))
    acc_ref[0:1, :] = jnp.concatenate([total, tail], axis=1)
    acc_ref[1:2, :] = jnp.concatenate([squares, tail], axis=1)
    for j in range(sums_ref.shape[0]):
        sums_ref[j] = acc_ref[...]


def enter(info, tokens, devices, fetch):
    seqs, _, width = tokens.shape
    outs = [moved((devices, 2, width + LANES), f32), near(tokens.shape, bf16)]
    scratch = [pltpu.VMEM((2, width + LANES), f32), pltpu.SemaphoreType.DMA((seqs, 1))]
    return call(enter_kernel, info, (), (), (tokens,), outs, scratch, "enter", fetch=fetch)


class Powers:
    @staticmethod
    def scratch(seqs, seq_devices, states, leaps):
        tables = [((1, 2 * states), f32), ((1, states), f32), ((2 * states // LANES, seqs * CHUNKS, LANES), f32)]
        if leaps:
            tables.append(((seq_devices * seqs, 2 * states), f32))
        return [pltpu.VMEM(*t) for t in tables]

    def __init__(self, k, back, where, decay_ref, phase_ref, lam_ref, scale_ref, table_ref, leap_ref=None):
        states = scale_ref.shape[1]
        groups, group = states // LANES, table_ref.shape[1]
        seqs, span, limit = where.seqs, where.span, where.span // CHUNKS
        rate = jnp.exp(decay_ref[k : k + 1, :])
        size, angle = jnp.exp(-rate), jnp.exp(phase_ref[k : k + 1, :])
        lam_ref[:, :states] = size * jnp.cos(angle)
        lam_ref[:, states:] = size * jnp.sin(angle) * (-1.0 if back else 1.0)
        scale_ref[...] = jnp.sqrt(1.0 - jnp.exp(-2.0 * rate))
        self.lam, self.scale, self.table, self.leaps = lam_ref, scale_ref, table_ref, leap_ref
        shift = 0 if not back else (-1 if k == 0 else 1)
        chunk_count = jnp.clip(where.steps_left() + shift, 0, limit)
        if leap_ref is not None:
            total = leap_ref.shape[0]
            line = lax.broadcasted_iota(jnp.int32, (total, LANES), 0)
            span_left = jnp.zeros((total, LANES), jnp.int32)
            for s, length in enumerate(where.lengths):
                span_left = jnp.where(line % seqs == s, length - span * (line // seqs), span_left)
            span_count = jnp.clip(span_left + shift, 0, span)
        for low in range(groups):
            real_lanes = slice(low * LANES, (low + 1) * LANES)
            imag_lanes = slice((groups + low) * LANES, (groups + low + 1) * LANES)
            br, bi = lam_ref[:, real_lanes], lam_ref[:, imag_lanes]
            cr = jnp.ones((group, LANES), f32)
            ci = jnp.zeros((group, LANES), f32)
            if leap_ref is not None:
                pr = jnp.ones((total, LANES), f32)
                pi = jnp.zeros((total, LANES), f32)
            for bit in range((limit if leap_ref is None else span).bit_length()):
                if (1 << bit) <= limit:
                    nr, ni = cmul(cr, ci, br, bi)
                    odd = (chunk_count & (1 << bit)) != 0
                    cr, ci = jnp.where(odd, nr, cr), jnp.where(odd, ni, ci)
                if leap_ref is not None:
                    nr, ni = cmul(pr, pi, br, bi)
                    odd = (span_count & (1 << bit)) != 0
                    pr, pi = jnp.where(odd, nr, pr), jnp.where(odd, ni, pi)
                br, bi = cmul(br, bi, br, bi)
            table_ref[low] = cr
            table_ref[groups + low] = ci
            if leap_ref is not None:
                leap_ref[:, real_lanes] = pr
                leap_ref[:, imag_lanes] = pi


def stretch_part(ends_ref, power_ref, reverse, seqs):
    groups = ends_ref.shape[0] // 2
    reals, imags = [], []
    for low in range(groups):
        real = jnp.zeros((seqs, LANES), f32)
        imag = jnp.zeros((seqs, LANES), f32)
        for c in order(CHUNKS, reverse):
            here = pl.ds(c, seqs, stride=CHUNKS)
            real, imag = cmul(power_ref[low, here, :], power_ref[groups + low, here, :], real, imag)
            real += ends_ref[low, here, :]
            imag += ends_ref[groups + low, here, :]
        reals.append(real)
        imags.append(imag)
    return jnp.concatenate(reals + imags, axis=1)


def chunk_starts(start_ref, place, parts_ref, leaps_ref, ends_ref, power_ref, reverse):
    devices, seqs, width = parts_ref.shape
    states = width // 2
    groups = states // LANES
    real = jnp.zeros((seqs, states), f32)
    imag = jnp.zeros((seqs, states), f32)
    for j in order(devices, reverse):
        ahead = (j > place) if reverse else (j < place)
        leap, part = leaps_ref[seqs * j : seqs * (j + 1), :], parts_ref[j]
        next_real, next_imag = cmul(leap[:, :states], leap[:, states:], real, imag)
        real = jnp.where(ahead, next_real + part[:, :states], real)
        imag = jnp.where(ahead, next_imag + part[:, states:], imag)
    for low in range(groups):
        hr = real[:, low * LANES : (low + 1) * LANES]
        hi = imag[:, low * LANES : (low + 1) * LANES]
        for c in order(CHUNKS, reverse):
            here = pl.ds(c, seqs, stride=CHUNKS)
            start_ref[low, here, :] = hr
            start_ref[groups + low, here, :] = hi
            hr, hi = cmul(power_ref[low, here, :], power_ref[groups + low, here, :], hr, hi)
            hr += ends_ref[low, here, :]
            hi += ends_ref[groups + low, here, :]


def scan_block(h_ref, drive, left, lam, shift, first, steps, reverse, out_ref=None):
    groups, group, _ = h_ref.shape
    groups = groups // 2
    masks = [left > first + t + shift for t in range(steps)]
    for low in range(groups):
        real_lanes = slice(low * LANES, (low + 1) * LANES)
        imag_lanes = slice((groups + low) * LANES, (groups + low + 1) * LANES)
        hr, hi = h_ref[low], h_ref[groups + low]
        lr, li = lam[:, real_lanes], lam[:, imag_lanes]
        for t in order(steps, reverse):
            ur, ui = drive(t, real_lanes, imag_lanes)
            nr, ni = cmul(lr, li, hr, hi)
            hr = jnp.where(masks[t], nr, hr) + ur
            hi = jnp.where(masks[t], ni, hi) + ui
            if out_ref is not None:
                out_ref[t * group : (t + 1) * group, real_lanes] = hr
                out_ref[t * group : (t + 1) * group, imag_lanes] = hi
        h_ref[low] = hr
        h_ref[groups + low] = hi


def input_drive(lifted, scale, left, first, steps):
    group = left.shape[0]
    masks = [left > first + t for t in range(steps)]

    def drive(t, real_lanes, imag_lanes):
        here = slice(t * group, (t + 1) * group)
        factor = jnp.where(masks[t], scale[:, real_lanes], 0.0)
        return factor * lifted[here, real_lanes], factor * lifted[here, imag_lanes]

    return drive


def blocks_of(rows, group, reverse):
    size = rows // BLOCKS
    for block in order(BLOCKS, reverse):
        yield block, block * (size // group), slice(block * size, (block + 1) * size)


def lift_kernel(k, seqs, info_ref, sums_ref, gain_ref, shift_ref, decay_ref, phase_ref, *refs):
    reverse = k == 1
    if k == 0:
        x_ref, weight_ref, normed_ref, lifted_ref, ends_ref, part_ref, stats_ref, rows_ref, wide_ref = refs[:9]
        refs = refs[9:]
    else:
        count_ref, x_ref, weight_ref, normed_ref, lifted_ref, ends_ref, part_ref, stats_ref = refs[:8]
        refs = refs[8:]
    rows, width = normed_ref.shape
    group = ends_ref.shape[1]
    size = rows // BLOCKS
    steps = size // group
    where = Where(info_ref, seqs, rows // seqs)
    powers = Powers(k, False, where, decay_ref, phase_ref, *refs)
    if k == 0:
        shuffle_rows(wide_ref, x_ref)
    sums = jnp.sum(sums_ref[...], axis=0)
    if k == 0:
        count = sums[0:1, width : width + 1]
    else:
        count = count_ref[2:3, 0:1]
    average = sums[0:1, :width] / count
    root = lax.rsqrt(sums[1:2, :width] / count - average * average + norm_eps)
    stats_ref[0:1, :] = average
    stats_ref[1:2, :] = root
    stats_ref[2:3, :] = jnp.broadcast_to(count, (1, width))
    gain, shift = gain_ref[k : k + 1, :], shift_ref[k : k + 1, :]
    lam, scale = powers.lam[...], powers.scale[...]
    left = where.steps_left()
    ends_ref[...] = jnp.zeros_like(ends_ref)
    for _, first, now in blocks_of(rows, group, reverse):
        if k == 0:
            x = wide_ref[first : first + steps].reshape(size, width)
            rows_ref[now, :] = x.astype(bf16)
        else:
            x = x_ref[now, :]
        normed = ((x - average) * root * gain + shift).astype(bf16)
        normed_ref[now, :] = normed
        lifted = dot(normed, weight_ref[...]).astype(bf16)
        lifted_ref[now, :] = lifted
        drive = input_drive(lifted.astype(f32), scale, left, first, steps)
        scan_block(ends_ref, drive, left, lam, 0, first, steps, reverse)
    part = stretch_part(ends_ref, powers.table, reverse, seqs)
    for j in range(part_ref.shape[0]):
        part_ref[j] = part


def lift(k, seqs, seq_devices, info, inputs, arrays, rows, fetch):
    gain, decay = inputs[1], inputs[3]
    width, states = gain.shape[1], decay.shape[1]
    outs = [
        near((rows, width), bf16),
        near((rows, 2 * states), bf16),
        near((2 * states // LANES, seqs * CHUNKS, LANES), f32),
        moved((seq_devices, seqs, 2 * states), f32),
        moved((8, width), f32),
    ]
    scratch = []
    if k == 0:
        outs.append(near((rows, width), bf16))
        scratch.append(pltpu.VMEM((rows // seqs // CHUNKS, seqs, CHUNKS, width), f32))
    scratch += Powers.scratch(seqs, seq_devices, states, False)
    return call(partial(lift_kernel, k, seqs), info, inputs, arrays, (), outs, scratch, "lift", fetch=fetch)


def mix_kernel(k, info_ref, parts_ref, skip_ref, bias_ref, decay_ref, phase_ref, *refs):
    reverse = k == 1
    (ends_ref, lifted_ref, normed_ref, x_ref, mix_ref, glu_ref) = refs[:6]
    tables, refs = refs[-4:], refs[6:-4]
    if reverse:
        state_ref, activated_ref, slope_ref, gate_ref, gate_slope_ref, masked_ref, h_ref, states_ref = refs
    else:
        next_ref, sums_ref, kept_out, h_ref, states_ref, acc_ref, kept_ref, sems = refs
        pack = kept_pack(x_ref.shape[1], lifted_ref.shape[1])
        state_ref, activated_ref, slope_ref, gate_ref, gate_slope_ref = pack.views(
            kept_ref, "state", "activated", "slope", "gate", "gate_slope"
        )
        copies = []
    seqs = parts_ref.shape[1]
    rows, width = x_ref.shape
    group = ends_ref.shape[1]
    steps = rows // BLOCKS // group
    where = Where(info_ref, seqs, rows // seqs)
    powers = Powers(k, False, where, decay_ref, phase_ref, *tables)
    chunk_starts(h_ref, where.seq, parts_ref, powers.leaps, ends_ref, powers.table, reverse)
    left = where.steps_left()
    skip, bias = skip_ref[k : k + 1, :], bias_ref[k : k + 1, :]
    lam, scale = powers.lam[...], powers.scale[...]
    total = jnp.zeros((1, width), f32)
    squares = jnp.zeros((1, width), f32)
    for block, first, now in blocks_of(rows, group, reverse):
        drive = input_drive(lifted_ref[now, :].astype(f32), scale, left, first, steps)
        scan_block(h_ref, drive, left, lam, 0, first, steps, reverse, states_ref)
        state = states_ref[...].astype(bf16)
        state_ref[now, :] = state
        mixed = dot(state, mix_ref[...]) + skip * normed_ref[now, :].astype(f32)
        base, cube = 0.7978845608028654, 0.044715
        square = mixed * mixed
        bend = jnp.tanh(mixed * (base + (base * cube) * square))
        half = 0.5 + 0.5 * bend
        activated = (mixed * half).astype(bf16)
        activated_ref[now, :] = activated
        slope_ref[now, :] = (
            half + mixed * (half - half * half) * (2.0 * base + (6.0 * base * cube) * square)
        ).astype(bf16)
        projected = dot(activated, glu_ref[...]) + bias
        gate = 0.5 + 0.5 * jnp.tanh(0.5 * projected[:, width:])
        gated = projected[:, :width] * gate
        gate_ref[now, :] = gate.astype(bf16)
        gate_slope_ref[now, :] = (gated - gated * gate).astype(bf16)
        after = x_ref[now, :].astype(f32) + gated
        masked = after * wide(valid_rows(left, first, steps), width)
        if reverse:
            masked_ref[now, :] = masked.astype(bf16)
        else:
            next_ref[now, :] = after
            total += jnp.sum(masked, axis=0, keepdims=True)
            squares += jnp.sum(masked * after, axis=0, keepdims=True)
            parts = copy_parts(kept_ref.at[now, :], kept_out.at[now, :], sems.at[block])
            begin(parts)
            copies += parts
    if not reverse:
        acc_ref[0:1, :] = total
        acc_ref[1:2, :] = squares
        for j in range(sums_ref.shape[0]):
            sums_ref[j] = acc_ref[...]
        finished(copies)


def mix(k, info, inputs, arrays, devices, fetch, spill=()):
    parts = inputs[0]
    ends, lifted, _, x = arrays[:4]
    rows, width = x.shape
    states = lifted.shape[1]
    seq_devices, seqs, _ = parts.shape
    scratch = [pltpu.VMEM(ends.shape, f32), pltpu.VMEM((rows // BLOCKS, states), f32)]
    if k == 1:
        outs = [near((rows, states), bf16)] + [near((rows, width), bf16)] * 5
    else:
        kept = (rows, kept_pack(width, states).width)
        outs = [near((rows, width), f32), moved((devices, 2, width), f32), (in_hbm, pltpu.HBM(kept, bf16))]
        scratch += [pltpu.VMEM((2, width), f32), pltpu.VMEM(kept, bf16), pltpu.SemaphoreType.DMA((BLOCKS, 1))]
    scratch += Powers.scratch(seqs, seq_devices, states // 2, True)
    return call(
        partial(mix_kernel, k), info, inputs, arrays, (), outs, scratch, "mix", fetch=fetch, spill=spill
    )


def glu_back_kernel(k, seqs, info_ref, decay_ref, phase_ref, *refs):
    reverse = k == 0
    if k == 0:
        sums_ref, stats_ref, gain_ref, shift_ref, lift_pack_ref, kept_ref, normed_in, glu_in, mix_in = refs[:9]
        tables, refs = refs[-3:], refs[9:-3]
    else:
        start_ref, normed_ref, slope_ref, gate_ref, gate_slope_ref, glu_ref, mix_ref = refs[:7]
        tables, refs = refs[-3:], refs[7:-3]
    out_ref, bias_grad_ref, skip_grad_ref, ends_ref, part_ref = refs[:5]
    refs = refs[5:]
    rows, width = out_ref.shape[0], skip_grad_ref.shape[1]
    states = 2 * decay_ref.shape[1]
    names = ("projected", "mixed", "dh", "back")
    projected_ref, mixed_ref, dh_ref, back_ref = glu_pack(width, states).views(out_ref, *names)
    if k == 0:
        total_ref, normed_ref, slopes_ref, glu_ref, mix_ref, sems, weight_sems = refs
        pack = kept_pack(width, states)
        back_normed_ref, start_ref, later_ref = lift_pack(width, states).views(
            lift_pack_ref, "back_normed", "back", "normed"
        )
        slope_ref, gate_ref, gate_slope_ref = pack.views(slopes_ref, "slope", "gate", "gate_slope")
    group = ends_ref.shape[1]
    size = rows // BLOCKS
    steps = size // group
    where = Where(info_ref, seqs, rows // seqs)
    if k == 1:
        (wide_ref,) = refs
        shuffle_rows(wide_ref, start_ref)
    else:
        copies = {}
        for block, _, now in blocks_of(rows, group, reverse):
            lanes = slice(0, 3 * width)
            copies[block] = copy_parts(kept_ref.at[now, lanes], slopes_ref.at[now, :], sems.at[0, block])
            copies[block] += copy_parts(normed_in.at[now, :], normed_ref.at[now, :], sems.at[1, block])
        weights = copy_parts(glu_in.at[k], glu_ref, weight_sems.at[0])
        weights += copy_parts(mix_in.at[k], mix_ref, weight_sems.at[1])
        for n, block in enumerate(order(BLOCKS, reverse)):
            begin(copies[block])
            if n == 0:
                begin(weights)
        sums = jnp.sum(sums_ref[...], axis=0)
        total_ref[...] = sums
        root, count = stats_ref[1:2, :], stats_ref[2:3, 0:1]
        gain, shift = gain_ref[1:2, :], shift_ref[1:2, :]
        by_normed = sums[0:1] / count
        fixed = (gain * sums[1:2] - shift * sums[0:1]) / count
    powers = Powers(k, True, where, decay_ref, phase_ref, *tables)
    left = where.steps_left()
    lam = powers.lam[...]
    ends_ref[...] = jnp.zeros_like(ends_ref)
    bias_grad = jnp.zeros((1, 2 * width), f32)
    skip_grad = jnp.zeros((1, width), f32)
    for block, first, now in blocks_of(rows, group, reverse):
        valid = wide(valid_rows(left, first, steps), width)
        if k == 1:
            back = wide_ref[first : first + steps].reshape(size, width) * valid
        else:
            finished(copies[block])
            back = start_ref[now, :].astype(f32) + root * (
                gain * back_normed_ref[now, :].astype(f32)
                - valid * (fixed + by_normed * later_ref[now, :].astype(f32))
            )
        back_ref[now, :] = back.astype(bf16)
        value_back = (back * gate_ref[now, :].astype(f32)).astype(bf16)
        gate_back = (back * gate_slope_ref[now, :].astype(f32)).astype(bf16)
        back_projected = jnp.concatenate([value_back, gate_back], axis=1)
        projected_ref[now, :] = back_projected
        bias_grad += jnp.sum(back_projected.astype(f32), axis=0, keepdims=True)
        if k == 0 and block == BLOCKS - 1:
            finished(weights)
        back_activated = dot_t(back_projected, glu_ref[...])
        back_mixed = (slope_ref[now, :].astype(f32) * back_activated).astype(bf16)
        mixed_ref[now, :] = back_mixed
        skip_grad += jnp.sum(back_mixed.astype(f32) * normed_ref[now, :].astype(f32), axis=0, keepdims=True)
        back_state = dot_t(back_mixed, mix_ref[...]).astype(bf16)
        dh_ref[now, :] = back_state
        wide_state = back_state.astype(f32)

        def drive(t, real_lanes, imag_lanes):
            at = slice(t * group, (t + 1) * group)
            return wide_state[at, real_lanes], wide_state[at, imag_lanes]

        shift = 1 if reverse else -1
        scan_block(ends_ref, drive, left, lam, shift, first, steps, reverse)
    bias_grad_ref[...] = bias_grad
    skip_grad_ref[...] = skip_grad
    part = stretch_part(ends_ref, powers.table, reverse, seqs)
    for j in range(part_ref.shape[0]):
        part_ref[j] = part


def glu_back(k, seqs, seq_devices, info, inputs, arrays, away, rows, width, after, fetch, spill=()):
    states = inputs[0].shape[1]
    outs = [
        near((rows, glu_pack(width, 2 * states).width), bf16),
        moved((1, 2 * width), f32),
        moved((1, width), f32),
        near((2 * states // LANES, seqs * CHUNKS, LANES), f32),
        moved((seq_devices, seqs, 2 * states), f32),
    ]
    if k == 1:
        scratch = [pltpu.VMEM((rows // seqs // CHUNKS, seqs, CHUNKS, width), f32)]
    else:
        outs += [moved((2, width), f32), near((rows, width), bf16)]
        scratch = [
            pltpu.VMEM((rows, 3 * width), bf16),
            pltpu.VMEM((width, 2 * width), bf16),
            pltpu.VMEM((2 * states, width), bf16),
            pltpu.SemaphoreType.DMA((2, BLOCKS, 1)),
            pltpu.SemaphoreType.DMA((2, 1)),
        ]
    scratch += Powers.scratch(seqs, seq_devices, states, False)
    return call(
        partial(glu_back_kernel, k, seqs), info, inputs, arrays, away, outs, scratch, "glu_back", after, fetch, spill
    )


def lift_back_kernel(
    k, info_ref, parts_ref, stats_ref, skip_ref, decay_ref, phase_ref, gain_ref, shift_ref, *refs
):
    reverse = last = k == 0
    if last:
        small_refs, refs = refs[:2], refs[2:]
    ends_ref, glu_pack_ref = refs[:2]
    states, width = 2 * decay_ref.shape[1], stats_ref.shape[1]
    mixed_ref, dh_ref, back_ref = glu_pack(width, states).views(glu_pack_ref, "mixed", "dh", "back")
    normed_ref, state_ref, weight_ref = refs[2:5]
    tables, refs = refs[-4:], refs[5:-4]
    if last:
        back_lifted_ref, sums_ref, ahead_ref = refs[:3]
        refs = refs[3:]
    else:
        out_ref, sums_ref, lam_grad_ref, scale_grad_ref = refs[:4]
        back_lifted_ref, back_normed_ref, kept_back_ref, kept_normed_ref = lift_pack(width, states).views(
            out_ref, "lifted", "back_normed", "back", "normed"
        )
        kept_back_ref[...] = back_ref[...]
        kept_normed_ref[...] = normed_ref[...]
        refs = refs[4:]
    h_ref, low_ref, acc_ref, lam_acc_ref, scale_acc_ref = refs
    rows, width = normed_ref.shape
    group = ends_ref.shape[1]
    seqs = parts_ref.shape[1]
    steps = rows // BLOCKS // group
    states = decay_ref.shape[1]
    where = Where(info_ref, seqs, rows // seqs)
    powers = Powers(k, True, where, decay_ref, phase_ref, *tables)
    chunk_starts(h_ref, where.seq, parts_ref, powers.leaps, ends_ref, powers.table, reverse)
    lam_acc_ref[...] = jnp.zeros_like(lam_acc_ref)
    scale_acc_ref[...] = jnp.zeros_like(scale_acc_ref)
    left = where.steps_left()
    lam, scale = powers.lam[...], powers.scale[...]
    root, gain, shift_row = stats_ref[1:2, :], gain_ref[k : k + 1, :], shift_ref[k : k + 1, :]
    skip = skip_ref[k : k + 1, :]
    gain_sum = jnp.zeros((1, width), f32)
    shift_sum = jnp.zeros((1, width), f32)
    shift = 1 if reverse else -1
    for _, first, now in blocks_of(rows, group, reverse):
        moving = [left > first + t + shift for t in range(steps)]
        valid = [left > first + t for t in range(steps)]
        dh = dh_ref[now, :].astype(f32)
        normed = normed_ref[now, :]
        lifted = dot(normed, weight_ref[...]).astype(bf16).astype(f32)
        state = state_ref[now, :].astype(f32)
        for low in range(0, states, LANES):
            real_lanes = slice(low, low + LANES)
            imag_lanes = slice(states + low, states + low + LANES)
            gr, gi = h_ref[low // LANES], h_ref[(states + low) // LANES]
            lr, li = lam[:, real_lanes], lam[:, imag_lanes]
            part = scale[:, real_lanes]
            sum_r, sum_i = lam_acc_ref[:, real_lanes], lam_acc_ref[:, imag_lanes]
            sum_s = scale_acc_ref[:, real_lanes]
            for t in order(steps, reverse):
                at = slice(t * group, (t + 1) * group)
                hr, hi = state[at, real_lanes], state[at, imag_lanes]
                ur, ui = lifted[at, real_lanes], lifted[at, imag_lanes]
                mr, mi = jnp.where(moving[t], gr, 0.0), jnp.where(moving[t], gi, 0.0)
                sum_r += mr * hr + mi * hi
                sum_i += mi * hr - mr * hi
                nr, ni = cmul(lr, li, gr, gi)
                gr = jnp.where(moving[t], nr, gr) + dh[at, real_lanes]
                gi = jnp.where(moving[t], ni, gi) + dh[at, imag_lanes]
                vr, vi = jnp.where(valid[t], gr, 0.0), jnp.where(valid[t], gi, 0.0)
                sum_s += vr * ur + vi * ui
                low_ref[at, real_lanes] = part * vr
                low_ref[at, imag_lanes] = part * vi
            h_ref[low // LANES] = gr
            h_ref[(states + low) // LANES] = gi
            lam_acc_ref[:, real_lanes] = sum_r
            lam_acc_ref[:, imag_lanes] = sum_i
            scale_acc_ref[:, real_lanes] = sum_s
        back_lifted = low_ref[...].astype(bf16)
        back_lifted_ref[now, :] = back_lifted
        back_normed = dot_t(back_lifted, weight_ref[...]) + skip * mixed_ref[now, :].astype(f32)
        gain_sum += jnp.sum(back_normed * normed.astype(f32), axis=0, keepdims=True)
        shift_sum += jnp.sum(back_normed, axis=0, keepdims=True)
        if last:
            ahead_ref[now, :] = (back_ref[now, :].astype(f32) + (root * gain) * back_normed).astype(bf16)
        else:
            back_normed_ref[now, :] = back_normed.astype(bf16)
    lam_grad = jnp.sum(lam_acc_ref[...], axis=0, keepdims=True)
    scale_grad = jnp.sum(scale_acc_ref[...], axis=0, keepdims=True)
    acc_ref[0:1, :] = (gain_sum - shift_row * shift_sum) / gain
    acc_ref[1:2, :] = shift_sum
    devices = sums_ref.shape[0]
    if last:
        skip_grad_ref, bias_grad_ref = small_refs
        acc_ref[2:3, :] = skip_grad_ref[...]
        acc_ref[3:4, :] = bias_grad_ref[:, :width]
        acc_ref[4:5, :] = bias_grad_ref[:, width:]
        acc_ref[5:6, :states] = lam_grad[:, :states]
        acc_ref[5:6, states : 2 * states] = lam_grad[:, states:]
        acc_ref[6:7, :states] = scale_grad
        acc_ref[6:7, states:] = jnp.zeros((1, width - states), f32)
        acc_ref[7:8, :] = jnp.zeros((1, width), f32)
    else:
        lam_grad_ref[...] = lam_grad
        scale_grad_ref[...] = scale_grad
    for j in range(devices):
        sums_ref[j] = acc_ref[...]


def lift_back(k, info, inputs, arrays, devices, after=(), fetch=()):
    parts, stats, decay = inputs[0], inputs[1], inputs[3]
    ends, packed = arrays[:2]
    rows, width, states = packed.shape[0], stats.shape[1], 2 * decay.shape[1]
    seq_devices, seqs, _ = parts.shape
    table = ends.shape
    acc = (8, width) if k == 0 else (2, width)
    if k == 0:
        outs = [near((rows, states), bf16), moved((devices,) + acc, f32), moved((rows, width), bf16)]
    else:
        outs = [near((rows, lift_pack(width, states).width), bf16), moved((devices, 2, width), f32)]
        outs += [moved((1, states), f32), moved((1, states // 2), f32)]
    scratch = [
        pltpu.VMEM(table, f32),
        pltpu.VMEM((rows // BLOCKS, states), f32),
        pltpu.VMEM(acc, f32),
        pltpu.VMEM((table[1], states), f32),
        pltpu.VMEM((table[1], states // 2), f32),
    ]
    scratch += Powers.scratch(seqs, seq_devices, states // 2, True)
    return call(partial(lift_back_kernel, k), info, inputs, arrays, (), outs, scratch, "lift_back", after, fetch)


def halves_kernel(parts, pairs, small, info_ref, *refs):
    keep_ref, send_ref = refs[-2:]
    width = keep_ref.shape[1]
    even = lax.axis_index("seq") % 2 == 0
    if small:
        small_refs, refs = refs[:4], refs[4:]
    products = [t_dot(*(refs[n][:, lanes] for n, lanes in pair)) for pair in pairs]
    first = 0
    for n, rows, (r, c), (q, d) in parts:
        a = products[n][r : r + rows, c : c + width].astype(bf16)
        b = products[n][q : q + rows, d : d + width].astype(bf16)
        keep_ref[first : first + rows, :] = jnp.where(even, a, b)
        send_ref[first : first + rows, :] = jnp.where(even, b, a)
        first += rows
    if small:
        skip_ref, bias_ref, lam_ref, scale_ref = small_refs
        extra = keep_ref.shape[0] - first
        low = jnp.concatenate([skip_ref[...], bias_ref[:, :width], bias_ref[:, width:]], axis=0)
        scale = jnp.concatenate([scale_ref[...], jnp.zeros((1, width - scale_ref.shape[1]), f32)], axis=1)
        high = jnp.concatenate([lam_ref[...], scale, jnp.zeros((1, width), f32)], axis=0)
        low, high = (jnp.concatenate([x, jnp.zeros((extra - 3, width), f32)], axis=0).astype(bf16) for x in (low, high))
        keep_ref[first:, :] = jnp.where(even, low, high)
        send_ref[first:, :] = jnp.where(even, high, low)


def halves(info, parts, pairs, small, arrays, width, name, after=()):
    rows = sum(p[1] for p in parts)
    if small:
        rows += EXTRA * (lax.axis_size("seq") // 2)
    outs = [moved((rows, width), bf16)] * 2
    return call(partial(halves_kernel, parts, pairs, bool(small)), info, small, arrays, (), outs, [], name, after)


def place_of(axis):
    return lax.axis_index("batch") if axis == "batch" else lax.axis_index("seq") // 2


def total_of(refs, rows):
    total = refs[0][rows, :].astype(f32)
    for ref in refs[1:]:
        total += ref[rows, :].astype(f32)
    return total


def split_kernel(chips, sets, xor, info_ref, *refs):
    n_in = 2 * len(sets)
    outs = refs[n_in:]
    place = place_of("seq")
    for m in range(chips):
        chip = place ^ m if xor else m
        low = 0
        for n, parts in enumerate(sets):
            first = 0
            for rows in parts:
                share = rows // chips
                start = first + chip * share
                if xor:
                    start = pl.multiple_of(start, 16)
                total = total_of(refs[2 * n : 2 * n + 2], pl.ds(start, share))
                if xor:
                    outs[m][low : low + share, :] = total.astype(outs[m].dtype)
                else:
                    base = m * (outs[0].shape[0] // chips) + low
                    outs[0][base : base + share, :] = total.astype(outs[0].dtype)
                first, low = first + rows, low + share


def split(info, sets, arrays, xor, after=()):
    chips = lax.axis_size("seq") // 2
    width = arrays[0].shape[1]
    rows = sum(map(sum, sets))
    outs = [moved((rows, width), bf16)]
    if xor:
        outs = [moved((rows // chips, width), f32)] + [moved((rows // chips, width), bf16)] * (chips - 1)
    return call(partial(split_kernel, chips, sets, xor), info, arrays, (), (), outs, [], "split", after, us=0.8)


def cut_kernel(extra, info_ref, *refs):
    low_ref, refs = refs[-1], refs[:-1]
    batches, share, width = low_ref.shape
    arrays, outs = refs[:-batches], refs[-batches:]
    place = place_of("batch")
    rows = batches * share
    low_ref[...] = total_of(arrays, slice(0, rows)).reshape(batches, share, width)
    under = total_of(arrays, slice(rows, rows + extra)) if extra else None
    for m in range(batches):
        outs[m][:share, :] = low_ref[place ^ m].astype(outs[m].dtype)
        if extra:
            outs[m][share:, :] = under.astype(outs[m].dtype)


def cut(info, arrays, extra, after=()):
    batches = lax.axis_size("batch")
    rows, width = arrays[0].shape
    share = (rows - extra) // batches
    outs = [moved((share + extra, width), f32)] + [moved((share + extra, width), bf16)] * (batches - 1)
    scratch = [pltpu.VMEM((batches, share, width), f32)]
    return call(partial(cut_kernel, extra), info, arrays, (), (), outs, scratch, "cut", after, us=1.2)


def sum_kernel(info_ref, *refs):
    total = refs[0][...].astype(f32)
    for ref in refs[1:-1]:
        total += ref[...].astype(f32)
    refs[-1][...] = total.astype(bf16)


def sum_of(info, arrays, after=()):
    return call(sum_kernel, info, arrays, (), (), [moved(arrays[0].shape, bf16)], [], "total", after, us=0.6)


def join_kernel(info_ref, *refs):
    pieces, out_ref, low_ref = refs[:-2], refs[-2], refs[-1]
    batches, share, width = low_ref.shape
    place = place_of("batch")
    for m, ref in enumerate(pieces):
        low_ref[place ^ m] = ref[:share, :].astype(f32)
    rows = batches * share
    out_ref[:rows, :] = low_ref[...].reshape(rows, width).astype(bf16)
    if out_ref.shape[0] > rows:
        out_ref[rows:, :] = pieces[0][share:, :]


def join(info, arrays, extra, after=()):
    batches = len(arrays)
    rows, width = arrays[0].shape
    share = rows - extra
    outs = [moved((batches * share + extra, width), bf16)]
    scratch = [pltpu.VMEM((batches, share, width), f32)]
    return call(join_kernel, info, arrays, (), (), outs, scratch, "join", after, us=0.6)


def trade(x, axis, mask):
    size = lax.axis_size(axis)
    return lax.ppermute(x, axis, [(i, i ^ mask) for i in range(size)])


def sent(arrays, axis, masks):
    return [arrays[0]] + [trade(x, axis, m) for x, m in zip(arrays[1:], masks)]


def to_others(x, axis, masks):
    return [x] + [trade(x, axis, m) for m in masks]


def gate_kernel(*refs):
    pass


def gate(info, arrays, after):
    outs = [(in_hbm, pltpu.HBM(x.shape, x.dtype)) for x in arrays]
    aliases = {1 + i: i for i in range(len(arrays))}
    return run(gate_kernel, info, list(map(there, arrays)), [in_hbm] * len(arrays), outs, [], "gate", after, aliases, 0.5)


def small_grads(sums, norm1, low, high, decay_log, phase_log, refs):
    gain_ref, shift_ref, decay_grad_ref, phase_grad_ref, skip_grad_ref, bias_grad_ref = refs
    blocks, states = decay_log.shape
    width = sums.shape[1]
    rows = (
        [sums[n : n + 1] for n in range(2, 7)],
        [low[0:1], low[1:2], low[2:3], high[0:1], high[1:2]],
    )
    norms = ([sums[0:1], sums[1:2]], [norm1[0:1], norm1[1:2]])
    for k in range(blocks):
        gain_ref[k : k + 1, :], shift_ref[k : k + 1, :] = norms[k]
        skip, bias_low, bias_high, lam, scale = rows[k]
        skip_grad_ref[k : k + 1, :] = skip
        bias_grad_ref[k : k + 1, :width] = bias_low
        bias_grad_ref[k : k + 1, width:] = bias_high
        rate, angle = jnp.exp(decay_log[k : k + 1]), jnp.exp(phase_log[k : k + 1])
        size, fade = jnp.exp(-rate), jnp.exp(-2.0 * rate)
        lam_real, lam_imag = size * jnp.cos(angle), size * jnp.sin(angle)
        real, imag = lam[:, :states], lam[:, states : 2 * states]
        by_rate = scale[:, :states] * fade * lax.rsqrt(1.0 - fade) - (real * lam_real + imag * lam_imag)
        decay_grad_ref[k : k + 1, :] = rate * by_rate
        phase_grad_ref[k : k + 1, :] = angle * (imag * lam_real - real * lam_imag)


def results_kernel(chips, info_ref, sums_ref, norm1_ref, decay_ref, phase_ref, *refs):
    pieces, refs = refs[: 4 * chips], refs[4 * chips :]
    glu_ref, mix_ref, lift_ref, *small_refs = refs[:9]
    low_ref, under_ref, wide_ref, in_sems, sems = refs[9:]
    place = place_of("seq")
    core = lax.axis_index("seq") % 2
    _, rows, width = wide_ref.shape
    half, quarter = rows // 2, rows // 4
    arriving = []
    for n, piece in enumerate(pieces):
        parts = [pltpu.make_async_copy(piece.at[pl.ds(0, rows), :], low_ref.at[n], in_sems.at[n, 0])]
        if n >= 2 * chips:
            under = piece.at[pl.ds(rows, EXTRA), :]
            parts.append(pltpu.make_async_copy(under, under_ref.at[n - 2 * chips], in_sems.at[n, 1]))
        begin(parts)
        arriving.append(parts)
    copies = []
    extras = [jnp.zeros((EXTRA, width), f32)] * 2
    for n in range(4 * chips):
        finished(arriving[n])
        k, n_in = divmod(n, 2 * chips)
        chip, side = place ^ (n_in % chips), core if n_in < chips else 1 - core
        if k == 1:
            extra = under_ref[n_in].astype(f32)
            extras[n_in // chips] = jnp.where(chip == 0, extra, extras[n_in // chips])
        column = pl.multiple_of(side * width, width)
        row = pl.multiple_of(chip * half, 8)
        low = pl.multiple_of(side * (quarter * chips) + chip * quarter, 8)
        wide_ref[n] = low_ref[n].astype(f32)
        for i, (first, size, target) in enumerate(
            (
                (0, half, glu_ref.at[k, pl.ds(row, half), pl.ds(column, width)]),
                (half, quarter, mix_ref.at[k, pl.ds(low, quarter), :]),
                (half + quarter, quarter, lift_ref.at[k, pl.ds(low, quarter), :]),
            )
        ):
            copies.append(pltpu.make_async_copy(wide_ref.at[n, pl.ds(first, size), :], target, sems.at[n, i]))
            copies[-1].start()
    even = core == 0
    small_grads(
        jnp.sum(sums_ref[...], axis=0),
        norm1_ref[...],
        jnp.where(even, extras[0], extras[1]),
        jnp.where(even, extras[1], extras[0]),
        decay_ref[...],
        phase_ref[...],
        small_refs,
    )
    finished(copies)


def results(info, sums, norm1, decay_log, phase_log, pieces, after=()):
    rows, width = pieces[0].shape
    count = len(pieces)
    anywhere = pl.BlockSpec(memory_space=pl.ANY)
    shapes = [(2, width, 2 * width), (2, width, width), (2, width, width)]
    outs = [(anywhere, jax.ShapeDtypeStruct(shape, f32)) for shape in shapes]
    blocks, states = decay_log.shape
    outs += [moved((blocks, n), f32) for n in (width, width, states, states, width, 2 * width)]
    scratch = [
        pltpu.VMEM((count, rows, width), bf16),
        pltpu.VMEM((count // 2, EXTRA, width), bf16),
        pltpu.VMEM((count, rows, width), f32),
        pltpu.SemaphoreType.DMA((count, 2)),
        pltpu.SemaphoreType.DMA((count, 3)),
    ]
    inputs = (sums, norm1, decay_log, phase_log)
    kernel = partial(results_kernel, count // 4)
    return call(kernel, info, inputs, (), pieces, outs, scratch, "results", after, us=7.0)


def leave_kernel(seqs, info_ref, rows_ref, out_ref, wide_ref):
    _, span, width = out_ref.shape
    wide_ref[...] = rows_ref[...].astype(f32).reshape(wide_ref.shape)
    shuffle = shuffle_matrix(span, True)
    for s in range(seqs):
        out_ref[s] = dot(shuffle, wide_ref[:, s].reshape(span, width).astype(bf16)).astype(bf16)


def leave(info, rows, seqs, after=()):
    span, width = rows.shape[0] // seqs, rows.shape[1]
    scratch = [pltpu.VMEM((span // CHUNKS, seqs, CHUNKS, width), f32)]
    outs = [moved((seqs, span, width), bf16)]
    return call(partial(leave_kernel, seqs), info, (rows,), (), (), outs, scratch, "leave", after)


def input_grad_kernel(
    info_ref, sums_ref, tokens_ref, ahead_ref, stats_ref, gain_ref, grad_ref, wide_ref
):
    seqs, span, width = tokens_ref.shape
    where = Where(info_ref, seqs, span)
    wide_ref[...] = ahead_ref[...].astype(f32).reshape(wide_ref.shape)
    shuffle = shuffle_matrix(span, True)
    average, root = stats_ref[0:1, :], stats_ref[1:2, :]
    factor = root * gain_ref[0:1, :] / stats_ref[2:3, 0:1]
    sums = jnp.sum(sums_ref[...], axis=0)
    by_gain = factor * sums[0:1] * root
    fixed = factor * sums[1:2] - by_gain * average
    step = lax.broadcasted_iota(jnp.int32, (span, 1), 0)
    for s in range(seqs):
        valid = (step < where.lefts[s]).astype(f32)
        ahead = dot(shuffle, wide_ref[:, s].reshape(span, width).astype(bf16))
        grad_ref[s] = (ahead - valid * (fixed + by_gain * tokens_ref[s].astype(f32))).astype(bf16)


def input_grads(info, sums, tokens, ahead, stats, gain, after=()):
    seqs, span, width = tokens.shape
    outs = [moved(tokens.shape, bf16)]
    scratch = [pltpu.VMEM((span // CHUNKS, seqs, CHUNKS, width), f32)]
    return call(
        input_grad_kernel, info, (sums, tokens, ahead, stats, gain), (), (), outs, scratch, "input_grad", after, us=2.0
    )


def to_all(x, axes):
    return lax.all_to_all(x, axes, split_axis=0, concat_axis=0, tiled=True)


def local(
    tokens,
    lengths,
    cotangent,
    norm_gain,
    norm_shift,
    lift_weight,
    decay_log,
    phase_log,
    skip_gain,
    mix_weight,
    glu_weight,
    glu_bias,
):
    both = ("seq", "batch")
    seq_devices, batches = lax.axis_size("seq"), lax.axis_size("batch")
    devices, chips = seq_devices * batches, seq_devices // 2
    seqs, span, width = tokens.shape
    rows = seqs * span
    info = lengths
    turns = (decay_log, phase_log)
    norms_in = (norm_gain, norm_shift)
    states = decay_log.shape[1]
    half = width // 2

    sums, tokens_here, lift_w = enter(info, tokens, devices, [(lift_weight, 0)])
    sums = to_all(sums, both)
    normed, lifted, ends, part, stats0, x, mix_w, glu_w = lift(
        0, seqs, seq_devices, info, (sums, *norms_in, *turns), (tokens_here, lift_w), rows,
        [(mix_weight, 0), (glu_weight, 0)],
    )
    x1, sums, kept, lift_w, normed0 = mix(
        0, info, (to_all(part, "seq"), skip_gain, glu_bias, *turns), (ends, lifted, normed, x, mix_w, glu_w),
        devices, [(lift_weight, 1)], (normed,),
    )
    sums = to_all(sums, both)

    normed1, lifted1, ends, part, stats1, mix_w, glu_w = lift(
        1, seqs, seq_devices, info, (sums, *norms_in, *turns, stats0), (x1, lift_w), rows,
        [(mix_weight, 1), (glu_weight, 1)],
    )
    state1, activated1, slope1, gate1, gate_slope1, masked, cot = mix(
        1, info, (to_all(part, "seq"), skip_gain, glu_bias, *turns), (ends, lifted1, normed1, x1, mix_w, glu_w),
        devices, [(cotangent, None)],
    )

    glu_packed, bias_grad1, skip_grad1, ends, part, lift_w, masked = glu_back(
        1, seqs, seq_devices, info, turns, (cot, normed1, slope1, gate1, gate_slope1, glu_w, mix_w), (), rows, width,
        (), [(lift_weight, 1)], [masked],
    )
    lift_packed, sums, lam_grad1, scale_grad1 = lift_back(
        1, info, (to_all(part, "seq"), stats1, skip_gain, *turns, *norms_in),
        (ends, glu_packed, normed1, state1, lift_w), devices,
    )
    glu_part, mix_part, lift_part = (0, width, (0, 0), (0, width)), (1, half, (0, 0), (half, 0)), (2, half, (0, 0), (half, 0))
    glu_lanes, lift_lanes = glu_pack(width, 2 * states).lanes, lift_pack(width, 2 * states).lanes
    kept_lanes, every = kept_pack(width, 2 * states).lanes, slice(None)
    out = halves(
        info,
        (glu_part, mix_part, lift_part),
        (
            ((0, every), (1, glu_lanes["projected"])),
            ((2, every), (1, glu_lanes["mixed"])),
            ((3, every), (4, lift_lanes["lifted"])),
        ),
        (skip_grad1, bias_grad1, lam_grad1, scale_grad1),
        (activated1, glu_packed, state1, normed1, lift_packed),
        width,
        "halves1",
    )
    keep1, send = out
    got1 = trade(send, "seq", 1)
    (produced,) = out = leave(info, masked, seqs, (out.tick,))
    shares = (width, half, half)
    z, xy = range(1, batches), range(2, seq_devices, 2)
    extra = EXTRA * chips
    out = split(info, ((*shares, extra),), [keep1, got1], True, (out.tick,))
    (sums,) = gate(info, [sums], (out.tick,))
    pieces1 = sent(out, "seq", xy)
    sums = to_all(sums, both)

    state_lanes = (slice(None), kept_lanes["state"])
    pieces1 = there1 = gate(info, pieces1, ())
    out = glu_back(
        0, seqs, seq_devices, info, (*turns, sums, stats1, *norms_in), (lift_packed,),
        (kept, normed0, glu_weight, mix_weight), rows, width, (there1.tick,),
        [(kept, state_lanes), (lift_weight, 0)],
    )
    glu_packed, bias_grad0, skip_grad0, ends, part, norm_sums1, normed, state, lift_w = out
    small = (skip_grad0, bias_grad0)
    activated_lanes = (slice(None), kept_lanes["activated"])
    back_lifted0, sums, ahead, activated = out = lift_back(
        0, info, (to_all(part, "seq"), stats0, skip_gain, *turns, *norms_in, *small),
        (ends, glu_packed, normed, state, lift_w), devices, (), [(kept, activated_lanes)],
    )

    keep0, send = out = halves(
        info,
        (glu_part, mix_part, lift_part),
        (
            ((0, every), (1, glu_lanes["projected"])),
            ((2, every), (1, glu_lanes["mixed"])),
            ((3, every), (4, every)),
        ),
        (),
        (activated, glu_packed, state, normed, back_lifted0),
        width,
        "halves0",
    )
    got0 = trade(send, "seq", 1)
    (sums,) = gate(info, [sums], (out.tick,))
    sums = to_all(sums, both)
    out1 = cut(info, pieces1, EXTRA, (out.tick,))
    out0 = split(info, (shares,), [keep0, got0], True, (out1.tick,))
    out0 = cut(info, sent(out0, "seq", xy), 0, (out0.tick,))
    sum1 = sum_of(info, sent(out1, "batch", z), (out0.tick,))
    sum0 = sum_of(info, sent(out0, "batch", z), (sum1.tick,))
    (own1,) = out = join(info, to_others(sum1[0], "batch", z), EXTRA, (sum0.tick,))
    (own0,) = out = join(info, to_others(sum0[0], "batch", z), 0, (out.tick,))
    total = to_others(own0, "seq", xy) + to_others(own1, "seq", xy)
    (input_grad,) = out = input_grads(info, sums, tokens, ahead, stats0, norm_gain, (out.tick,))
    total = gate(info, total, (out.tick,))
    other = [trade(x, "seq", 1) for x in total]
    total = total[:chips] + other[:chips] + total[chips:] + other[chips:]
    grad_glu, grad_mix, grad_lift, grad_gain, grad_shift, grad_decay, grad_phase, grad_skip, grad_bias = results(
        info, sums, norm_sums1, *turns, total
    )
    return (
        produced,
        input_grad,
        grad_gain,
        grad_shift,
        grad_lift,
        grad_decay,
        grad_phase,
        grad_skip,
        grad_mix,
        grad_glu,
        grad_bias,
    )


def solution(mesh):
    split = P("batch", "seq", None)
    placed = (split, P("batch"), split) + (P(),) * 9
    return jax.shard_map(
        local,
        mesh=mesh,
        in_specs=placed,
        out_specs=(split, split) + (P(),) * 9,
        check_vma=False,
    )
```

time: 243 us -> 210 us (0.86)
  local copies, waits for them, and re-layouts: 23.7 us -> 8.34 us
  waiting for transfers between devices: 54.2 us -> 39.8 us
  between operations: 14.5 us -> 1.38 us
  blocking collectives: 49.9 us -> 55.9 us
  starting transfers between devices: 36.6 us -> 41.7 us
    unnamed x94 -> x66, local copies, waits for them, and re-layouts: 22.4 us -> 8.34 us
    ppermute x22 -> x34, waiting for transfers between devices: 51.1 us -> 39.8 us  [trade(): return lax.ppermute(x, axis, [(i, i ^ mask) for i in range(size)])]
    ppermute x22 -> x34, starting transfers between devices: 25.5 us -> 36.4 us  [trade(): return lax.ppermute(x, axis, [(i, i ^ mask) for i in range(size)])]
    all_to_all x6, blocking collectives: 49.9 us -> 55.9 us  [to_all(): return lax.all_to_all(x, axes, split_axis=0, concat_axis=0, tiled=True)]
    all_to_all x2, starting transfers between devices: 11 us -> 5.22 us  [to_all(): return lax.all_to_all(x, axes, split_axis=0, concat_axis=0, tiled=True)]
    all_to_all x2, waiting for transfers between devices: 3.1 us -> 0.01 us  [to_all(): return lax.all_to_all(x, axes, split_axis=0, concat_axis=0, tiled=True)]
    pallas_call x25 -> x26, Pallas kernels: 61.4 us -> 62.5 us  [run(): pl.pallas_call(ticking, in_specs=[in_smem] + specs + [in_hbm] * len(after...]
  transfers between devices with their start and end apart: 26 -> 36, of which waited for: 15 -> 17; matrix products, arithmetic and copies ran while one was open for 1% -> 0% of each run, Pallas kernels for 13% -> 5%
where the time goes in v2:
time: 210 us
  Pallas kernels  62.5 us (30%)
  blocking collectives  55.9 us (27%)
  starting transfers between devices  41.7 us (20%)
  waiting for transfers between devices  39.8 us (19%)
  local copies, waits for them, and re-layouts  8.34 us (4%)
    pallas_call x26, Pallas kernels, run(): pl.pallas_call(ticking, in_specs=[in_smem] + specs + [in_hbm] * len(after...  62.5 us
    all_to_all x6, blocking collectives, to_all(): return lax.all_to_all(x, axes, split_axis=0, concat_axis=0, tiled=True)  55.9 us
    ppermute x34, waiting for transfers between devices, trade(): return lax.ppermute(x, axis, [(i, i ^ mask) for i in range(size)])  39.8 us
    ppermute x34, starting transfers between devices, trade(): return lax.ppermute(x, axis, [(i, i ^ mask) for i in range(size)])  36.4 us
    unnamed x66, local copies, waits for them, and re-layouts  8.34 us
    all_to_all x2, starting transfers between devices, to_all(): return lax.all_to_all(x, axes, split_axis=0, concat_axis=0, tiled=True)  5.22 us
  transfers between devices with their start and end apart: 36, of which 17 were waited for; matrix products, arithmetic and copies ran while one was open for 0% of the time, Pallas kernels for 5%

profile of v2, /device:TPU:0, one launch (start us, length us, event | category | flops | bytes accessed | tf_op | source)
XLA Modules:
  0.0 209.6 jit_solution(14058750666523198956)
XLA Ops:
  3.6 16.0 %all_to_all.40.refs_1_ = f32[32,2,640]{2,1,0:T(2,128)S(1)} all-to-all(f32[32,2,640]{2,1,0:T(2,128)S(1)} %get-tuple-element.127), channel_id=1, replica_groups=mesh['seq'=8,'batch'=4] {'seq','batch'}, dimensions={0} | all-to-all | bytes 327680 | tf_op jit(solution)/shard_map/all_to_all | solution.py:1049
  22.0 7.4 %all_to_all.41.refs_1_ = f32[8,4,512]{2,1,0:T(4,128)S(1)} all-to-all(f32[8,4,512]{2,1,0:T(4,128)S(1)} %get-tuple-element.130), channel_id=1, replica_groups=mesh['seq'=8,'batch'=4] {'seq'}, dimensions={0} | all-to-all | bytes 131072 | tf_op jit(solution)/shard_map/all_to_all | solution.py:1049
  29.4 6.2 %mix.2 = (f32[1024,512]{1,0:T(8,128)S(1)}, f32[32,2,512]{2,1,0:T(2,128)S(1)}, bf16[1024,2560]{1,0:T(8,128)(2,1)}, bf16[512,512]{1,0:T(8,128)(2,1)S(1)}, bf16[1024,512]{1,0:T(8,128)(2,1)}, /*index=5*/f32[8,128]{1,0:T(8,128)}) custom-call(s32[4]{0:T(128)S(1)} %copy-done.13, f32[8,4,512]{2,1,0:T(4,128)S(1)} %all_to_all.41.refs_1_, f32[2,512]{1,0:T(2,128)S(1)} %copy-done.14, ...), custom_call_target="tpu_custom_call" | custom-call | tf_op jit(solution)/shard_map/mix/pallas_call | solution.py:64
  35.6 10.1 %all_to_all.42.refs_1_ = f32[32,2,512]{2,1,0:T(2,128)S(1)} all-to-all(f32[32,2,512]{2,1,0:T(2,128)S(1)} %get-tuple-element.137), channel_id=1, replica_groups=mesh['seq'=8,'batch'=4] {'seq','batch'}, dimensions={0} | all-to-all | bytes 262144 | tf_op jit(solution)/shard_map/all_to_all | solution.py:1049
  47.6 7.4 %all_to_all.43.refs_1_ = f32[8,4,512]{2,1,0:T(4,128)S(1)} all-to-all(f32[8,4,512]{2,1,0:T(4,128)S(1)} %get-tuple-element.141), channel_id=1, replica_groups=mesh['seq'=8,'batch'=4] {'seq'}, dimensions={0} | all-to-all | bytes 131072 | tf_op jit(solution)/shard_map/all_to_all | solution.py:1049
  55.0 5.1 %mix.3 = (bf16[1024,512]{1,0:T(8,128)(2,1)S(1)}, bf16[1024,512]{1,0:T(8,128)(2,1)S(1)}, bf16[1024,512]{1,0:T(8,128)(2,1)S(1)}, bf16[1024,512]{1,0:T(8,128)(2,1)S...) custom-call(s32[4]{0:T(128)S(1)} %copy-done.13, ...), custom_call_target="tpu_custom_call" | custom-call | tf_op jit(solution)/shard_map/mix/pallas_call | solution.py:64
  60.1 4.5 %glu_back.2 = (bf16[1024,2560]{1,0:T(8,128)(2,1)S(1)}, f32[1,1024]{1,0:T(1,128)S(1)}, f32[1,512]{1,0:T(1,128)S(1)}, f32[4,32,128]{2,1,0:T(8,128)S(1)}, f32[8,4,5...) custom-call(s32[4]{0:T(128)S(1)} %copy-done.13, ...), custom_call_target="tpu_custom_call" | custom-call | tf_op jit(solution)/shard_map/glu_back/pallas_call | solution.py:64
  64.7 7.4 %all_to_all.44.refs_1_ = f32[8,4,512]{2,1,0:T(4,128)S(1)} all-to-all(f32[8,4,512]{2,1,0:T(4,128)S(1)} %get-tuple-element.155), channel_id=1, replica_groups=mesh['seq'=8,'batch'=4] {'seq'}, dimensions={0} | all-to-all | bytes 131072 | tf_op jit(solution)/shard_map/all_to_all | solution.py:1049
  72.1 3.1 %lift_back.2 = (bf16[1024,2048]{1,0:T(8,128)(2,1)S(1)}, f32[32,2,512]{2,1,0:T(2,128)S(1)}, f32[1,512]{1,0:T(1,128)S(1)}, f32[1,256]{1,0:T(1,128)S(1)}, f32[8,128]{1,0:T(8,128)}) custom-call(s32[4]{0:T(128)S(1)} %copy-done.13, f32[8,4,512]{2,1,0:T(4,128)S(1)} %all_to_all.44.refs_1_, f32[8,512]{1,0:T(8,128)S(1)} %get-tuple-element.156.refs_2_.refs_4_, ...), custom_call_target="tpu_custom_call" | custom-call | tf_op jit(solution)/shard_map/lift_back/pallas_call | solution.py:64
  75.2 2.9 %halves1.1 = (bf16[1088,512]{1,0:T(8,128)(2,1)S(1)}, bf16[1088,512]{1,0:T(8,128)(2,1)S(1)}, f32[8,128]{1,0:T(8,128)}) custom-call(s32[4]{0:T(128)S(1)} %copy-done.13, f32[1,512]{1,0:T(1,128)S(1)} %get-tuple-element.153.refs_1_, f32[1,1024]{1,0:T(1,128)S(1)} %get-tuple-element.154.refs_2_, f32[1,512]{1,0:T(1,128)S(1)} %get-tuple-element.161.refs_3_, ...), custom_call_target="tpu_custom_call" | custom-call | tf_op jit(solution)/shard_map/halves1/pallas_call | solution.py:64
  89.3 2.8 %collective-permute-done.1.refs_2_ = bf16[272,512]{1,0:T(8,128)(2,1)S(1)} collective-permute-done((bf16[272,512]{1,0:T(8,128)(2,1)S(1)}, bf16[272,512]{1,0:T(8,128)(2,1)S(1)}, u32[]{:S(2)}, u32[]{:S(2)}) %collective-permute-start.1) | collective-permute-done | bytes 278560 | tf_op jit(solution)/shard_map/ppermute | solution.py:889
  92.1 6.8 %collective-permute-done.2.refs_3_ = bf16[272,512]{1,0:T(8,128)(2,1)S(1)} collective-permute-done((bf16[272,512]{1,0:T(8,128)(2,1)S(1)}, bf16[272,512]{1,0:T(8,128)(2,1)S(1)}, u32[]{:S(2)}, u32[]{:S(2)}) %collective-permute-start.2) | collective-permute-done | bytes 278560 | tf_op jit(solution)/shard_map/ppermute | solution.py:889
  102.4 7.4 %glu_back.3 = (bf16[1024,2560]{1,0:T(8,128)(2,1)S(1)}, f32[1,1024]{1,0:T(1,128)S(1)}, f32[1,512]{1,0:T(1,128)S(1)}, f32[4,32,128]{2,1,0:T(8,128)S(1)}, f32[8,4,5...) custom-call(s32[4]{0:T(128)S(1)} %copy-done.13, ...), custom_call_target="tpu_custom_call" | custom-call | tf_op jit(solution)/shard_map/glu_back/pallas_call | solution.py:64
  109.9 7.6 %all_to_all.45.refs_1_ = f32[8,4,512]{2,1,0:T(4,128)S(1)} all-to-all(f32[8,4,512]{2,1,0:T(4,128)S(1)} %get-tuple-element.180), channel_id=1, replica_groups=mesh['seq'=8,'batch'=4] {'seq'}, dimensions={0} | all-to-all | bytes 131072 | tf_op jit(solution)/shard_map/all_to_all | solution.py:1049
  117.4 4.4 %lift_back.3 = (bf16[1024,512]{1,0:T(8,128)(2,1)S(1)}, f32[32,8,512]{2,1,0:T(8,128)S(1)}, bf16[1024,512]{1,0:T(8,128)(2,1)S(1)}, bf16[1024,512]{1,0:T(8,128)(2,1)S(1)}, f32[8,128]{1,0:T(8,128)}) custom-call(s32[4]{0:T(128)S(1)} %copy-done.13, f32[8,4,512]{2,1,0:T(4,128)S(1)} %all_to_all.45.refs_1_, f32[8,512]{1,0:T(8,128)S(1)} %get-tuple-element.138.refs_6_.refs_2_.refs_4_, ...), custom_call_target="tpu_custom_call" | custom-call | tf_op jit(solution)/shard_map/lift_back/pallas_call | solution.py:64
  122.7 3.9 %halves0.1 = (bf16[1024,512]{1,0:T(8,128)(2,1)S(1)}, bf16[1024,512]{1,0:T(8,128)(2,1)}, f32[8,128]{1,0:T(8,128)}) custom-call(s32[4]{0:T(128)S(1)} %copy-done.13, bf16[1024,512]{1,0:T(8,128)(2,1)S(1)} %get-tuple-element.189.refs_1_, bf16[1024,2560]{1,0:T(8,128)(2,1)S(1)} %get-tuple-element.184.refs_11_.refs_2_, ...), custom_call_target="tpu_custom_call" | custom-call | tf_op jit(solution)/shard_map/halves0/pallas_call | solution.py:64
  141.8 3.5 %collective-permute-done.5.refs_2_ = bf16[256,512]{1,0:T(8,128)(2,1)S(1)} collective-permute-done((bf16[256,512]{1,0:T(8,128)(2,1)S(1)}, bf16[256,512]{1,0:T(8,128)(2,1)S(1)}, u32[]{:S(2)}, u32[]{:S(2)}) %collective-permute-start.5) | collective-permute-done | bytes 262176 | tf_op jit(solution)/shard_map/ppermute | solution.py:889
  145.2 2.9 %collective-permute-start.13 = (bf16[80,512]{1,0:T(8,128)(2,1)S(1)}, bf16[80,512]{1,0:T(8,128)(2,1)S(1)}, u32[]{:S(2)}, u32[]{:S(2)}) collective-permute-start(bf16[80,512]{1,0:T(8,128)(2,1)S(1)} %get-tuple-element.213), channel_id=1, source_target_pairs={{0,3},{1,2},{2,1},{3,0},{4,7},{5,6},{6,5},{7,4},{8,11},{9,10},{10,... | collective-permute-start | bytes 245768 | tf_op jit(solution)/shard_map/ppermute | solution.py:889
  161.8 3.2 %collective-permute-done.9.refs_3_ = bf16[64,512]{1,0:T(8,128)(2,1)S(1)} collective-permute-done((bf16[64,512]{1,0:T(8,128)(2,1)S(1)}, bf16[64,512]{1,0:T(8,128)(2,1)S(1)}, u32[]{:S(2)}, u32[]{:S(2)}) %collective-permute-start.9) | collective-permute-done | bytes 65568 | tf_op jit(solution)/shard_map/ppermute | solution.py:889
  165.6 4.4 %collective-permute-done.18.refs_3_ = bf16[80,512]{1,0:T(8,128)(2,1)S(1)} collective-permute-done((bf16[80,512]{1,0:T(8,128)(2,1)S(1)}, bf16[80,512]{1,0:T(8,128)(2,1)S(1)}, u32[]{:S(2)}, u32[]{:S(2)}) %collective-permute-start.18) | collective-permute-done | bytes 81952 | tf_op jit(solution)/shard_map/ppermute | solution.py:889
  186.0 3.7 %collective-permute-done.24.refs_7_ = bf16[272,512]{1,0:T(8,128)(2,1)} collective-permute-done((bf16[272,512]{1,0:T(8,128)(2,1)S(1)}, bf16[272,512]{1,0:T(8,128)(2,1)}, u32[]{:S(2)}, u32[]{:S(2)}) %collective-permute-start.24) | collective-permute-done | bytes 278560 | tf_op jit(solution)/shard_map/ppermute | solution.py:889
  189.8 4.2 %collective-permute-done.22.refs_4_ = bf16[256,512]{1,0:T(8,128)(2,1)} collective-permute-done((bf16[256,512]{1,0:T(8,128)(2,1)S(1)}, bf16[256,512]{1,0:T(8,128)(2,1)}, u32[]{:S(2)}, u32[]{:S(2)}) %collective-permute-start.22) | collective-permute-done | bytes 262176 | tf_op jit(solution)/shard_map/ppermute | solution.py:889
  194.0 3.1 %collective-permute-done.21.refs_3_ = bf16[256,512]{1,0:T(8,128)(2,1)} collective-permute-done((bf16[256,512]{1,0:T(8,128)(2,1)S(1)}, bf16[256,512]{1,0:T(8,128)(2,1)}, u32[]{:S(2)}, u32[]{:S(2)}) %collective-permute-start.21) | collective-permute-done | bytes 262176 | tf_op jit(solution)/shard_map/ppermute | solution.py:889
  203.3 6.1 %results.1 = (f32[2,512,1024]{2,1,0:T(8,128)}, f32[2,512,512]{2,1,0:T(8,128)}, f32[2,512,512]{2,1,0:T(8,128)}, f32[2,512]{1,0:T(2,128)}, f32[2,512]{1,0:T(2,128)...) custom-call(s32[4]{0:T(128)S(1)} %copy-done.13, ...), custom_call_target="tpu_custom_call" | custom-call | flops 7699999744 | bytes 21000000 | tf_op jit(solution)/shard_map/results/pallas_call | solution.py:64
  (146 shorter events, 74.1 us)
Async XLA Ops:
  82.6 9.5 %collective-permute-start.1 = (bf16[272,512]{1,0:T(8,128)(2,1)S(1)}, bf16[272,512]{1,0:T(8,128)(2,1)S(1)}, u32[]{:S(2)}, u32[]{:S(2)}) collective-permute-start(bf16[272,512]{1,0:T(8,128)(2,1)S(1)} %get-tuple-element.176), channel_id=1, source_target_pairs={{0,8},{4,12},{8,0},{12,4},{16,24},{20,28},{24,16},{28,20},{1,9},{5... | collective-permute-start | bytes 835592 | tf_op jit(solution)/shard_map/ppermute | solution.py:889
  83.2 15.7 %collective-permute-start.2 = (bf16[272,512]{1,0:T(8,128)(2,1)S(1)}, bf16[272,512]{1,0:T(8,128)(2,1)S(1)}, u32[]{:S(2)}, u32[]{:S(2)}) collective-permute-start(bf16[272,512]{1,0:T(8,128)(2,1)S(1)} %get-tuple-element.177), channel_id=1, source_target_pairs={{0,16},{4,20},{8,24},{12,28},{16,0},{20,4},{24,8},{28,12},{1,17},{... | collective-permute-start | bytes 835592 | tf_op jit(solution)/shard_map/ppermute | solution.py:889
  83.7 15.1 %collective-permute-start.3 = (bf16[272,512]{1,0:T(8,128)(2,1)S(1)}, bf16[272,512]{1,0:T(8,128)(2,1)S(1)}, u32[]{:S(2)}, u32[]{:S(2)}) collective-permute-start(bf16[272,512]{1,0:T(8,128)(2,1)S(1)} %get-tuple-element.178), channel_id=1, source_target_pairs={{0,24},{4,28},{8,16},{12,20},{16,8},{20,12},{24,0},{28,4},{1,25},{... | collective-permute-start | bytes 835592 | tf_op jit(solution)/shard_map/ppermute | solution.py:889
  86.7 13.5 %all-to-all-start.5 = ((f32[32,2,512]{2,1,0:T(2,128)}), f32[32,2,512]{2,1,0:T(2,128)S(1)}, u32[]{:S(2)}, u32[]{:S(2)}) async-start(f32[32,2,512]{2,1,0:T(2,128)} %get-tuple-element.172), calls=%async_computation.5 | async-start | bytes 262144 | tf_op jit(solution)/shard_map/all_to_all | solution.py:1049
  127.1 56.8 %all-to-all-start.7 = ((f32[32,8,512]{2,1,0:T(8,128)}), f32[32,8,512]{2,1,0:T(8,128)S(1)}, u32[]{:S(2)}, u32[]{:S(2)}) async-start(f32[32,8,512]{2,1,0:T(8,128)} %get-tuple-element.192), calls=%async_computation.7 | async-start | bytes 1048576 | tf_op jit(solution)/shard_map/all_to_all | solution.py:1049
  134.0 11.2 %collective-permute-start.5 = (bf16[256,512]{1,0:T(8,128)(2,1)S(1)}, bf16[256,512]{1,0:T(8,128)(2,1)S(1)}, u32[]{:S(2)}, u32[]{:S(2)}) collective-permute-start(bf16[256,512]{1,0:T(8,128)(2,1)S(1)} %get-tuple-element.202), channel_id=1, source_target_pairs={{0,8},{4,12},{8,0},{12,4},{16,24},{20,28},{24,16},{28,20},{1,9},{5... | collective-permute-start | bytes 786440 | tf_op jit(solution)/shard_map/ppermute | solution.py:889
  135.7 14.4 %collective-permute-start.6 = (bf16[256,512]{1,0:T(8,128)(2,1)S(1)}, bf16[256,512]{1,0:T(8,128)(2,1)S(1)}, u32[]{:S(2)}, u32[]{:S(2)}) collective-permute-start(bf16[256,512]{1,0:T(8,128)(2,1)S(1)} %get-tuple-element.203), channel_id=1, source_target_pairs={{0,16},{4,20},{8,24},{12,28},{16,0},{20,4},{24,8},{28,12},{1,17},{... | collective-permute-start | bytes 786440 | tf_op jit(solution)/shard_map/ppermute | solution.py:889
  137.2 14.2 %collective-permute-start.7 = (bf16[256,512]{1,0:T(8,128)(2,1)S(1)}, bf16[256,512]{1,0:T(8,128)(2,1)S(1)}, u32[]{:S(2)}, u32[]{:S(2)}) collective-permute-start(bf16[256,512]{1,0:T(8,128)(2,1)S(1)} %get-tuple-element.204), channel_id=1, source_target_pairs={{0,24},{4,28},{8,16},{12,20},{16,8},{20,12},{24,0},{28,4},{1,25},{... | collective-permute-start | bytes 786440 | tf_op jit(solution)/shard_map/ppermute | solution.py:889
  137.6 18.1 %collective-permute-start.11 = (bf16[80,512]{1,0:T(8,128)(2,1)S(1)}, bf16[80,512]{1,0:T(8,128)(2,1)S(1)}, u32[]{:S(2)}, u32[]{:S(2)}) collective-permute-start(bf16[80,512]{1,0:T(8,128)(2,1)S(1)} %get-tuple-element.211), channel_id=1, source_target_pairs={{0,1},{1,0},{2,3},{3,2},{4,5},{5,4},{6,7},{7,6},{8,9},{9,8},{10,11... | collective-permute-start | bytes 245768 | tf_op jit(solution)/shard_map/ppermute | solution.py:889
  139.3 17.5 %collective-permute-start.12 = (bf16[80,512]{1,0:T(8,128)(2,1)S(1)}, bf16[80,512]{1,0:T(8,128)(2,1)S(1)}, u32[]{:S(2)}, u32[]{:S(2)}) collective-permute-start(bf16[80,512]{1,0:T(8,128)(2,1)S(1)} %get-tuple-element.212), channel_id=1, source_target_pairs={{0,2},{1,3},{2,0},{3,1},{4,6},{5,7},{6,4},{7,5},{8,10},{9,11},{10,... | collective-permute-start | bytes 245768 | tf_op jit(solution)/shard_map/ppermute | solution.py:889
  145.2 11.6 %collective-permute-start.13 = (bf16[80,512]{1,0:T(8,128)(2,1)S(1)}, bf16[80,512]{1,0:T(8,128)(2,1)S(1)}, u32[]{:S(2)}, u32[]{:S(2)}) collective-permute-start(bf16[80,512]{1,0:T(8,128)(2,1)S(1)} %get-tuple-element.213), channel_id=1, source_target_pairs={{0,3},{1,2},{2,1},{3,0},{4,7},{5,6},{6,5},{7,4},{8,11},{9,10},{10,... | collective-permute-start | bytes 245768 | tf_op jit(solution)/shard_map/ppermute | solution.py:889
  152.1 8.0 %collective-permute-start.8 = (bf16[64,512]{1,0:T(8,128)(2,1)S(1)}, bf16[64,512]{1,0:T(8,128)(2,1)S(1)}, u32[]{:S(2)}, u32[]{:S(2)}) collective-permute-start(bf16[64,512]{1,0:T(8,128)(2,1)S(1)} %get-tuple-element.207), channel_id=1, source_target_pairs={{0,1},{1,0},{2,3},{3,2},{4,5},{5,4},{6,7},{7,6},{8,9},{9,8},{10,11... | collective-permute-start | bytes 196616 | tf_op jit(solution)/shard_map/ppermute | solution.py:889
  154.0 11.0 %collective-permute-start.9 = (bf16[64,512]{1,0:T(8,128)(2,1)S(1)}, bf16[64,512]{1,0:T(8,128)(2,1)S(1)}, u32[]{:S(2)}, u32[]{:S(2)}) collective-permute-start(bf16[64,512]{1,0:T(8,128)(2,1)S(1)} %get-tuple-element.208), channel_id=1, source_target_pairs={{0,2},{1,3},{2,0},{3,1},{4,6},{5,7},{6,4},{7,5},{8,10},{9,11},{10,... | collective-permute-start | bytes 196616 | tf_op jit(solution)/shard_map/ppermute | solution.py:889
  155.7 9.3 %collective-permute-start.10 = (bf16[64,512]{1,0:T(8,128)(2,1)S(1)}, bf16[64,512]{1,0:T(8,128)(2,1)S(1)}, u32[]{:S(2)}, u32[]{:S(2)}) collective-permute-start(bf16[64,512]{1,0:T(8,128)(2,1)S(1)} %get-tuple-element.209), channel_id=1, source_target_pairs={{0,3},{1,2},{2,1},{3,0},{4,7},{5,6},{6,5},{7,4},{8,11},{9,10},{10,... | collective-permute-start | bytes 196616 | tf_op jit(solution)/shard_map/ppermute | solution.py:889
  157.4 8.2 %collective-permute-start.19 = (bf16[80,512]{1,0:T(8,128)(2,1)S(1)}, bf16[80,512]{1,0:T(8,128)(2,1)S(1)}, u32[]{:S(2)}, u32[]{:S(2)}) collective-permute-start(bf16[80,512]{1,0:T(8,128)(2,1)S(1)} %get-tuple-element.217.refs_1_), channel_id=1, source_target_pairs={{0,3},{1,2},{2,1},{3,0},{4,7},{5,6},{6,5},{7,4},{8,11},{9,10},{10,... | collective-permute-start | bytes 245768 | tf_op jit(solution)/shard_map/ppermute | solution.py:889
  160.2 9.9 %collective-permute-start.18 = (bf16[80,512]{1,0:T(8,128)(2,1)S(1)}, bf16[80,512]{1,0:T(8,128)(2,1)S(1)}, u32[]{:S(2)}, u32[]{:S(2)}) collective-permute-start(bf16[80,512]{1,0:T(8,128)(2,1)S(1)} %get-tuple-element.217.refs_1_), channel_id=1, source_target_pairs={{0,2},{1,3},{2,0},{3,1},{4,6},{5,7},{6,4},{7,5},{8,10},{9,11},{10,... | collective-permute-start | bytes 245768 | tf_op jit(solution)/shard_map/ppermute | solution.py:889
  160.2 9.9 %collective-permute-start.17 = (bf16[80,512]{1,0:T(8,128)(2,1)S(1)}, bf16[80,512]{1,0:T(8,128)(2,1)S(1)}, u32[]{:S(2)}, u32[]{:S(2)}) collective-permute-start(bf16[80,512]{1,0:T(8,128)(2,1)S(1)} %get-tuple-element.217.refs_1_), channel_id=1, source_target_pairs={{0,1},{1,0},{2,3},{3,2},{4,5},{5,4},{6,7},{7,6},{8,9},{9,8},{10,11... | collective-permute-start | bytes 245768 | tf_op jit(solution)/shard_map/ppermute | solution.py:889
  170.7 12.0 %collective-permute-start.25 = (bf16[272,512]{1,0:T(8,128)(2,1)S(1)}, bf16[272,512]{1,0:T(8,128)(2,1)S(1)}, u32[]{:S(2)}, u32[]{:S(2)}) collective-permute-start(bf16[272,512]{1,0:T(8,128)(2,1)S(1)} %get-tuple-element.224.refs_5_), channel_id=1, source_target_pairs={{0,24},{4,28},{8,16},{12,20},{16,8},{20,12},{24,0},{28,4},{1,25},{... | collective-permute-start | bytes 835592 | tf_op jit(solution)/shard_map/ppermute | solution.py:889
  171.8 6.2 %collective-permute-start.16 = (bf16[64,512]{1,0:T(8,128)(2,1)S(1)}, bf16[64,512]{1,0:T(8,128)(2,1)S(1)}, u32[]{:S(2)}, u32[]{:S(2)}) collective-permute-start(bf16[64,512]{1,0:T(8,128)(2,1)S(1)} %get-tuple-element.216.refs_1_), channel_id=1, source_target_pairs={{0,3},{1,2},{2,1},{3,0},{4,7},{5,6},{6,5},{7,4},{8,11},{9,10},{10,... | collective-permute-start | bytes 196616 | tf_op jit(solution)/shard_map/ppermute | solution.py:889
  176.2 13.6 %collective-permute-start.24 = (bf16[272,512]{1,0:T(8,128)(2,1)S(1)}, bf16[272,512]{1,0:T(8,128)(2,1)}, u32[]{:S(2)}, u32[]{:S(2)}) collective-permute-start(bf16[272,512]{1,0:T(8,128)(2,1)S(1)} %get-tuple-element.224.refs_5_), channel_id=1, source_target_pairs={{0,16},{4,20},{8,24},{12,28},{16,0},{20,4},{24,8},{28,12},{1,17},{... | collective-permute-start | bytes 835592 | tf_op jit(solution)/shard_map/ppermute | solution.py:889
  178.0 11.8 %collective-permute-start.23 = (bf16[272,512]{1,0:T(8,128)(2,1)S(1)}, bf16[272,512]{1,0:T(8,128)(2,1)}, u32[]{:S(2)}, u32[]{:S(2)}) collective-permute-start(bf16[272,512]{1,0:T(8,128)(2,1)S(1)} %get-tuple-element.224.refs_5_), channel_id=1, source_target_pairs={{0,8},{4,12},{8,0},{12,4},{16,24},{20,28},{24,16},{28,20},{1,9},{5... | collective-permute-start | bytes 835592 | tf_op jit(solution)/shard_map/ppermute | solution.py:889
  180.4 13.6 %collective-permute-start.22 = (bf16[256,512]{1,0:T(8,128)(2,1)S(1)}, bf16[256,512]{1,0:T(8,128)(2,1)}, u32[]{:S(2)}, u32[]{:S(2)}) collective-permute-start(bf16[256,512]{1,0:T(8,128)(2,1)S(1)} %get-tuple-element.223.refs_1_), channel_id=1, source_target_pairs={{0,24},{4,28},{8,16},{12,20},{16,8},{20,12},{24,0},{28,4},{1,25},{... | collective-permute-start | bytes 786440 | tf_op jit(solution)/shard_map/ppermute | solution.py:889
  182.3 14.8 %collective-permute-start.21 = (bf16[256,512]{1,0:T(8,128)(2,1)S(1)}, bf16[256,512]{1,0:T(8,128)(2,1)}, u32[]{:S(2)}, u32[]{:S(2)}) collective-permute-start(bf16[256,512]{1,0:T(8,128)(2,1)S(1)} %get-tuple-element.223.refs_1_), channel_id=1, source_target_pairs={{0,16},{4,20},{8,24},{12,28},{16,0},{20,4},{24,8},{28,12},{1,17},{... | collective-permute-start | bytes 786440 | tf_op jit(solution)/shard_map/ppermute | solution.py:889
  182.7 14.4 %collective-permute-start.20 = (bf16[256,512]{1,0:T(8,128)(2,1)S(1)}, bf16[256,512]{1,0:T(8,128)(2,1)}, u32[]{:S(2)}, u32[]{:S(2)}) collective-permute-start(bf16[256,512]{1,0:T(8,128)(2,1)S(1)} %get-tuple-element.223.refs_1_), channel_id=1, source_target_pairs={{0,8},{4,12},{8,0},{12,4},{16,24},{20,28},{24,16},{28,20},{1,9},{5... | collective-permute-start | bytes 786440 | tf_op jit(solution)/shard_map/ppermute | solution.py:889
  (45 other events, 233.3 us)

commit v3 on v2

--- a/solution.py
+++ b/solution.py
@@ -16,7 +16,7 @@
 PARTS = 1
 EXTRA = 16
 LANES = 128
-VMEM_LIMIT = 24 * 1024 * 1024
+VMEM_LIMIT = 32 * 1024 * 1024
 
 in_vmem = pl.BlockSpec(memory_space=pltpu.VMEM)
 in_smem = pl.BlockSpec(memory_space=pltpu.SMEM)
@@ -628,16 +628,14 @@
     k, info_ref, parts_ref, stats_ref, skip_ref, decay_ref, phase_ref, gain_ref, shift_ref, *refs
 ):
     reverse = last = k == 0
-    if last:
-        small_refs, refs = refs[:2], refs[2:]
     ends_ref, glu_pack_ref = refs[:2]
     states, width = 2 * decay_ref.shape[1], stats_ref.shape[1]
     mixed_ref, dh_ref, back_ref = glu_pack(width, states).views(glu_pack_ref, "mixed", "dh", "back")
     normed_ref, state_ref, weight_ref = refs[2:5]
     tables, refs = refs[-4:], refs[5:-4]
     if last:
-        back_lifted_ref, sums_ref, ahead_ref = refs[:3]
-        refs = refs[3:]
+        back_lifted_ref, sums_ref, lam_grad_ref, scale_grad_ref, ahead_ref = refs[:5]
+        refs = refs[5:]
     else:
         out_ref, sums_ref, lam_grad_ref, scale_grad_ref = refs[:4]
         back_lifted_ref, back_normed_ref, kept_back_ref, kept_normed_ref = lift_pack(width, states).views(
@@ -711,21 +709,9 @@
     scale_grad = jnp.sum(scale_acc_ref[...], axis=0, keepdims=True)
     acc_ref[0:1, :] = (gain_sum - shift_row * shift_sum) / gain
     acc_ref[1:2, :] = shift_sum
-    devices = sums_ref.shape[0]
-    if last:
-        skip_grad_ref, bias_grad_ref = small_refs
-        acc_ref[2:3, :] = skip_grad_ref[...]
-        acc_ref[3:4, :] = bias_grad_ref[:, :width]
-        acc_ref[4:5, :] = bias_grad_ref[:, width:]
-        acc_ref[5:6, :states] = lam_grad[:, :states]
-        acc_ref[5:6, states : 2 * states] = lam_grad[:, states:]
-        acc_ref[6:7, :states] = scale_grad
-        acc_ref[6:7, states:] = jnp.zeros((1, width - states), f32)
-        acc_ref[7:8, :] = jnp.zeros((1, width), f32)
-    else:
-        lam_grad_ref[...] = lam_grad
-        scale_grad_ref[...] = scale_grad
-    for j in range(devices):
+    lam_grad_ref[...] = lam_grad
+    scale_grad_ref[...] = scale_grad
+    for j in range(sums_ref.shape[0]):
         sums_ref[j] = acc_ref[...]
 
 
@@ -735,12 +721,11 @@
     rows, width, states = packed.shape[0], stats.shape[1], 2 * decay.shape[1]
     seq_devices, seqs, _ = parts.shape
     table = ends.shape
-    acc = (8, width) if k == 0 else (2, width)
+    acc = (2, width)
+    outs = [near((rows, states if k == 0 else lift_pack(width, states).width), bf16), moved((devices,) + acc, f32)]
+    outs += [moved((1, states), f32), moved((1, states // 2), f32)]
     if k == 0:
-        outs = [near((rows, states), bf16), moved((devices,) + acc, f32), moved((rows, width), bf16)]
-    else:
-        outs = [near((rows, lift_pack(width, states).width), bf16), moved((devices, 2, width), f32)]
-        outs += [moved((1, states), f32), moved((1, states // 2), f32)]
+        outs.append(moved((rows, width), bf16))
     scratch = [
         pltpu.VMEM(table, f32),
         pltpu.VMEM((rows // BLOCKS, states), f32),
@@ -750,6 +735,16 @@
     ]
     scratch += Powers.scratch(seqs, seq_devices, states // 2, True)
     return call(partial(lift_back_kernel, k), info, inputs, arrays, (), outs, scratch, "lift_back", after, fetch)
+
+
+def two_parts(rows):
+    high = rows.astype(bf16).astype(f32)
+    return jnp.concatenate([high, rows - high], axis=0)
+
+
+def one_part(rows):
+    half = rows.shape[0] // 2
+    return rows[:half] + rows[half:]
 
 
 def halves_kernel(parts, pairs, small, info_ref, *refs):
@@ -772,7 +767,9 @@
         low = jnp.concatenate([skip_ref[...], bias_ref[:, :width], bias_ref[:, width:]], axis=0)
         scale = jnp.concatenate([scale_ref[...], jnp.zeros((1, width - scale_ref.shape[1]), f32)], axis=1)
         high = jnp.concatenate([lam_ref[...], scale, jnp.zeros((1, width), f32)], axis=0)
-        low, high = (jnp.concatenate([x, jnp.zeros((extra - 3, width), f32)], axis=0).astype(bf16) for x in (low, high))
+        rest = [jnp.zeros((EXTRA // 2 - 3, width), f32)], [jnp.zeros((extra - EXTRA, width), f32)]
+        low, high = (two_parts(jnp.concatenate([x, *rest[0]], axis=0)) for x in (low, high))
+        low, high = (jnp.concatenate([x, *rest[1]], axis=0).astype(bf16) for x in (low, high))
         keep_ref[first:, :] = jnp.where(even, low, high)
         send_ref[first:, :] = jnp.where(even, high, low)
 
@@ -811,6 +808,8 @@
                 if xor:
                     start = pl.multiple_of(start, 16)
                 total = total_of(refs[2 * n : 2 * n + 2], pl.ds(start, share))
+                if share == EXTRA:
+                    total = two_parts(one_part(total))
                 if xor:
                     outs[m][low : low + share, :] = total.astype(outs[m].dtype)
                 else:
@@ -836,11 +835,10 @@
     place = place_of("batch")
     rows = batches * share
     low_ref[...] = total_of(arrays, slice(0, rows)).reshape(batches, share, width)
-    under = total_of(arrays, slice(rows, rows + extra)) if extra else None
+    under = two_parts(one_part(total_of(arrays, slice(rows, rows + extra))))
     for m in range(batches):
         outs[m][:share, :] = low_ref[place ^ m].astype(outs[m].dtype)
-        if extra:
-            outs[m][share:, :] = under.astype(outs[m].dtype)
+        outs[m][share:, :] = under.astype(outs[m].dtype)
 
 
 def cut(info, arrays, extra, after=()):
@@ -856,7 +854,9 @@
     total = refs[0][...].astype(f32)
     for ref in refs[1:-1]:
         total += ref[...].astype(f32)
-    refs[-1][...] = total.astype(bf16)
+    rows = total.shape[0] - EXTRA
+    refs[-1][:rows, :] = total[:rows].astype(bf16)
+    refs[-1][rows:, :] = two_parts(one_part(total[rows:])).astype(bf16)
 
 
 def sum_of(info, arrays, after=()):
@@ -871,8 +871,7 @@
         low_ref[place ^ m] = ref[:share, :].astype(f32)
     rows = batches * share
     out_ref[:rows, :] = low_ref[...].reshape(rows, width).astype(bf16)
-    if out_ref.shape[0] > rows:
-        out_ref[rows:, :] = pieces[0][share:, :]
+    out_ref[rows:, :] = pieces[0][share:, :]
 
 
 def join(info, arrays, extra, after=()):
@@ -902,23 +901,20 @@
 
 
 def gate(info, arrays, after):
-    outs = [(in_hbm, pltpu.HBM(x.shape, x.dtype)) for x in arrays]
+    anywhere = pl.BlockSpec(memory_space=pl.ANY)
+    outs = [(anywhere, jax.ShapeDtypeStruct(x.shape, x.dtype)) for x in arrays]
     aliases = {1 + i: i for i in range(len(arrays))}
-    return run(gate_kernel, info, list(map(there, arrays)), [in_hbm] * len(arrays), outs, [], "gate", after, aliases, 0.5)
-
-
-def small_grads(sums, norm1, low, high, decay_log, phase_log, refs):
+    return run(gate_kernel, info, list(arrays), [anywhere] * len(arrays), outs, [], "gate", after, aliases)
+
+
+def small_grads(norms, rows, decay_log, phase_log, refs):
     gain_ref, shift_ref, decay_grad_ref, phase_grad_ref, skip_grad_ref, bias_grad_ref = refs
     blocks, states = decay_log.shape
-    width = sums.shape[1]
-    rows = (
-        [sums[n : n + 1] for n in range(2, 7)],
-        [low[0:1], low[1:2], low[2:3], high[0:1], high[1:2]],
-    )
-    norms = ([sums[0:1], sums[1:2]], [norm1[0:1], norm1[1:2]])
+    width = norms[0].shape[1]
     for k in range(blocks):
-        gain_ref[k : k + 1, :], shift_ref[k : k + 1, :] = norms[k]
-        skip, bias_low, bias_high, lam, scale = rows[k]
+        gain_ref[k : k + 1, :], shift_ref[k : k + 1, :] = norms[k][0:1], norms[k][1:2]
+        low, high = rows[k]
+        skip, bias_low, bias_high, lam, scale = low[0:1], low[1:2], low[2:3], high[0:1], high[1:2]
         skip_grad_ref[k : k + 1, :] = skip
         bias_grad_ref[k : k + 1, :width] = bias_low
         bias_grad_ref[k : k + 1, width:] = bias_high
@@ -931,10 +927,28 @@
         phase_grad_ref[k : k + 1, :] = angle * (imag * lam_real - real * lam_imag)
 
 
-def results_kernel(chips, info_ref, sums_ref, norm1_ref, decay_ref, phase_ref, *refs):
-    pieces, refs = refs[: 4 * chips], refs[4 * chips :]
-    glu_ref, mix_ref, lift_ref, *small_refs = refs[:9]
-    low_ref, under_ref, wide_ref, in_sems, sems = refs[9:]
+def input_grad(where, sums, stats_ref, gain_ref, tokens_ref, wide_ref, grad_ref):
+    seqs, span, width = tokens_ref.shape
+    shuffle = shuffle_matrix(span, True)
+    average, root = stats_ref[0:1, :], stats_ref[1:2, :]
+    factor = root * gain_ref[0:1, :] / stats_ref[2:3, 0:1]
+    by_gain = factor * sums[0:1] * root
+    fixed = factor * sums[1:2] - by_gain * average
+    step = lax.broadcasted_iota(jnp.int32, (span, 1), 0)
+    for s in range(seqs):
+        valid = (step < where.lefts[s]).astype(f32)
+        ahead = dot(shuffle, wide_ref[:, s].reshape(span, width).astype(bf16))
+        grad_ref[s] = (ahead - valid * (fixed + by_gain * tokens_ref[s].astype(f32))).astype(bf16)
+
+
+def results_kernel(chips, info_ref, sums_ref, norm1_ref, decay_ref, phase_ref, stats_ref, gain_ref, *refs):
+    (tokens_in, ahead_in), pieces, refs = refs[:2], refs[2 : 2 + 4 * chips], refs[2 + 4 * chips :]
+    glu_ref, mix_ref, lift_ref, grad_out, *small_refs = refs[:10]
+    low_ref, under_ref, wide_ref, tokens_ref, ahead_ref, rows_ref, grad_ref, in_sems, sems, own_sems = refs[10:]
+    own = [
+        pltpu.make_async_copy(ahead_in, ahead_ref, own_sems.at[0]),
+        pltpu.make_async_copy(tokens_in, tokens_ref, own_sems.at[1]),
+    ]
     place = place_of("seq")
     core = lax.axis_index("seq") % 2
     _, rows, width = wide_ref.shape
@@ -942,20 +956,18 @@
     arriving = []
     for n, piece in enumerate(pieces):
         parts = [pltpu.make_async_copy(piece.at[pl.ds(0, rows), :], low_ref.at[n], in_sems.at[n, 0])]
-        if n >= 2 * chips:
-            under = piece.at[pl.ds(rows, EXTRA), :]
-            parts.append(pltpu.make_async_copy(under, under_ref.at[n - 2 * chips], in_sems.at[n, 1]))
+        parts.append(pltpu.make_async_copy(piece.at[pl.ds(rows, EXTRA), :], under_ref.at[n], in_sems.at[n, 1]))
         begin(parts)
         arriving.append(parts)
+    begin(own)
     copies = []
-    extras = [jnp.zeros((EXTRA, width), f32)] * 2
+    extras = [[jnp.zeros((EXTRA // 2, width), f32)] * 2 for _ in range(2)]
     for n in range(4 * chips):
         finished(arriving[n])
         k, n_in = divmod(n, 2 * chips)
         chip, side = place ^ (n_in % chips), core if n_in < chips else 1 - core
-        if k == 1:
-            extra = under_ref[n_in].astype(f32)
-            extras[n_in // chips] = jnp.where(chip == 0, extra, extras[n_in // chips])
+        extra = one_part(under_ref[n].astype(f32))
+        extras[k][n_in // chips] = jnp.where(chip == 0, extra, extras[k][n_in // chips])
         column = pl.multiple_of(side * width, width)
         row = pl.multiple_of(chip * half, 8)
         low = pl.multiple_of(side * (quarter * chips) + chip * quarter, 8)
@@ -970,11 +982,16 @@
             copies.append(pltpu.make_async_copy(wide_ref.at[n, pl.ds(first, size), :], target, sems.at[n, i]))
             copies[-1].start()
     even = core == 0
+    sums = sums_ref[...]
+    finished(own)
+    rows_ref[...] = ahead_ref[...].astype(f32).reshape(rows_ref.shape)
+    seqs, span, _ = tokens_ref.shape
+    input_grad(Where(info_ref, seqs, span), sums, stats_ref, gain_ref, tokens_ref, rows_ref, grad_ref)
+    copies.append(pltpu.make_async_copy(grad_ref, grad_out, own_sems.at[2]))
+    copies[-1].start()
     small_grads(
-        jnp.sum(sums_ref[...], axis=0),
-        norm1_ref[...],
-        jnp.where(even, extras[0], extras[1]),
-        jnp.where(even, extras[1], extras[0]),
+        (sums, norm1_ref[...]),
+        [(jnp.where(even, mine, other), jnp.where(even, other, mine)) for mine, other in extras],
         decay_ref[...],
         phase_ref[...],
         small_refs,
@@ -982,24 +999,42 @@
     finished(copies)
 
 
-def results(info, sums, norm1, decay_log, phase_log, pieces, after=()):
+def results(info, sums, norm1, decay_log, phase_log, stats, gain, tokens, ahead, pieces, after=()):
+    seqs, span, _ = tokens.shape
     rows, width = pieces[0].shape
+    rows -= EXTRA
     count = len(pieces)
     anywhere = pl.BlockSpec(memory_space=pl.ANY)
     shapes = [(2, width, 2 * width), (2, width, width), (2, width, width)]
     outs = [(anywhere, jax.ShapeDtypeStruct(shape, f32)) for shape in shapes]
+    outs.append((anywhere, jax.ShapeDtypeStruct(tokens.shape, bf16)))
     blocks, states = decay_log.shape
     outs += [moved((blocks, n), f32) for n in (width, width, states, states, width, 2 * width)]
     scratch = [
         pltpu.VMEM((count, rows, width), bf16),
-        pltpu.VMEM((count // 2, EXTRA, width), bf16),
+        pltpu.VMEM((count, EXTRA, width), bf16),
         pltpu.VMEM((count, rows, width), f32),
+        pltpu.VMEM(tokens.shape, bf16),
+        pltpu.VMEM(ahead.shape, bf16),
+        pltpu.VMEM((span // CHUNKS, seqs, CHUNKS, width), f32),
+        pltpu.VMEM(tokens.shape, bf16),
         pltpu.SemaphoreType.DMA((count, 2)),
         pltpu.SemaphoreType.DMA((count, 3)),
+        pltpu.SemaphoreType.DMA((3,)),
     ]
-    inputs = (sums, norm1, decay_log, phase_log)
-    kernel = partial(results_kernel, count // 4)
-    return call(kernel, info, inputs, (), pieces, outs, scratch, "results", after, us=7.0)
+    inputs = [sums, norm1, decay_log, phase_log, stats, gain]
+    given = [*inputs, *map(there, (tokens, ahead)), *pieces]
+    specs = [in_vmem] * len(inputs) + [in_hbm] * 2 + [anywhere] * count
+    return run(partial(results_kernel, count // 4), info, given, specs, outs, scratch, "results", after, us=7.0)
+
+
+def norms_kernel(info_ref, sums_ref, total_ref):
+    total_ref[...] = jnp.sum(sums_ref[...], axis=0)
+
+
+def norms(info, sums, after=()):
+    outs = [moved(sums.shape[1:], f32)]
+    return call(norms_kernel, info, (sums,), (), (), outs, [], "norms", after, us=0.6)
 
 
 def leave_kernel(seqs, info_ref, rows_ref, out_ref, wide_ref):
@@ -1015,34 +1050,6 @@
     scratch = [pltpu.VMEM((span // CHUNKS, seqs, CHUNKS, width), f32)]
     outs = [moved((seqs, span, width), bf16)]
     return call(partial(leave_kernel, seqs), info, (rows,), (), (), outs, scratch, "leave", after)
-
-
-def input_grad_kernel(
-    info_ref, sums_ref, tokens_ref, ahead_ref, stats_ref, gain_ref, grad_ref, wide_ref
-):
-    seqs, span, width = tokens_ref.shape
-    where = Where(info_ref, seqs, span)
-    wide_ref[...] = ahead_ref[...].astype(f32).reshape(wide_ref.shape)
-    shuffle = shuffle_matrix(span, True)
-    average, root = stats_ref[0:1, :], stats_ref[1:2, :]
-    factor = root * gain_ref[0:1, :] / stats_ref[2:3, 0:1]
-    sums = jnp.sum(sums_ref[...], axis=0)
-    by_gain = factor * sums[0:1] * root
-    fixed = factor * sums[1:2] - by_gain * average
-    step = lax.broadcasted_iota(jnp.int32, (span, 1), 0)
-    for s in range(seqs):
-        valid = (step < where.lefts[s]).astype(f32)
-        ahead = dot(shuffle, wide_ref[:, s].reshape(span, width).astype(bf16))
-        grad_ref[s] = (ahead - valid * (fixed + by_gain * tokens_ref[s].astype(f32))).astype(bf16)
-
-
-def input_grads(info, sums, tokens, ahead, stats, gain, after=()):
-    seqs, span, width = tokens.shape
-    outs = [moved(tokens.shape, bf16)]
-    scratch = [pltpu.VMEM((span // CHUNKS, seqs, CHUNKS, width), f32)]
-    return call(
-        input_grad_kernel, info, (sums, tokens, ahead, stats, gain), (), (), outs, scratch, "input_grad", after, us=2.0
-    )
 
 
 def to_all(x, axes):
@@ -1126,22 +1133,20 @@
     z, xy = range(1, batches), range(2, seq_devices, 2)
     extra = EXTRA * chips
     out = split(info, ((*shares, extra),), [keep1, got1], True, (out.tick,))
-    (sums,) = gate(info, [sums], (out.tick,))
     pieces1 = sent(out, "seq", xy)
     sums = to_all(sums, both)
 
     state_lanes = (slice(None), kept_lanes["state"])
-    pieces1 = there1 = gate(info, pieces1, ())
     out = glu_back(
         0, seqs, seq_devices, info, (*turns, sums, stats1, *norms_in), (lift_packed,),
-        (kept, normed0, glu_weight, mix_weight), rows, width, (there1.tick,),
+        (kept, normed0, glu_weight, mix_weight), rows, width, (),
         [(kept, state_lanes), (lift_weight, 0)],
     )
     glu_packed, bias_grad0, skip_grad0, ends, part, norm_sums1, normed, state, lift_w = out
-    small = (skip_grad0, bias_grad0)
     activated_lanes = (slice(None), kept_lanes["activated"])
-    back_lifted0, sums, ahead, activated = out = lift_back(
-        0, info, (to_all(part, "seq"), stats0, skip_gain, *turns, *norms_in, *small),
+    parts, *pieces1 = gate(info, [to_all(part, "seq"), *pieces1], ())
+    back_lifted0, sums, lam_grad0, scale_grad0, ahead, activated = out = lift_back(
+        0, info, (parts, stats0, skip_gain, *turns, *norms_in),
         (ends, glu_packed, normed, state, lift_w), devices, (), [(kept, activated_lanes)],
     )
 
@@ -1153,32 +1158,31 @@
             ((2, every), (1, glu_lanes["mixed"])),
             ((3, every), (4, every)),
         ),
-        (),
+        (skip_grad0, bias_grad0, lam_grad0, scale_grad0),
         (activated, glu_packed, state, normed, back_lifted0),
         width,
         "halves0",
     )
     got0 = trade(send, "seq", 1)
-    (sums,) = gate(info, [sums], (out.tick,))
+    out1 = cut(info, pieces1, EXTRA, (out.tick,))
+    out0 = split(info, ((*shares, extra),), [keep0, got0], True, (out1.tick,))
+    (sums,) = gate(info, [sums], (out0.tick,))
     sums = to_all(sums, both)
-    out1 = cut(info, pieces1, EXTRA, (out.tick,))
-    out0 = split(info, (shares,), [keep0, got0], True, (out1.tick,))
-    out0 = cut(info, sent(out0, "seq", xy), 0, (out0.tick,))
     sum1 = sum_of(info, sent(out1, "batch", z), (out0.tick,))
-    sum0 = sum_of(info, sent(out0, "batch", z), (sum1.tick,))
-    (own1,) = out = join(info, to_others(sum1[0], "batch", z), EXTRA, (sum0.tick,))
-    (own0,) = out = join(info, to_others(sum0[0], "batch", z), 0, (out.tick,))
-    total = to_others(own0, "seq", xy) + to_others(own1, "seq", xy)
-    (input_grad,) = out = input_grads(info, sums, tokens, ahead, stats0, norm_gain, (out.tick,))
-    total = gate(info, total, (out.tick,))
-    other = [trade(x, "seq", 1) for x in total]
-    total = total[:chips] + other[:chips] + total[chips:] + other[chips:]
-    grad_glu, grad_mix, grad_lift, grad_gain, grad_shift, grad_decay, grad_phase, grad_skip, grad_bias = results(
-        info, sums, norm_sums1, *turns, total
-    )
+    (own1,) = out = join(info, to_others(sum1[0], "batch", z), EXTRA, (sum1.tick,))
+    out0 = cut(info, sent(out0, "seq", xy), EXTRA, (out.tick,))
+    (sums,) = out = norms(info, sums, (out0.tick,))
+    sum0 = sum_of(info, sent(out0, "batch", z), (out.tick,))
+    (own0,) = join(info, to_others(sum0[0], "batch", z), EXTRA)
+    pieces = []
+    for own in (own0, own1):
+        total = to_others(own, "seq", xy)
+        pieces += total + [trade(x, "seq", 1) for x in total]
+    out = results(info, sums, norm_sums1, *turns, stats0, norm_gain, tokens, ahead, pieces)
+    grad_glu, grad_mix, grad_lift, tokens_grad, grad_gain, grad_shift, grad_decay, grad_phase, grad_skip, grad_bias = out
     return (
         produced,
-        input_grad,
+        tokens_grad,
         grad_gain,
         grad_shift,
         grad_lift,

time: 210 us -> 195 us (0.929)
  waiting for transfers between devices: 39.8 us -> 30.3 us
  local copies, waits for them, and re-layouts: 8.34 us -> 2.9 us
    ppermute x34, waiting for transfers between devices: 39.8 us -> 29.7 us  [trade(): return lax.ppermute(x, axis, [(i, i ^ mask) for i in range(size)])]
    unnamed x66 -> x24, local copies, waits for them, and re-layouts: 8.34 us -> 2.9 us
    ppermute x34, starting transfers between devices: 36.4 us -> 34.1 us  [trade(): return lax.ppermute(x, axis, [(i, i ^ mask) for i in range(size)])]
    pallas_call x26 -> x24, Pallas kernels: 62.5 us -> 64 us  [run(): pl.pallas_call(ticking, in_specs=[in_smem] + specs + [in_hbm] * len(after...]
  transfers between devices with their start and end apart: 36 -> 36, of which waited for: 17 -> 11; matrix products, arithmetic and copies ran while one was open for 0% -> 0% of each run, Pallas kernels for 5% -> 9%
where the time goes in v3:
time: 195 us; the launch traced here: 194 us
  Pallas kernels  64 us (33%)
  blocking collectives  56.1 us (29%)
  starting transfers between devices  39.8 us (20%)
  waiting for transfers between devices  30.3 us (16%)
  local copies, waits for them, and re-layouts  2.9 us (1%)
    pallas_call x24, Pallas kernels, run(): pl.pallas_call(ticking, in_specs=[in_smem] + specs + [in_hbm] * len(after...  64 us
    all_to_all x6, blocking collectives, to_all(): return lax.all_to_all(x, axes, split_axis=0, concat_axis=0, tiled=True)  56.1 us
    ppermute x34, starting transfers between devices, trade(): return lax.ppermute(x, axis, [(i, i ^ mask) for i in range(size)])  34.1 us
    ppermute x34, waiting for transfers between devices, trade(): return lax.ppermute(x, axis, [(i, i ^ mask) for i in range(size)])  29.7 us
    all_to_all x2, starting transfers between devices, to_all(): return lax.all_to_all(x, axes, split_axis=0, concat_axis=0, tiled=True)  5.65 us
  transfers between devices with their start and end apart: 36, of which 11 were waited for; matrix products, arithmetic and copies ran while one was open for 0% of the time, Pallas kernels for 9%

profile of v3, /device:TPU:0, one launch (start us, length us, event | category | flops | bytes accessed | tf_op | source)
XLA Modules:
  0.0 194.2 jit_solution(12480264199089331207)
XLA Ops:
  3.6 16.0 %all_to_all.40.refs_1_ = f32[32,2,640]{2,1,0:T(2,128)S(1)} all-to-all(f32[32,2,640]{2,1,0:T(2,128)S(1)} %get-tuple-element.118), channel_id=1, replica_groups=mesh['seq'=8,'batch'=4] {'seq','batch'}, dimensions={0} | all-to-all | bytes 327680 | tf_op jit(solution)/shard_map/all_to_all | solution.py:1056
  22.0 7.4 %all_to_all.41.refs_1_ = f32[8,4,512]{2,1,0:T(4,128)S(1)} all-to-all(f32[8,4,512]{2,1,0:T(4,128)S(1)} %get-tuple-element.121), channel_id=1, replica_groups=mesh['seq'=8,'batch'=4] {'seq'}, dimensions={0} | all-to-all | bytes 131072 | tf_op jit(solution)/shard_map/all_to_all | solution.py:1056
  29.4 6.3 %mix.2 = (f32[1024,512]{1,0:T(8,128)S(1)}, f32[32,2,512]{2,1,0:T(2,128)S(1)}, bf16[1024,2560]{1,0:T(8,128)(2,1)}, bf16[512,512]{1,0:T(8,128)(2,1)S(1)}, bf16[1024,512]{1,0:T(8,128)(2,1)}, /*index=5*/f32[8,128]{1,0:T(8,128)}) custom-call(s32[4]{0:T(128)S(1)} %copy-done.8, f32[8,4,512]{2,1,0:T(4,128)S(1)} %all_to_all.41.refs_1_, f32[2,512]{1,0:T(2,128)S(1)} %copy-done.9, ...), custom_call_target="tpu_custom_call" | custom-call | tf_op jit(solution)/shard_map/mix/pallas_call | solution.py:64
  35.7 10.1 %all_to_all.42.refs_1_ = f32[32,2,512]{2,1,0:T(2,128)S(1)} all-to-all(f32[32,2,512]{2,1,0:T(2,128)S(1)} %get-tuple-element.128), channel_id=1, replica_groups=mesh['seq'=8,'batch'=4] {'seq','batch'}, dimensions={0} | all-to-all | bytes 262144 | tf_op jit(solution)/shard_map/all_to_all | solution.py:1056
  47.8 7.4 %all_to_all.43.refs_1_ = f32[8,4,512]{2,1,0:T(4,128)S(1)} all-to-all(f32[8,4,512]{2,1,0:T(4,128)S(1)} %get-tuple-element.132), channel_id=1, replica_groups=mesh['seq'=8,'batch'=4] {'seq'}, dimensions={0} | all-to-all | bytes 131072 | tf_op jit(solution)/shard_map/all_to_all | solution.py:1056
  55.2 5.2 %mix.3 = (bf16[1024,512]{1,0:T(8,128)(2,1)S(1)}, bf16[1024,512]{1,0:T(8,128)(2,1)S(1)}, bf16[1024,512]{1,0:T(8,128)(2,1)S(1)}, bf16[1024,512]{1,0:T(8,128)(2,1)S...) custom-call(s32[4]{0:T(128)S(1)} %copy-done.8, ...), custom_call_target="tpu_custom_call" | custom-call | tf_op jit(solution)/shard_map/mix/pallas_call | solution.py:64
  60.5 4.8 %glu_back.2 = (bf16[1024,2560]{1,0:T(8,128)(2,1)S(1)}, f32[1,1024]{1,0:T(1,128)S(1)}, f32[1,512]{1,0:T(1,128)S(1)}, f32[4,32,128]{2,1,0:T(8,128)S(1)}, f32[8,4,5...) custom-call(s32[4]{0:T(128)S(1)} %copy-done.8, ...), custom_call_target="tpu_custom_call" | custom-call | tf_op jit(solution)/shard_map/glu_back/pallas_call | solution.py:64
  65.2 7.4 %all_to_all.44.refs_1_ = f32[8,4,512]{2,1,0:T(4,128)S(1)} all-to-all(f32[8,4,512]{2,1,0:T(4,128)S(1)} %get-tuple-element.146), channel_id=1, replica_groups=mesh['seq'=8,'batch'=4] {'seq'}, dimensions={0} | all-to-all | bytes 131072 | tf_op jit(solution)/shard_map/all_to_all | solution.py:1056
  72.6 3.9 %lift_back.2 = (bf16[1024,2048]{1,0:T(8,128)(2,1)S(1)}, f32[32,2,512]{2,1,0:T(2,128)}, f32[1,512]{1,0:T(1,128)S(1)}, f32[1,256]{1,0:T(1,128)S(1)}, f32[8,128]{1,0:T(8,128)}) custom-call(s32[4]{0:T(128)S(1)} %copy-done.8, f32[8,4,512]{2,1,0:T(4,128)S(1)} %all_to_all.44.refs_1_, f32[8,512]{1,0:T(8,128)S(1)} %get-tuple-element.147.refs_2_.refs_4_, ...), custom_call_target="tpu_custom_call" | custom-call | tf_op jit(solution)/shard_map/lift_back/pallas_call | solution.py:64
  76.5 3.9 %halves1.1 = (bf16[1088,512]{1,0:T(8,128)(2,1)S(1)}, bf16[1088,512]{1,0:T(8,128)(2,1)}, f32[8,128]{1,0:T(8,128)}) custom-call(s32[4]{0:T(128)S(1)} %copy-done.8, f32[1,512]{1,0:T(1,128)S(1)} %get-tuple-element.144.refs_1_, f32[1,1024]{1,0:T(1,128)S(1)} %get-tuple-element.145.refs_2_, f32[1,512]{1,0:T(1,128)S(1)} %get-tuple-element.152.refs_3_, ...), custom_call_target="tpu_custom_call" | custom-call | tf_op jit(solution)/shard_map/halves1/pallas_call | solution.py:64
  80.5 2.8 %all-to-all-start.5 = ((f32[32,2,512]{2,1,0:T(2,128)}), f32[32,2,512]{2,1,0:T(2,128)S(1)}, u32[]{:S(2)}, u32[]{:S(2)}) async-start(f32[32,2,512]{2,1,0:T(2,128)} %get-tuple-element.158), calls=%async_computation.5 | async-start | bytes 262144 | tf_op jit(solution)/shard_map/all_to_all | solution.py:1056
  93.7 7.5 %glu_back.3 = (bf16[1024,2560]{1,0:T(8,128)(2,1)S(1)}, f32[1,1024]{1,0:T(1,128)S(1)}, f32[1,512]{1,0:T(1,128)S(1)}, f32[4,32,128]{2,1,0:T(8,128)S(1)}, f32[8,4,5...) custom-call(s32[4]{0:T(128)S(1)} %copy-done.8, ...), custom_call_target="tpu_custom_call" | custom-call | tf_op jit(solution)/shard_map/glu_back/pallas_call | solution.py:64
  101.2 7.8 %all_to_all.45.refs_1_ = f32[8,4,512]{2,1,0:T(4,128)S(1)} all-to-all(f32[8,4,512]{2,1,0:T(4,128)S(1)} %get-tuple-element.161), channel_id=1, replica_groups=mesh['seq'=8,'batch'=4] {'seq'}, dimensions={0} | all-to-all | bytes 131072 | tf_op jit(solution)/shard_map/all_to_all | solution.py:1056
  109.6 5.2 %lift_back.3 = (bf16[1024,512]{1,0:T(8,128)(2,1)S(1)}, f32[32,2,512]{2,1,0:T(2,128)}, f32[1,512]{1,0:T(1,128)S(1)}, f32[1,256]{1,0:T(1,128)S(1)}, bf16[1024,512]...) custom-call(s32[4]{0:T(128)S(1)} %copy-done.8, f32[8,4,512]{2,1,0:T(4,128)S(1)} %get-tuple-element.169.refs_1_, ...), custom_call_target="tpu_custom_call" | custom-call | tf_op jit(solution)/shard_map/lift_back/pallas_call | solution.py:64
  114.8 2.9 %halves0.1 = (bf16[1088,512]{1,0:T(8,128)(2,1)S(1)}, bf16[1088,512]{1,0:T(8,128)(2,1)S(1)}, f32[8,128]{1,0:T(8,128)}) custom-call(s32[4]{0:T(128)S(1)} %copy-done.8, f32[1,512]{1,0:T(1,128)S(1)} %get-tuple-element.176.refs_1_, f32[1,1024]{1,0:T(1,128)S(1)} %get-tuple-element.177.refs_2_, f32[1,512]{1,0:T(1,128)S(1)} %get-tuple-element.178.refs_3_, ...), custom_call_target="tpu_custom_call" | custom-call | tf_op jit(solution)/shard_map/halves0/pallas_call | solution.py:64
  130.3 2.6 %collective-permute-start.13 = (bf16[80,512]{1,0:T(8,128)(2,1)S(1)}, bf16[80,512]{1,0:T(8,128)(2,1)S(1)}, u32[]{:S(2)}, u32[]{:S(2)}) collective-permute-start(bf16[80,512]{1,0:T(8,128)(2,1)S(1)} %get-tuple-element.200.refs_1_), channel_id=1, source_target_pairs={{0,3},{1,2},{2,1},{3,0},{4,7},{5,6},{6,5},{7,4},{8,11},{9,10},{10,... | collective-permute-start | bytes 245768 | tf_op jit(solution)/shard_map/ppermute | solution.py:888
  133.5 4.1 %collective-permute-done.13.refs_4_ = bf16[80,512]{1,0:T(8,128)(2,1)S(1)} collective-permute-done((bf16[80,512]{1,0:T(8,128)(2,1)S(1)}, bf16[80,512]{1,0:T(8,128)(2,1)S(1)}, u32[]{:S(2)}, u32[]{:S(2)}) %collective-permute-start.13) | collective-permute-done | bytes 81952 | tf_op jit(solution)/shard_map/ppermute | solution.py:888
  140.5 2.9 %all-to-all-start.7 = ((f32[32,2,512]{2,1,0:T(2,128)}), f32[32,2,512]{2,1,0:T(2,128)S(1)}, u32[]{:S(2)}, u32[]{:S(2)}) async-start(f32[32,2,512]{2,1,0:T(2,128)} %get-tuple-element.191), calls=%async_computation.7 | async-start | bytes 262144 | tf_op jit(solution)/shard_map/all_to_all | solution.py:1056
  149.3 2.5 %collective-permute-start.15 = (bf16[80,512]{1,0:T(8,128)(2,1)S(1)}, bf16[80,512]{1,0:T(8,128)(2,1)S(1)}, u32[]{:S(2)}, u32[]{:S(2)}) collective-permute-start(bf16[80,512]{1,0:T(8,128)(2,1)S(1)} %get-tuple-element.209), channel_id=1, source_target_pairs={{0,2},{1,3},{2,0},{3,1},{4,6},{5,7},{6,4},{7,5},{8,10},{9,11},{10,... | collective-permute-start | bytes 245768 | tf_op jit(solution)/shard_map/ppermute | solution.py:888
  153.0 5.3 %collective-permute-done.15.refs_3_ = bf16[80,512]{1,0:T(8,128)(2,1)S(1)} collective-permute-done((bf16[80,512]{1,0:T(8,128)(2,1)S(1)}, bf16[80,512]{1,0:T(8,128)(2,1)S(1)}, u32[]{:S(2)}, u32[]{:S(2)}) %collective-permute-start.15) | collective-permute-done | bytes 81952 | tf_op jit(solution)/shard_map/ppermute | solution.py:888
  160.0 2.5 %collective-permute-start.19 = (bf16[80,512]{1,0:T(8,128)(2,1)S(1)}, bf16[80,512]{1,0:T(8,128)(2,1)S(1)}, u32[]{:S(2)}, u32[]{:S(2)}) collective-permute-start(bf16[80,512]{1,0:T(8,128)(2,1)S(1)} %get-tuple-element.212.refs_1_), channel_id=1, source_target_pairs={{0,3},{1,2},{2,1},{3,0},{4,7},{5,6},{6,5},{7,4},{8,11},{9,10},{10,... | collective-permute-start | bytes 245768 | tf_op jit(solution)/shard_map/ppermute | solution.py:888
  173.0 6.4 %collective-permute-done.22.refs_12_ = bf16[272,512]{1,0:T(8,128)(2,1)S(1)} collective-permute-done((bf16[272,512]{1,0:T(8,128)(2,1)S(1)}, bf16[272,512]{1,0:T(8,128)(2,1)S(1)}, u32[]{:S(2)}, u32[]{:S(2)}) %collective-permute-start.22) | collective-permute-done | bytes 278560 | tf_op jit(solution)/shard_map/ppermute | solution.py:888
  179.4 5.5 %collective-permute-done.21.refs_11_ = bf16[272,512]{1,0:T(8,128)(2,1)S(1)} collective-permute-done((bf16[272,512]{1,0:T(8,128)(2,1)S(1)}, bf16[272,512]{1,0:T(8,128)(2,1)S(1)}, u32[]{:S(2)}, u32[]{:S(2)}) %collective-permute-start.21) | collective-permute-done | bytes 278560 | tf_op jit(solution)/shard_map/ppermute | solution.py:888
  186.9 7.2 %results.1 = (f32[2,512,1024]{2,1,0:T(8,128)}, f32[2,512,512]{2,1,0:T(8,128)}, f32[2,512,512]{2,1,0:T(8,128)}, bf16[4,256,512]{2,1,0:T(8,128)(2,1)}, f32[2,512]{...) custom-call(s32[4]{0:T(128)S(1)} %copy-done.8, ...), custom_call_target="tpu_custom_call" | custom-call | flops 7699999744 | bytes 21000000 | tf_op jit(solution)/shard_map/results/pallas_call | solution.py:64
  (102 shorter events, 55.6 us)
Async XLA Ops:
  80.5 11.1 %all-to-all-start.5 = ((f32[32,2,512]{2,1,0:T(2,128)}), f32[32,2,512]{2,1,0:T(2,128)S(1)}, u32[]{:S(2)}, u32[]{:S(2)}) async-start(f32[32,2,512]{2,1,0:T(2,128)} %get-tuple-element.158), calls=%async_computation.5 | async-start | bytes 262144 | tf_op jit(solution)/shard_map/all_to_all | solution.py:1056
  87.4 21.6 %collective-permute-start.1 = (bf16[272,512]{1,0:T(8,128)(2,1)}, bf16[272,512]{1,0:T(8,128)(2,1)S(1)}, u32[]{:S(2)}, u32[]{:S(2)}) collective-permute-start(bf16[272,512]{1,0:T(8,128)(2,1)} %get-tuple-element.166), channel_id=1, source_target_pairs={{0,8},{4,12},{8,0},{12,4},{16,24},{20,28},{24,16},{28,20},{1,9},{5... | collective-permute-start | bytes 835592 | tf_op jit(solution)/shard_map/ppermute | solution.py:888
  88.8 20.2 %collective-permute-start.2 = (bf16[272,512]{1,0:T(8,128)(2,1)S(1)}, bf16[272,512]{1,0:T(8,128)(2,1)S(1)}, u32[]{:S(2)}, u32[]{:S(2)}) collective-permute-start(bf16[272,512]{1,0:T(8,128)(2,1)S(1)} %get-tuple-element.167), channel_id=1, source_target_pairs={{0,16},{4,20},{8,24},{12,28},{16,0},{20,4},{24,8},{28,12},{1,17},{... | collective-permute-start | bytes 835592 | tf_op jit(solution)/shard_map/ppermute | solution.py:888
  90.3 18.7 %collective-permute-start.3 = (bf16[272,512]{1,0:T(8,128)(2,1)S(1)}, bf16[272,512]{1,0:T(8,128)(2,1)S(1)}, u32[]{:S(2)}, u32[]{:S(2)}) collective-permute-start(bf16[272,512]{1,0:T(8,128)(2,1)S(1)} %get-tuple-element.168), channel_id=1, source_target_pairs={{0,24},{4,28},{8,16},{12,20},{16,8},{20,12},{24,0},{28,4},{1,25},{... | collective-permute-start | bytes 835592 | tf_op jit(solution)/shard_map/ppermute | solution.py:888
  120.1 9.5 %collective-permute-start.9 = (bf16[80,512]{1,0:T(8,128)(2,1)S(1)}, bf16[80,512]{1,0:T(8,128)(2,1)S(1)}, u32[]{:S(2)}, u32[]{:S(2)}) collective-permute-start(bf16[80,512]{1,0:T(8,128)(2,1)S(1)} %get-tuple-element.198), channel_id=1, source_target_pairs={{0,2},{1,3},{2,0},{3,1},{4,6},{5,7},{6,4},{7,5},{8,10},{9,11},{10,... | collective-permute-start | bytes 245768 | tf_op jit(solution)/shard_map/ppermute | solution.py:888
  122.6 7.1 %collective-permute-start.10 = (bf16[80,512]{1,0:T(8,128)(2,1)S(1)}, bf16[80,512]{1,0:T(8,128)(2,1)S(1)}, u32[]{:S(2)}, u32[]{:S(2)}) collective-permute-start(bf16[80,512]{1,0:T(8,128)(2,1)S(1)} %get-tuple-element.199), channel_id=1, source_target_pairs={{0,3},{1,2},{2,1},{3,0},{4,7},{5,6},{6,5},{7,4},{8,11},{9,10},{10,... | collective-permute-start | bytes 245768 | tf_op jit(solution)/shard_map/ppermute | solution.py:888
  123.8 23.1 %collective-permute-start.5 = (bf16[272,512]{1,0:T(8,128)(2,1)S(1)}, bf16[272,512]{1,0:T(8,128)(2,1)S(1)}, u32[]{:S(2)}, u32[]{:S(2)}) collective-permute-start(bf16[272,512]{1,0:T(8,128)(2,1)S(1)} %get-tuple-element.193), channel_id=1, source_target_pairs={{0,8},{4,12},{8,0},{12,4},{16,24},{20,28},{24,16},{28,20},{1,9},{5... | collective-permute-start | bytes 835592 | tf_op jit(solution)/shard_map/ppermute | solution.py:888
  124.5 22.5 %collective-permute-start.6 = (bf16[272,512]{1,0:T(8,128)(2,1)S(1)}, bf16[272,512]{1,0:T(8,128)(2,1)S(1)}, u32[]{:S(2)}, u32[]{:S(2)}) collective-permute-start(bf16[272,512]{1,0:T(8,128)(2,1)S(1)} %get-tuple-element.194), channel_id=1, source_target_pairs={{0,16},{4,20},{8,24},{12,28},{16,0},{20,4},{24,8},{28,12},{1,17},{... | collective-permute-start | bytes 835592 | tf_op jit(solution)/shard_map/ppermute | solution.py:888
  125.0 21.9 %collective-permute-start.7 = (bf16[272,512]{1,0:T(8,128)(2,1)S(1)}, bf16[272,512]{1,0:T(8,128)(2,1)S(1)}, u32[]{:S(2)}, u32[]{:S(2)}) collective-permute-start(bf16[272,512]{1,0:T(8,128)(2,1)S(1)} %get-tuple-element.195), channel_id=1, source_target_pairs={{0,24},{4,28},{8,16},{12,20},{16,8},{20,12},{24,0},{28,4},{1,25},{... | collective-permute-start | bytes 835592 | tf_op jit(solution)/shard_map/ppermute | solution.py:888
  130.3 7.3 %collective-permute-start.13 = (bf16[80,512]{1,0:T(8,128)(2,1)S(1)}, bf16[80,512]{1,0:T(8,128)(2,1)S(1)}, u32[]{:S(2)}, u32[]{:S(2)}) collective-permute-start(bf16[80,512]{1,0:T(8,128)(2,1)S(1)} %get-tuple-element.200.refs_1_), channel_id=1, source_target_pairs={{0,3},{1,2},{2,1},{3,0},{4,7},{5,6},{6,5},{7,4},{8,11},{9,10},{10,... | collective-permute-start | bytes 245768 | tf_op jit(solution)/shard_map/ppermute | solution.py:888
  132.9 10.5 %collective-permute-start.12 = (bf16[80,512]{1,0:T(8,128)(2,1)S(1)}, bf16[80,512]{1,0:T(8,128)(2,1)S(1)}, u32[]{:S(2)}, u32[]{:S(2)}) collective-permute-start(bf16[80,512]{1,0:T(8,128)(2,1)S(1)} %get-tuple-element.200.refs_1_), channel_id=1, source_target_pairs={{0,2},{1,3},{2,0},{3,1},{4,6},{5,7},{6,4},{7,5},{8,10},{9,11},{10,... | collective-permute-start | bytes 245768 | tf_op jit(solution)/shard_map/ppermute | solution.py:888
  140.5 18.3 %all-to-all-start.7 = ((f32[32,2,512]{2,1,0:T(2,128)}), f32[32,2,512]{2,1,0:T(2,128)S(1)}, u32[]{:S(2)}, u32[]{:S(2)}) async-start(f32[32,2,512]{2,1,0:T(2,128)} %get-tuple-element.191), calls=%async_computation.7 | async-start | bytes 262144 | tf_op jit(solution)/shard_map/all_to_all | solution.py:1056
  144.0 18.5 %collective-permute-start.29 = (bf16[272,512]{1,0:T(8,128)(2,1)S(1)}, bf16[272,512]{1,0:T(8,128)(2,1)S(1)}, u32[]{:S(2)}, u32[]{:S(2)}) collective-permute-start(bf16[272,512]{1,0:T(8,128)(2,1)S(1)} %get-tuple-element.214.refs_17_), channel_id=1, source_target_pairs={{0,24},{4,28},{8,16},{12,20},{16,8},{20,12},{24,0},{28,4},{1,25},{... | collective-permute-start | bytes 835592 | tf_op jit(solution)/shard_map/ppermute | solution.py:888
  146.4 16.1 %collective-permute-start.28 = (bf16[272,512]{1,0:T(8,128)(2,1)S(1)}, bf16[272,512]{1,0:T(8,128)(2,1)S(1)}, u32[]{:S(2)}, u32[]{:S(2)}) collective-permute-start(bf16[272,512]{1,0:T(8,128)(2,1)S(1)} %get-tuple-element.214.refs_17_), channel_id=1, source_target_pairs={{0,16},{4,20},{8,24},{12,28},{16,0},{20,4},{24,8},{28,12},{1,17},{... | collective-permute-start | bytes 835592 | tf_op jit(solution)/shard_map/ppermute | solution.py:888
  149.3 8.9 %collective-permute-start.15 = (bf16[80,512]{1,0:T(8,128)(2,1)S(1)}, bf16[80,512]{1,0:T(8,128)(2,1)S(1)}, u32[]{:S(2)}, u32[]{:S(2)}) collective-permute-start(bf16[80,512]{1,0:T(8,128)(2,1)S(1)} %get-tuple-element.209), channel_id=1, source_target_pairs={{0,2},{1,3},{2,0},{3,1},{4,6},{5,7},{6,4},{7,5},{8,10},{9,11},{10,... | collective-permute-start | bytes 245768 | tf_op jit(solution)/shard_map/ppermute | solution.py:888
  151.8 7.6 %collective-permute-start.16 = (bf16[80,512]{1,0:T(8,128)(2,1)S(1)}, bf16[80,512]{1,0:T(8,128)(2,1)S(1)}, u32[]{:S(2)}, u32[]{:S(2)}) collective-permute-start(bf16[80,512]{1,0:T(8,128)(2,1)S(1)} %get-tuple-element.210), channel_id=1, source_target_pairs={{0,3},{1,2},{2,1},{3,0},{4,7},{5,6},{6,5},{7,4},{8,11},{9,10},{10,... | collective-permute-start | bytes 245768 | tf_op jit(solution)/shard_map/ppermute | solution.py:888
  153.0 18.2 %collective-permute-start.30 = (bf16[272,512]{1,0:T(8,128)(2,1)S(1)}, bf16[272,512]{1,0:T(8,128)(2,1)S(1)}, u32[]{:S(2)}, u32[]{:S(2)}) collective-permute-start(bf16[272,512]{1,0:T(8,128)(2,1)S(1)} %get-tuple-element.214.refs_17_), channel_id=1, source_target_pairs={{0,4},{4,0},{8,12},{12,8},{16,20},{20,16},{24,28},{28,24},{1,5},{5... | collective-permute-start | bytes 835592 | tf_op jit(solution)/shard_map/ppermute | solution.py:888
  158.2 13.6 %collective-permute-start.27 = (bf16[272,512]{1,0:T(8,128)(2,1)S(1)}, bf16[272,512]{1,0:T(8,128)(2,1)S(1)}, u32[]{:S(2)}, u32[]{:S(2)}) collective-permute-start(bf16[272,512]{1,0:T(8,128)(2,1)S(1)} %get-tuple-element.214.refs_17_), channel_id=1, source_target_pairs={{0,8},{4,12},{8,0},{12,4},{16,24},{20,28},{24,16},{28,20},{1,9},{5... | collective-permute-start | bytes 835592 | tf_op jit(solution)/shard_map/ppermute | solution.py:888
  160.0 6.5 %collective-permute-start.19 = (bf16[80,512]{1,0:T(8,128)(2,1)S(1)}, bf16[80,512]{1,0:T(8,128)(2,1)S(1)}, u32[]{:S(2)}, u32[]{:S(2)}) collective-permute-start(bf16[80,512]{1,0:T(8,128)(2,1)S(1)} %get-tuple-element.212.refs_1_), channel_id=1, source_target_pairs={{0,3},{1,2},{2,1},{3,0},{4,7},{5,6},{6,5},{7,4},{8,11},{9,10},{10,... | collective-permute-start | bytes 245768 | tf_op jit(solution)/shard_map/ppermute | solution.py:888
  168.9 10.5 %collective-permute-start.22 = (bf16[272,512]{1,0:T(8,128)(2,1)S(1)}, bf16[272,512]{1,0:T(8,128)(2,1)S(1)}, u32[]{:S(2)}, u32[]{:S(2)}) collective-permute-start(bf16[272,512]{1,0:T(8,128)(2,1)S(1)} %get-tuple-element.213.refs_9_), channel_id=1, source_target_pairs={{0,24},{4,28},{8,16},{12,20},{16,8},{20,12},{24,0},{28,4},{1,25},{... | collective-permute-start | bytes 835592 | tf_op jit(solution)/shard_map/ppermute | solution.py:888
  171.2 13.7 %collective-permute-start.21 = (bf16[272,512]{1,0:T(8,128)(2,1)S(1)}, bf16[272,512]{1,0:T(8,128)(2,1)S(1)}, u32[]{:S(2)}, u32[]{:S(2)}) collective-permute-start(bf16[272,512]{1,0:T(8,128)(2,1)S(1)} %get-tuple-element.213.refs_9_), channel_id=1, source_target_pairs={{0,16},{4,20},{8,24},{12,28},{16,0},{20,4},{24,8},{28,12},{1,17},{... | collective-permute-start | bytes 835592 | tf_op jit(solution)/shard_map/ppermute | solution.py:888
  171.8 13.2 %collective-permute-start.20 = (bf16[272,512]{1,0:T(8,128)(2,1)S(1)}, bf16[272,512]{1,0:T(8,128)(2,1)S(1)}, u32[]{:S(2)}, u32[]{:S(2)}) collective-permute-start(bf16[272,512]{1,0:T(8,128)(2,1)S(1)} %get-tuple-element.213.refs_9_), channel_id=1, source_target_pairs={{0,8},{4,12},{8,0},{12,4},{16,24},{20,28},{24,16},{28,20},{1,9},{5... | collective-permute-start | bytes 835592 | tf_op jit(solution)/shard_map/ppermute | solution.py:888
  172.5 13.0 %collective-permute-start.31 = (bf16[272,512]{1,0:T(8,128)(2,1)S(1)}, bf16[272,512]{1,0:T(8,128)(2,1)S(1)}, u32[]{:S(2)}, u32[]{:S(2)}) collective-permute-start(bf16[272,512]{1,0:T(8,128)(2,1)S(1)} %collective-permute-done.27.refs_18_), channel_id=1, source_target_pairs={{0,4},{4,0},{8,12},{12,8},{16,20},{20,16},{24,28},{28,24},{1,5},{5... | collective-permute-start | bytes 835592 | tf_op jit(solution)/shard_map/ppermute | solution.py:888
  172.5 12.9 %collective-permute-start.23 = (bf16[272,512]{1,0:T(8,128)(2,1)S(1)}, bf16[272,512]{1,0:T(8,128)(2,1)S(1)}, u32[]{:S(2)}, u32[]{:S(2)}) collective-permute-start(bf16[272,512]{1,0:T(8,128)(2,1)S(1)} %get-tuple-element.213.refs_9_), channel_id=1, source_target_pairs={{0,4},{4,0},{8,12},{12,8},{16,20},{20,16},{24,28},{28,24},{1,5},{5... | collective-permute-start | bytes 835592 | tf_op jit(solution)/shard_map/ppermute | solution.py:888
  (24 other events, 188.6 us)

commit v4 on v3

--- a/solution.py
+++ b/solution.py
@@ -13,6 +13,7 @@
 
 CHUNKS = 8
 BLOCKS = 4
+BACK_BLOCKS = 2
 PARTS = 1
 EXTRA = 16
 LANES = 128
@@ -353,9 +354,9 @@
     return drive
 
 
-def blocks_of(rows, group, reverse):
-    size = rows // BLOCKS
-    for block in order(BLOCKS, reverse):
+def blocks_of(rows, group, reverse, blocks=BLOCKS):
+    size = rows // blocks
+    for block in order(blocks, reverse):
         yield block, block * (size // group), slice(block * size, (block + 1) * size)
 
 
@@ -529,7 +530,7 @@
         )
         slope_ref, gate_ref, gate_slope_ref = pack.views(slopes_ref, "slope", "gate", "gate_slope")
     group = ends_ref.shape[1]
-    size = rows // BLOCKS
+    size = rows // BACK_BLOCKS
     steps = size // group
     where = Where(info_ref, seqs, rows // seqs)
     if k == 1:
@@ -537,13 +538,13 @@
         shuffle_rows(wide_ref, start_ref)
     else:
         copies = {}
-        for block, _, now in blocks_of(rows, group, reverse):
+        for block, _, now in blocks_of(rows, group, reverse, BACK_BLOCKS):
             lanes = slice(0, 3 * width)
             copies[block] = copy_parts(kept_ref.at[now, lanes], slopes_ref.at[now, :], sems.at[0, block])
             copies[block] += copy_parts(normed_in.at[now, :], normed_ref.at[now, :], sems.at[1, block])
         weights = copy_parts(glu_in.at[k], glu_ref, weight_sems.at[0])
         weights += copy_parts(mix_in.at[k], mix_ref, weight_sems.at[1])
-        for n, block in enumerate(order(BLOCKS, reverse)):
+        for n, block in enumerate(order(BACK_BLOCKS, reverse)):
             begin(copies[block])
             if n == 0:
                 begin(weights)
@@ -559,7 +560,7 @@
     ends_ref[...] = jnp.zeros_like(ends_ref)
     bias_grad = jnp.zeros((1, 2 * width), f32)
     skip_grad = jnp.zeros((1, width), f32)
-    for block, first, now in blocks_of(rows, group, reverse):
+    for block, first, now in blocks_of(rows, group, reverse, BACK_BLOCKS):
         valid = wide(valid_rows(left, first, steps), width)
         if k == 1:
             back = wide_ref[first : first + steps].reshape(size, width) * valid
@@ -575,7 +576,7 @@
         back_projected = jnp.concatenate([value_back, gate_back], axis=1)
         projected_ref[now, :] = back_projected
         bias_grad += jnp.sum(back_projected.astype(f32), axis=0, keepdims=True)
-        if k == 0 and block == BLOCKS - 1:
+        if k == 0 and block == BACK_BLOCKS - 1:
             finished(weights)
         back_activated = dot_t(back_projected, glu_ref[...])
         back_mixed = (slope_ref[now, :].astype(f32) * back_activated).astype(bf16)
@@ -615,7 +616,7 @@
             pltpu.VMEM((rows, 3 * width), bf16),
             pltpu.VMEM((width, 2 * width), bf16),
             pltpu.VMEM((2 * states, width), bf16),
-            pltpu.SemaphoreType.DMA((2, BLOCKS, 1)),
+            pltpu.SemaphoreType.DMA((2, BACK_BLOCKS, 1)),
             pltpu.SemaphoreType.DMA((2, 1)),
         ]
     scratch += Powers.scratch(seqs, seq_devices, states, False)
@@ -648,7 +649,7 @@
     rows, width = normed_ref.shape
     group = ends_ref.shape[1]
     seqs = parts_ref.shape[1]
-    steps = rows // BLOCKS // group
+    steps = rows // BACK_BLOCKS // group
     states = decay_ref.shape[1]
     where = Where(info_ref, seqs, rows // seqs)
     powers = Powers(k, True, where, decay_ref, phase_ref, *tables)
@@ -662,7 +663,7 @@
     gain_sum = jnp.zeros((1, width), f32)
     shift_sum = jnp.zeros((1, width), f32)
     shift = 1 if reverse else -1
-    for _, first, now in blocks_of(rows, group, reverse):
+    for _, first, now in blocks_of(rows, group, reverse, BACK_BLOCKS):
         moving = [left > first + t + shift for t in range(steps)]
         valid = [left > first + t for t in range(steps)]
         dh = dh_ref[now, :].astype(f32)
@@ -728,7 +729,7 @@
         outs.append(moved((rows, width), bf16))
     scratch = [
         pltpu.VMEM(table, f32),
-        pltpu.VMEM((rows // BLOCKS, states), f32),
+        pltpu.VMEM((rows // BACK_BLOCKS, states), f32),
         pltpu.VMEM(acc, f32),
         pltpu.VMEM((table[1], states), f32),
         pltpu.VMEM((table[1], states // 2), f32),
@@ -1166,14 +1167,14 @@
     got0 = trade(send, "seq", 1)
     out1 = cut(info, pieces1, EXTRA, (out.tick,))
     out0 = split(info, ((*shares, extra),), [keep0, got0], True, (out1.tick,))
-    (sums,) = gate(info, [sums], (out0.tick,))
+    sum1 = sum_of(info, sent(out1, "batch", z), (out0.tick,))
+    (sums,) = gate(info, [sums], (sum1.tick,))
     sums = to_all(sums, both)
-    sum1 = sum_of(info, sent(out1, "batch", z), (out0.tick,))
     (own1,) = out = join(info, to_others(sum1[0], "batch", z), EXTRA, (sum1.tick,))
     out0 = cut(info, sent(out0, "seq", xy), EXTRA, (out.tick,))
-    (sums,) = out = norms(info, sums, (out0.tick,))
-    sum0 = sum_of(info, sent(out0, "batch", z), (out.tick,))
-    (own0,) = join(info, to_others(sum0[0], "batch", z), EXTRA)
+    sum0 = sum_of(info, sent(out0, "batch", z))
+    (own0,) = out = join(info, to_others(sum0[0], "batch", z), EXTRA)
+    (sums,) = norms(info, sums, (out.tick,))
     pieces = []
     for own in (own0, own1):
         total = to_others(own, "seq", xy)

time: 195 us -> 190 us (0.974)
  waiting for transfers between devices: 30.3 us -> 27.6 us
  Pallas kernels: 64 us -> 61.6 us
    ppermute x34, waiting for transfers between devices: 29.7 us -> 26.5 us  [trade(): return lax.ppermute(x, axis, [(i, i ^ mask) for i in range(size)])]
    pallas_call x24, Pallas kernels: 64 us -> 61.6 us  [run(): pl.pallas_call(ticking, in_specs=[in_smem] + specs + [in_hbm] * len(after...]
  transfers between devices with their start and end apart: 36 -> 36, of which waited for: 11 -> 13; matrix products, arithmetic and copies ran while one was open for 0% -> 0% of each run, Pallas kernels for 9% -> 9%
where the time goes in v4:
time: 190 us; the launch traced here: 189 us
  Pallas kernels  61.6 us (32%)
  blocking collectives  56.1 us (30%)
  starting transfers between devices  39.9 us (21%)
  waiting for transfers between devices  27.6 us (15%)
  local copies, waits for them, and re-layouts  2.9 us (2%)
    pallas_call x24, Pallas kernels, run(): pl.pallas_call(ticking, in_specs=[in_smem] + specs + [in_hbm] * len(after...  61.6 us
    all_to_all x6, blocking collectives, to_all(): return lax.all_to_all(x, axes, split_axis=0, concat_axis=0, tiled=True)  56.1 us
    ppermute x34, starting transfers between devices, trade(): return lax.ppermute(x, axis, [(i, i ^ mask) for i in range(size)])  34.5 us
    ppermute x34, waiting for transfers between devices, trade(): return lax.ppermute(x, axis, [(i, i ^ mask) for i in range(size)])  26.5 us
    all_to_all x2, starting transfers between devices, to_all(): return lax.all_to_all(x, axes, split_axis=0, concat_axis=0, tiled=True)  5.39 us
  transfers between devices with their start and end apart: 36, of which 13 were waited for; matrix products, arithmetic and copies ran while one was open for 0% of the time, Pallas kernels for 9%

profile of v4, /device:TPU:0, one launch (start us, length us, event | category | flops | bytes accessed | tf_op | source)
XLA Modules:
  0.0 189.3 jit_solution(1355043827583611496)
XLA Ops:
  3.6 16.0 %all_to_all.40.refs_1_ = f32[32,2,640]{2,1,0:T(2,128)S(1)} all-to-all(f32[32,2,640]{2,1,0:T(2,128)S(1)} %get-tuple-element.117), channel_id=1, replica_groups=mesh['seq'=8,'batch'=4] {'seq','batch'}, dimensions={0} | all-to-all | bytes 327680 | tf_op jit(solution)/shard_map/all_to_all | solution.py:1057
  22.0 7.4 %all_to_all.41.refs_1_ = f32[8,4,512]{2,1,0:T(4,128)S(1)} all-to-all(f32[8,4,512]{2,1,0:T(4,128)S(1)} %get-tuple-element.120), channel_id=1, replica_groups=mesh['seq'=8,'batch'=4] {'seq'}, dimensions={0} | all-to-all | bytes 131072 | tf_op jit(solution)/shard_map/all_to_all | solution.py:1057
  29.4 6.3 %mix.2 = (f32[1024,512]{1,0:T(8,128)S(1)}, f32[32,2,512]{2,1,0:T(2,128)S(1)}, bf16[1024,2560]{1,0:T(8,128)(2,1)}, bf16[512,512]{1,0:T(8,128)(2,1)S(1)}, bf16[1024,512]{1,0:T(8,128)(2,1)}, /*index=5*/f32[8,128]{1,0:T(8,128)}) custom-call(s32[4]{0:T(128)S(1)} %copy-done.8, f32[8,4,512]{2,1,0:T(4,128)S(1)} %all_to_all.41.refs_1_, f32[2,512]{1,0:T(2,128)S(1)} %copy-done.9, ...), custom_call_target="tpu_custom_call" | custom-call | tf_op jit(solution)/shard_map/mix/pallas_call | solution.py:65
  35.7 10.1 %all_to_all.42.refs_1_ = f32[32,2,512]{2,1,0:T(2,128)S(1)} all-to-all(f32[32,2,512]{2,1,0:T(2,128)S(1)} %get-tuple-element.127), channel_id=1, replica_groups=mesh['seq'=8,'batch'=4] {'seq','batch'}, dimensions={0} | all-to-all | bytes 262144 | tf_op jit(solution)/shard_map/all_to_all | solution.py:1057
  47.8 7.4 %all_to_all.43.refs_1_ = f32[8,4,512]{2,1,0:T(4,128)S(1)} all-to-all(f32[8,4,512]{2,1,0:T(4,128)S(1)} %get-tuple-element.131), channel_id=1, replica_groups=mesh['seq'=8,'batch'=4] {'seq'}, dimensions={0} | all-to-all | bytes 131072 | tf_op jit(solution)/shard_map/all_to_all | solution.py:1057
  55.2 5.2 %mix.3 = (bf16[1024,512]{1,0:T(8,128)(2,1)S(1)}, bf16[1024,512]{1,0:T(8,128)(2,1)S(1)}, bf16[1024,512]{1,0:T(8,128)(2,1)S(1)}, bf16[1024,512]{1,0:T(8,128)(2,1)S...) custom-call(s32[4]{0:T(128)S(1)} %copy-done.8, ...), custom_call_target="tpu_custom_call" | custom-call | tf_op jit(solution)/shard_map/mix/pallas_call | solution.py:65
  60.5 3.4 %glu_back.2 = (bf16[1024,2560]{1,0:T(8,128)(2,1)S(1)}, f32[1,1024]{1,0:T(1,128)S(1)}, f32[1,512]{1,0:T(1,128)S(1)}, f32[4,32,128]{2,1,0:T(8,128)S(1)}, f32[8,4,5...) custom-call(s32[4]{0:T(128)S(1)} %copy-done.8, ...), custom_call_target="tpu_custom_call" | custom-call | tf_op jit(solution)/shard_map/glu_back/pallas_call | solution.py:65
  63.9 7.4 %all_to_all.44.refs_1_ = f32[8,4,512]{2,1,0:T(4,128)S(1)} all-to-all(f32[8,4,512]{2,1,0:T(4,128)S(1)} %get-tuple-element.145), channel_id=1, replica_groups=mesh['seq'=8,'batch'=4] {'seq'}, dimensions={0} | all-to-all | bytes 131072 | tf_op jit(solution)/shard_map/all_to_all | solution.py:1057
  71.3 3.9 %lift_back.2 = (bf16[1024,2048]{1,0:T(8,128)(2,1)S(1)}, f32[32,2,512]{2,1,0:T(2,128)}, f32[1,512]{1,0:T(1,128)S(1)}, f32[1,256]{1,0:T(1,128)S(1)}, f32[8,128]{1,0:T(8,128)}) custom-call(s32[4]{0:T(128)S(1)} %copy-done.8, f32[8,4,512]{2,1,0:T(4,128)S(1)} %all_to_all.44.refs_1_, f32[8,512]{1,0:T(8,128)S(1)} %get-tuple-element.146.refs_2_.refs_4_, ...), custom_call_target="tpu_custom_call" | custom-call | tf_op jit(solution)/shard_map/lift_back/pallas_call | solution.py:65
  75.2 3.9 %halves1.1 = (bf16[1088,512]{1,0:T(8,128)(2,1)S(1)}, bf16[1088,512]{1,0:T(8,128)(2,1)}, f32[8,128]{1,0:T(8,128)}) custom-call(s32[4]{0:T(128)S(1)} %copy-done.8, f32[1,512]{1,0:T(1,128)S(1)} %get-tuple-element.143.refs_1_, f32[1,1024]{1,0:T(1,128)S(1)} %get-tuple-element.144.refs_2_, f32[1,512]{1,0:T(1,128)S(1)} %get-tuple-element.151.refs_3_, ...), custom_call_target="tpu_custom_call" | custom-call | tf_op jit(solution)/shard_map/halves1/pallas_call | solution.py:65
  79.1 2.8 %all-to-all-start.5 = ((f32[32,2,512]{2,1,0:T(2,128)}), f32[32,2,512]{2,1,0:T(2,128)S(1)}, u32[]{:S(2)}, u32[]{:S(2)}) async-start(f32[32,2,512]{2,1,0:T(2,128)} %get-tuple-element.157), calls=%async_computation.5 | async-start | bytes 262144 | tf_op jit(solution)/shard_map/all_to_all | solution.py:1057
  92.4 6.5 %glu_back.3 = (bf16[1024,2560]{1,0:T(8,128)(2,1)S(1)}, f32[1,1024]{1,0:T(1,128)S(1)}, f32[1,512]{1,0:T(1,128)S(1)}, f32[4,32,128]{2,1,0:T(8,128)S(1)}, f32[8,4,5...) custom-call(s32[4]{0:T(128)S(1)} %copy-done.8, ...), custom_call_target="tpu_custom_call" | custom-call | tf_op jit(solution)/shard_map/glu_back/pallas_call | solution.py:65
  98.9 7.8 %all_to_all.45.refs_1_ = f32[8,4,512]{2,1,0:T(4,128)S(1)} all-to-all(f32[8,4,512]{2,1,0:T(4,128)S(1)} %get-tuple-element.160), channel_id=1, replica_groups=mesh['seq'=8,'batch'=4] {'seq'}, dimensions={0} | all-to-all | bytes 131072 | tf_op jit(solution)/shard_map/all_to_all | solution.py:1057
  107.2 4.7 %lift_back.3 = (bf16[1024,512]{1,0:T(8,128)(2,1)S(1)}, f32[32,2,512]{2,1,0:T(2,128)}, f32[1,512]{1,0:T(1,128)S(1)}, f32[1,256]{1,0:T(1,128)S(1)}, bf16[1024,512]...) custom-call(s32[4]{0:T(128)S(1)} %copy-done.8, f32[8,4,512]{2,1,0:T(4,128)S(1)} %get-tuple-element.168.refs_1_, ...), custom_call_target="tpu_custom_call" | custom-call | tf_op jit(solution)/shard_map/lift_back/pallas_call | solution.py:65
  112.0 2.9 %halves0.1 = (bf16[1088,512]{1,0:T(8,128)(2,1)S(1)}, bf16[1088,512]{1,0:T(8,128)(2,1)S(1)}, f32[8,128]{1,0:T(8,128)}) custom-call(s32[4]{0:T(128)S(1)} %copy-done.8, f32[1,512]{1,0:T(1,128)S(1)} %get-tuple-element.179.refs_1_, f32[1,1024]{1,0:T(1,128)S(1)} %get-tuple-element.180.refs_2_, f32[1,512]{1,0:T(1,128)S(1)} %get-tuple-element.181.refs_3_, ...), custom_call_target="tpu_custom_call" | custom-call | tf_op jit(solution)/shard_map/halves0/pallas_call | solution.py:65
  117.3 2.5 %collective-permute-start.5 = (bf16[80,512]{1,0:T(8,128)(2,1)S(1)}, bf16[80,512]{1,0:T(8,128)(2,1)S(1)}, u32[]{:S(2)}, u32[]{:S(2)}) collective-permute-start(bf16[80,512]{1,0:T(8,128)(2,1)S(1)} %get-tuple-element.188), channel_id=1, source_target_pairs={{0,2},{1,3},{2,0},{3,1},{4,6},{5,7},{6,4},{7,5},{8,10},{9,11},{10,... | collective-permute-start | bytes 245768 | tf_op jit(solution)/shard_map/ppermute | solution.py:889
  127.4 2.7 %collective-permute-start.13 = (bf16[80,512]{1,0:T(8,128)(2,1)S(1)}, bf16[80,512]{1,0:T(8,128)(2,1)S(1)}, u32[]{:S(2)}, u32[]{:S(2)}) collective-permute-start(bf16[80,512]{1,0:T(8,128)(2,1)S(1)} %get-tuple-element.200.refs_1_), channel_id=1, source_target_pairs={{0,3},{1,2},{2,1},{3,0},{4,7},{5,6},{6,5},{7,4},{8,11},{9,10},{10,... | collective-permute-start | bytes 245768 | tf_op jit(solution)/shard_map/ppermute | solution.py:889
  130.7 4.0 %collective-permute-done.13.refs_4_ = bf16[80,512]{1,0:T(8,128)(2,1)S(1)} collective-permute-done((bf16[80,512]{1,0:T(8,128)(2,1)S(1)}, bf16[80,512]{1,0:T(8,128)(2,1)S(1)}, u32[]{:S(2)}, u32[]{:S(2)}) %collective-permute-start.13) | collective-permute-done | bytes 81952 | tf_op jit(solution)/shard_map/ppermute | solution.py:889
  134.7 2.5 %collective-permute-start.11 = (bf16[80,512]{1,0:T(8,128)(2,1)S(1)}, bf16[80,512]{1,0:T(8,128)(2,1)S(1)}, u32[]{:S(2)}, u32[]{:S(2)}) collective-permute-start(bf16[80,512]{1,0:T(8,128)(2,1)S(1)} %get-tuple-element.200.refs_1_), channel_id=1, source_target_pairs={{0,1},{1,0},{2,3},{3,2},{4,5},{5,4},{6,7},{7,6},{8,9},{9,8},{10,11... | collective-permute-start | bytes 245768 | tf_op jit(solution)/shard_map/ppermute | solution.py:889
  147.6 4.5 %collective-permute-done.15.refs_3_ = bf16[80,512]{1,0:T(8,128)(2,1)S(1)} collective-permute-done((bf16[80,512]{1,0:T(8,128)(2,1)S(1)}, bf16[80,512]{1,0:T(8,128)(2,1)S(1)}, u32[]{:S(2)}, u32[]{:S(2)}) %collective-permute-start.15) | collective-permute-done | bytes 81952 | tf_op jit(solution)/shard_map/ppermute | solution.py:889
  167.0 2.6 %all-to-all-start.7 = ((f32[32,2,512]{2,1,0:T(2,128)}), f32[32,2,512]{2,1,0:T(2,128)S(1)}, u32[]{:S(2)}, u32[]{:S(2)}) async-start(f32[32,2,512]{2,1,0:T(2,128)} %get-tuple-element.195), calls=%async_computation.7 | async-start | bytes 262144 | tf_op jit(solution)/shard_map/all_to_all | solution.py:1057
  170.2 3.2 %collective-permute-done.22.refs_12_ = bf16[272,512]{1,0:T(8,128)(2,1)S(1)} collective-permute-done((bf16[272,512]{1,0:T(8,128)(2,1)S(1)}, bf16[272,512]{1,0:T(8,128)(2,1)S(1)}, u32[]{:S(2)}, u32[]{:S(2)}) %collective-permute-start.22) | collective-permute-done | bytes 278560 | tf_op jit(solution)/shard_map/ppermute | solution.py:889
  173.4 6.0 %collective-permute-done.21.refs_11_ = bf16[272,512]{1,0:T(8,128)(2,1)S(1)} collective-permute-done((bf16[272,512]{1,0:T(8,128)(2,1)S(1)}, bf16[272,512]{1,0:T(8,128)(2,1)S(1)}, u32[]{:S(2)}, u32[]{:S(2)}) %collective-permute-start.21) | collective-permute-done | bytes 278560 | tf_op jit(solution)/shard_map/ppermute | solution.py:889
  181.5 7.6 %results.1 = (f32[2,512,1024]{2,1,0:T(8,128)}, f32[2,512,512]{2,1,0:T(8,128)}, f32[2,512,512]{2,1,0:T(8,128)}, bf16[4,256,512]{2,1,0:T(8,128)(2,1)}, f32[2,512]{...) custom-call(s32[4]{0:T(128)S(1)} %copy-done.8, ...), custom_call_target="tpu_custom_call" | custom-call | flops 7699999744 | bytes 21000000 | tf_op jit(solution)/shard_map/results/pallas_call | solution.py:65
  (102 shorter events, 56.7 us)
Async XLA Ops:
  79.1 11.1 %all-to-all-start.5 = ((f32[32,2,512]{2,1,0:T(2,128)}), f32[32,2,512]{2,1,0:T(2,128)S(1)}, u32[]{:S(2)}, u32[]{:S(2)}) async-start(f32[32,2,512]{2,1,0:T(2,128)} %get-tuple-element.157), calls=%async_computation.5 | async-start | bytes 262144 | tf_op jit(solution)/shard_map/all_to_all | solution.py:1057
  86.1 20.6 %collective-permute-start.1 = (bf16[272,512]{1,0:T(8,128)(2,1)}, bf16[272,512]{1,0:T(8,128)(2,1)S(1)}, u32[]{:S(2)}, u32[]{:S(2)}) collective-permute-start(bf16[272,512]{1,0:T(8,128)(2,1)} %get-tuple-element.165), channel_id=1, source_target_pairs={{0,8},{4,12},{8,0},{12,4},{16,24},{20,28},{24,16},{28,20},{1,9},{5... | collective-permute-start | bytes 835592 | tf_op jit(solution)/shard_map/ppermute | solution.py:889
  87.5 19.2 %collective-permute-start.2 = (bf16[272,512]{1,0:T(8,128)(2,1)S(1)}, bf16[272,512]{1,0:T(8,128)(2,1)S(1)}, u32[]{:S(2)}, u32[]{:S(2)}) collective-permute-start(bf16[272,512]{1,0:T(8,128)(2,1)S(1)} %get-tuple-element.166), channel_id=1, source_target_pairs={{0,16},{4,20},{8,24},{12,28},{16,0},{20,4},{24,8},{28,12},{1,17},{... | collective-permute-start | bytes 835592 | tf_op jit(solution)/shard_map/ppermute | solution.py:889
  89.0 17.7 %collective-permute-start.3 = (bf16[272,512]{1,0:T(8,128)(2,1)S(1)}, bf16[272,512]{1,0:T(8,128)(2,1)S(1)}, u32[]{:S(2)}, u32[]{:S(2)}) collective-permute-start(bf16[272,512]{1,0:T(8,128)(2,1)S(1)} %get-tuple-element.167), channel_id=1, source_target_pairs={{0,24},{4,28},{8,16},{12,20},{16,8},{20,12},{24,0},{28,4},{1,25},{... | collective-permute-start | bytes 835592 | tf_op jit(solution)/shard_map/ppermute | solution.py:889
  117.3 9.5 %collective-permute-start.5 = (bf16[80,512]{1,0:T(8,128)(2,1)S(1)}, bf16[80,512]{1,0:T(8,128)(2,1)S(1)}, u32[]{:S(2)}, u32[]{:S(2)}) collective-permute-start(bf16[80,512]{1,0:T(8,128)(2,1)S(1)} %get-tuple-element.188), channel_id=1, source_target_pairs={{0,2},{1,3},{2,0},{3,1},{4,6},{5,7},{6,4},{7,5},{8,10},{9,11},{10,... | collective-permute-start | bytes 245768 | tf_op jit(solution)/shard_map/ppermute | solution.py:889
  121.0 21.3 %collective-permute-start.8 = (bf16[272,512]{1,0:T(8,128)(2,1)S(1)}, bf16[272,512]{1,0:T(8,128)(2,1)S(1)}, u32[]{:S(2)}, u32[]{:S(2)}) collective-permute-start(bf16[272,512]{1,0:T(8,128)(2,1)S(1)} %get-tuple-element.197), channel_id=1, source_target_pairs={{0,8},{4,12},{8,0},{12,4},{16,24},{20,28},{24,16},{28,20},{1,9},{5... | collective-permute-start | bytes 835592 | tf_op jit(solution)/shard_map/ppermute | solution.py:889
  121.7 20.7 %collective-permute-start.9 = (bf16[272,512]{1,0:T(8,128)(2,1)S(1)}, bf16[272,512]{1,0:T(8,128)(2,1)S(1)}, u32[]{:S(2)}, u32[]{:S(2)}) collective-permute-start(bf16[272,512]{1,0:T(8,128)(2,1)S(1)} %get-tuple-element.198), channel_id=1, source_target_pairs={{0,16},{4,20},{8,24},{12,28},{16,0},{20,4},{24,8},{28,12},{1,17},{... | collective-permute-start | bytes 835592 | tf_op jit(solution)/shard_map/ppermute | solution.py:889
  122.2 20.1 %collective-permute-start.10 = (bf16[272,512]{1,0:T(8,128)(2,1)S(1)}, bf16[272,512]{1,0:T(8,128)(2,1)S(1)}, u32[]{:S(2)}, u32[]{:S(2)}) collective-permute-start(bf16[272,512]{1,0:T(8,128)(2,1)S(1)} %get-tuple-element.199), channel_id=1, source_target_pairs={{0,24},{4,28},{8,16},{12,20},{16,8},{20,12},{24,0},{28,4},{1,25},{... | collective-permute-start | bytes 835592 | tf_op jit(solution)/shard_map/ppermute | solution.py:889
  127.4 7.3 %collective-permute-start.13 = (bf16[80,512]{1,0:T(8,128)(2,1)S(1)}, bf16[80,512]{1,0:T(8,128)(2,1)S(1)}, u32[]{:S(2)}, u32[]{:S(2)}) collective-permute-start(bf16[80,512]{1,0:T(8,128)(2,1)S(1)} %get-tuple-element.200.refs_1_), channel_id=1, source_target_pairs={{0,3},{1,2},{2,1},{3,0},{4,7},{5,6},{6,5},{7,4},{8,11},{9,10},{10,... | collective-permute-start | bytes 245768 | tf_op jit(solution)/shard_map/ppermute | solution.py:889
  130.1 7.4 %collective-permute-start.12 = (bf16[80,512]{1,0:T(8,128)(2,1)S(1)}, bf16[80,512]{1,0:T(8,128)(2,1)S(1)}, u32[]{:S(2)}, u32[]{:S(2)}) collective-permute-start(bf16[80,512]{1,0:T(8,128)(2,1)S(1)} %get-tuple-element.200.refs_1_), channel_id=1, source_target_pairs={{0,2},{1,3},{2,0},{3,1},{4,6},{5,7},{6,4},{7,5},{8,10},{9,11},{10,... | collective-permute-start | bytes 245768 | tf_op jit(solution)/shard_map/ppermute | solution.py:889
  140.2 15.9 %collective-permute-start.29 = (bf16[272,512]{1,0:T(8,128)(2,1)S(1)}, bf16[272,512]{1,0:T(8,128)(2,1)S(1)}, u32[]{:S(2)}, u32[]{:S(2)}) collective-permute-start(bf16[272,512]{1,0:T(8,128)(2,1)S(1)} %get-tuple-element.212.refs_17_), channel_id=1, source_target_pairs={{0,24},{4,28},{8,16},{12,20},{16,8},{20,12},{24,0},{28,4},{1,25},{... | collective-permute-start | bytes 835592 | tf_op jit(solution)/shard_map/ppermute | solution.py:889
  140.8 15.3 %collective-permute-start.28 = (bf16[272,512]{1,0:T(8,128)(2,1)S(1)}, bf16[272,512]{1,0:T(8,128)(2,1)S(1)}, u32[]{:S(2)}, u32[]{:S(2)}) collective-permute-start(bf16[272,512]{1,0:T(8,128)(2,1)S(1)} %get-tuple-element.212.refs_17_), channel_id=1, source_target_pairs={{0,16},{4,20},{8,24},{12,28},{16,0},{20,4},{24,8},{28,12},{1,17},{... | collective-permute-start | bytes 835592 | tf_op jit(solution)/shard_map/ppermute | solution.py:889
  145.7 7.9 %collective-permute-start.16 = (bf16[80,512]{1,0:T(8,128)(2,1)S(1)}, bf16[80,512]{1,0:T(8,128)(2,1)S(1)}, u32[]{:S(2)}, u32[]{:S(2)}) collective-permute-start(bf16[80,512]{1,0:T(8,128)(2,1)S(1)} %get-tuple-element.205), channel_id=1, source_target_pairs={{0,3},{1,2},{2,1},{3,0},{4,7},{5,6},{6,5},{7,4},{8,11},{9,10},{10,... | collective-permute-start | bytes 245768 | tf_op jit(solution)/shard_map/ppermute | solution.py:889
  147.6 15.9 %collective-permute-start.30 = (bf16[272,512]{1,0:T(8,128)(2,1)S(1)}, bf16[272,512]{1,0:T(8,128)(2,1)S(1)}, u32[]{:S(2)}, u32[]{:S(2)}) collective-permute-start(bf16[272,512]{1,0:T(8,128)(2,1)S(1)} %get-tuple-element.212.refs_17_), channel_id=1, source_target_pairs={{0,4},{4,0},{8,12},{12,8},{16,20},{20,16},{24,28},{28,24},{1,5},{5... | collective-permute-start | bytes 835592 | tf_op jit(solution)/shard_map/ppermute | solution.py:889
  152.1 12.8 %collective-permute-start.27 = (bf16[272,512]{1,0:T(8,128)(2,1)S(1)}, bf16[272,512]{1,0:T(8,128)(2,1)S(1)}, u32[]{:S(2)}, u32[]{:S(2)}) collective-permute-start(bf16[272,512]{1,0:T(8,128)(2,1)S(1)} %get-tuple-element.212.refs_17_), channel_id=1, source_target_pairs={{0,8},{4,12},{8,0},{12,4},{16,24},{20,28},{24,16},{28,20},{1,9},{5... | collective-permute-start | bytes 835592 | tf_op jit(solution)/shard_map/ppermute | solution.py:889
  160.5 9.1 %collective-permute-start.33 = (bf16[272,512]{1,0:T(8,128)(2,1)S(1)}, bf16[272,512]{1,0:T(8,128)(2,1)S(1)}, u32[]{:S(2)}, u32[]{:S(2)}) collective-permute-start(bf16[272,512]{1,0:T(8,128)(2,1)S(1)} %collective-permute-done.29.refs_20_), channel_id=1, source_target_pairs={{0,4},{4,0},{8,12},{12,8},{16,20},{20,16},{24,28},{28,24},{1,5},{5... | collective-permute-start | bytes 835592 | tf_op jit(solution)/shard_map/ppermute | solution.py:889
  162.3 7.5 %collective-permute-start.32 = (bf16[272,512]{1,0:T(8,128)(2,1)S(1)}, bf16[272,512]{1,0:T(8,128)(2,1)S(1)}, u32[]{:S(2)}, u32[]{:S(2)}) collective-permute-start(bf16[272,512]{1,0:T(8,128)(2,1)S(1)} %collective-permute-done.28.refs_19_), channel_id=1, source_target_pairs={{0,4},{4,0},{8,12},{12,8},{16,20},{20,16},{24,28},{28,24},{1,5},{5... | collective-permute-start | bytes 835592 | tf_op jit(solution)/shard_map/ppermute | solution.py:889
  162.9 10.5 %collective-permute-start.22 = (bf16[272,512]{1,0:T(8,128)(2,1)S(1)}, bf16[272,512]{1,0:T(8,128)(2,1)S(1)}, u32[]{:S(2)}, u32[]{:S(2)}) collective-permute-start(bf16[272,512]{1,0:T(8,128)(2,1)S(1)} %get-tuple-element.211.refs_9_), channel_id=1, source_target_pairs={{0,24},{4,28},{8,16},{12,20},{16,8},{20,12},{24,0},{28,4},{1,25},{... | collective-permute-start | bytes 835592 | tf_op jit(solution)/shard_map/ppermute | solution.py:889
  163.5 15.9 %collective-permute-start.21 = (bf16[272,512]{1,0:T(8,128)(2,1)S(1)}, bf16[272,512]{1,0:T(8,128)(2,1)S(1)}, u32[]{:S(2)}, u32[]{:S(2)}) collective-permute-start(bf16[272,512]{1,0:T(8,128)(2,1)S(1)} %get-tuple-element.211.refs_9_), channel_id=1, source_target_pairs={{0,16},{4,20},{8,24},{12,28},{16,0},{20,4},{24,8},{28,12},{1,17},{... | collective-permute-start | bytes 835592 | tf_op jit(solution)/shard_map/ppermute | solution.py:889
  165.0 14.4 %collective-permute-start.20 = (bf16[272,512]{1,0:T(8,128)(2,1)S(1)}, bf16[272,512]{1,0:T(8,128)(2,1)S(1)}, u32[]{:S(2)}, u32[]{:S(2)}) collective-permute-start(bf16[272,512]{1,0:T(8,128)(2,1)S(1)} %get-tuple-element.211.refs_9_), channel_id=1, source_target_pairs={{0,8},{4,12},{8,0},{12,4},{16,24},{20,28},{24,16},{28,20},{1,9},{5... | collective-permute-start | bytes 835592 | tf_op jit(solution)/shard_map/ppermute | solution.py:889
  167.0 13.3 %all-to-all-start.7 = ((f32[32,2,512]{2,1,0:T(2,128)}), f32[32,2,512]{2,1,0:T(2,128)S(1)}, u32[]{:S(2)}, u32[]{:S(2)}) async-start(f32[32,2,512]{2,1,0:T(2,128)} %get-tuple-element.195), calls=%async_computation.7 | async-start | bytes 262144 | tf_op jit(solution)/shard_map/all_to_all | solution.py:1057
  169.6 11.3 %collective-permute-start.31 = (bf16[272,512]{1,0:T(8,128)(2,1)S(1)}, bf16[272,512]{1,0:T(8,128)(2,1)}, u32[]{:S(2)}, u32[]{:S(2)}) collective-permute-start(bf16[272,512]{1,0:T(8,128)(2,1)S(1)} %collective-permute-done.27.refs_18_), channel_id=1, source_target_pairs={{0,4},{4,0},{8,12},{12,8},{16,20},{20,16},{24,28},{28,24},{1,5},{5... | collective-permute-start | bytes 835592 | tf_op jit(solution)/shard_map/ppermute | solution.py:889
  169.8 11.2 %collective-permute-start.23 = (bf16[272,512]{1,0:T(8,128)(2,1)S(1)}, bf16[272,512]{1,0:T(8,128)(2,1)}, u32[]{:S(2)}, u32[]{:S(2)}) collective-permute-start(bf16[272,512]{1,0:T(8,128)(2,1)S(1)} %get-tuple-element.211.refs_9_), channel_id=1, source_target_pairs={{0,4},{4,0},{8,12},{12,8},{16,20},{20,16},{24,28},{28,24},{1,5},{5... | collective-permute-start | bytes 835592 | tf_op jit(solution)/shard_map/ppermute | solution.py:889
  173.4 7.6 %collective-permute-start.26 = (bf16[272,512]{1,0:T(8,128)(2,1)S(1)}, bf16[272,512]{1,0:T(8,128)(2,1)}, u32[]{:S(2)}, u32[]{:S(2)}) collective-permute-start(bf16[272,512]{1,0:T(8,128)(2,1)S(1)} %collective-permute-done.22.refs_12_), channel_id=1, source_target_pairs={{0,4},{4,0},{8,12},{12,8},{16,20},{20,16},{24,28},{28,24},{1,5},{5... | collective-permute-start | bytes 835592 | tf_op jit(solution)/shard_map/ppermute | solution.py:889
  (24 other events, 192.1 us)

commit v5 on v4

--- a/solution.py
+++ b/solution.py
@@ -441,7 +441,8 @@
     seqs = parts_ref.shape[1]
     rows, width = x_ref.shape
     group = ends_ref.shape[1]
-    steps = rows // BLOCKS // group
+    blocks = 2 if reverse else BLOCKS
+    steps = rows // blocks // group
     where = Where(info_ref, seqs, rows // seqs)
     powers = Powers(k, False, where, decay_ref, phase_ref, *tables)
     chunk_starts(h_ref, where.seq, parts_ref, powers.leaps, ends_ref, powers.table, reverse)
@@ -450,7 +451,7 @@
     lam, scale = powers.lam[...], powers.scale[...]
     total = jnp.zeros((1, width), f32)
     squares = jnp.zeros((1, width), f32)
-    for block, first, now in blocks_of(rows, group, reverse):
+    for block, first, now in blocks_of(rows, group, reverse, blocks):
         drive = input_drive(lifted_ref[now, :].astype(f32), scale, left, first, steps)
         scan_block(h_ref, drive, left, lam, 0, first, steps, reverse, states_ref)
         state = states_ref[...].astype(bf16)
@@ -495,7 +496,7 @@
     rows, width = x.shape
     states = lifted.shape[1]
     seq_devices, seqs, _ = parts.shape
-    scratch = [pltpu.VMEM(ends.shape, f32), pltpu.VMEM((rows // BLOCKS, states), f32)]
+    scratch = [pltpu.VMEM(ends.shape, f32), pltpu.VMEM((rows // (2 if k == 1 else BLOCKS), states), f32)]
     if k == 1:
         outs = [near((rows, states), bf16)] + [near((rows, width), bf16)] * 5
     else:
@@ -649,7 +650,7 @@
     rows, width = normed_ref.shape
     group = ends_ref.shape[1]
     seqs = parts_ref.shape[1]
-    steps = rows // BACK_BLOCKS // group
+    steps = rows // 1 // group
     states = decay_ref.shape[1]
     where = Where(info_ref, seqs, rows // seqs)
     powers = Powers(k, True, where, decay_ref, phase_ref, *tables)
@@ -663,7 +664,7 @@
     gain_sum = jnp.zeros((1, width), f32)
     shift_sum = jnp.zeros((1, width), f32)
     shift = 1 if reverse else -1
-    for _, first, now in blocks_of(rows, group, reverse, BACK_BLOCKS):
+    for _, first, now in blocks_of(rows, group, reverse, 1):
         moving = [left > first + t + shift for t in range(steps)]
         valid = [left > first + t for t in range(steps)]
         dh = dh_ref[now, :].astype(f32)
@@ -729,7 +730,7 @@
         outs.append(moved((rows, width), bf16))
     scratch = [
         pltpu.VMEM(table, f32),
-        pltpu.VMEM((rows // BACK_BLOCKS, states), f32),
+        pltpu.VMEM((rows // 1, states), f32),
         pltpu.VMEM(acc, f32),
         pltpu.VMEM((table[1], states), f32),
         pltpu.VMEM((table[1], states // 2), f32),
@@ -945,7 +946,7 @@
 def results_kernel(chips, info_ref, sums_ref, norm1_ref, decay_ref, phase_ref, stats_ref, gain_ref, *refs):
     (tokens_in, ahead_in), pieces, refs = refs[:2], refs[2 : 2 + 4 * chips], refs[2 + 4 * chips :]
     glu_ref, mix_ref, lift_ref, grad_out, *small_refs = refs[:10]
-    low_ref, under_ref, wide_ref, tokens_ref, ahead_ref, rows_ref, grad_ref, in_sems, sems, own_sems = refs[10:]
+    low_ref, wide_ref, tokens_ref, ahead_ref, rows_ref, grad_ref, in_sems, sems, own_sems = refs[10:]
     own = [
         pltpu.make_async_copy(ahead_in, ahead_ref, own_sems.at[0]),
         pltpu.make_async_copy(tokens_in, tokens_ref, own_sems.at[1]),
@@ -956,8 +957,7 @@
     half, quarter = rows // 2, rows // 4
     arriving = []
     for n, piece in enumerate(pieces):
-        parts = [pltpu.make_async_copy(piece.at[pl.ds(0, rows), :], low_ref.at[n], in_sems.at[n, 0])]
-        parts.append(pltpu.make_async_copy(piece.at[pl.ds(rows, EXTRA), :], under_ref.at[n], in_sems.at[n, 1]))
+        parts = [pltpu.make_async_copy(piece, low_ref.at[n], in_sems.at[n])]
         begin(parts)
         arriving.append(parts)
     begin(own)
@@ -967,12 +967,12 @@
         finished(arriving[n])
         k, n_in = divmod(n, 2 * chips)
         chip, side = place ^ (n_in % chips), core if n_in < chips else 1 - core
-        extra = one_part(under_ref[n].astype(f32))
+        extra = one_part(low_ref[n, rows:, :].astype(f32))
         extras[k][n_in // chips] = jnp.where(chip == 0, extra, extras[k][n_in // chips])
         column = pl.multiple_of(side * width, width)
         row = pl.multiple_of(chip * half, 8)
         low = pl.multiple_of(side * (quarter * chips) + chip * quarter, 8)
-        wide_ref[n] = low_ref[n].astype(f32)
+        wide_ref[n] = low_ref[n, :rows, :].astype(f32)
         for i, (first, size, target) in enumerate(
             (
                 (0, half, glu_ref.at[k, pl.ds(row, half), pl.ds(column, width)]),
@@ -1012,14 +1012,13 @@
     blocks, states = decay_log.shape
     outs += [moved((blocks, n), f32) for n in (width, width, states, states, width, 2 * width)]
     scratch = [
-        pltpu.VMEM((count, rows, width), bf16),
-        pltpu.VMEM((count, EXTRA, width), bf16),
+        pltpu.VMEM((count, rows + EXTRA, width), bf16),
         pltpu.VMEM((count, rows, width), f32),
         pltpu.VMEM(tokens.shape, bf16),
         pltpu.VMEM(ahead.shape, bf16),
         pltpu.VMEM((span // CHUNKS, seqs, CHUNKS, width), f32),
         pltpu.VMEM(tokens.shape, bf16),
-        pltpu.SemaphoreType.DMA((count, 2)),
+        pltpu.SemaphoreType.DMA((count,)),
         pltpu.SemaphoreType.DMA((count, 3)),
         pltpu.SemaphoreType.DMA((3,)),
     ]

time: 190 us -> 189 us (level)
  no operation moved by 1% of the time
where the time goes in v5:
time: 189 us
  Pallas kernels  61.1 us (32%)
  blocking collectives  56.1 us (30%)
  starting transfers between devices  39.8 us (21%)
  waiting for transfers between devices  27.8 us (15%)
  local copies, waits for them, and re-layouts  2.9 us (2%)
    pallas_call x24, Pallas kernels, run(): pl.pallas_call(ticking, in_specs=[in_smem] + specs + [in_hbm] * len(after...  61.1 us
    all_to_all x6, blocking collectives, to_all(): return lax.all_to_all(x, axes, split_axis=0, concat_axis=0, tiled=True)  56.1 us
    ppermute x34, starting transfers between devices, trade(): return lax.ppermute(x, axis, [(i, i ^ mask) for i in range(size)])  34.4 us
    ppermute x34, waiting for transfers between devices, trade(): return lax.ppermute(x, axis, [(i, i ^ mask) for i in range(size)])  26.7 us
    all_to_all x2, starting transfers between devices, to_all(): return lax.all_to_all(x, axes, split_axis=0, concat_axis=0, tiled=True)  5.39 us
  transfers between devices with their start and end apart: 36, of which 13 were waited for; matrix products, arithmetic and copies ran while one was open for 0% of the time, Pallas kernels for 9%

profile of v5, /device:TPU:0, one launch (start us, length us, event | category | flops | bytes accessed | tf_op | source)
XLA Modules:
  0.0 188.8 jit_solution(303402088078922828)
XLA Ops:
  3.6 16.0 %all_to_all.40.refs_1_ = f32[32,2,640]{2,1,0:T(2,128)S(1)} all-to-all(f32[32,2,640]{2,1,0:T(2,128)S(1)} %get-tuple-element.117), channel_id=1, replica_groups=mesh['seq'=8,'batch'=4] {'seq','batch'}, dimensions={0} | all-to-all | bytes 327680 | tf_op jit(solution)/shard_map/all_to_all | solution.py:1056
  22.0 7.4 %all_to_all.41.refs_1_ = f32[8,4,512]{2,1,0:T(4,128)S(1)} all-to-all(f32[8,4,512]{2,1,0:T(4,128)S(1)} %get-tuple-element.120), channel_id=1, replica_groups=mesh['seq'=8,'batch'=4] {'seq'}, dimensions={0} | all-to-all | bytes 131072 | tf_op jit(solution)/shard_map/all_to_all | solution.py:1056
  29.4 6.3 %mix.2 = (f32[1024,512]{1,0:T(8,128)S(1)}, f32[32,2,512]{2,1,0:T(2,128)S(1)}, bf16[1024,2560]{1,0:T(8,128)(2,1)}, bf16[512,512]{1,0:T(8,128)(2,1)S(1)}, bf16[1024,512]{1,0:T(8,128)(2,1)}, /*index=5*/f32[8,128]{1,0:T(8,128)}) custom-call(s32[4]{0:T(128)S(1)} %copy-done.8, f32[8,4,512]{2,1,0:T(4,128)S(1)} %all_to_all.41.refs_1_, f32[2,512]{1,0:T(2,128)S(1)} %copy-done.9, ...), custom_call_target="tpu_custom_call" | custom-call | tf_op jit(solution)/shard_map/mix/pallas_call | solution.py:65
  35.7 10.1 %all_to_all.42.refs_1_ = f32[32,2,512]{2,1,0:T(2,128)S(1)} all-to-all(f32[32,2,512]{2,1,0:T(2,128)S(1)} %get-tuple-element.127), channel_id=1, replica_groups=mesh['seq'=8,'batch'=4] {'seq','batch'}, dimensions={0} | all-to-all | bytes 262144 | tf_op jit(solution)/shard_map/all_to_all | solution.py:1056
  47.8 7.4 %all_to_all.43.refs_1_ = f32[8,4,512]{2,1,0:T(4,128)S(1)} all-to-all(f32[8,4,512]{2,1,0:T(4,128)S(1)} %get-tuple-element.131), channel_id=1, replica_groups=mesh['seq'=8,'batch'=4] {'seq'}, dimensions={0} | all-to-all | bytes 131072 | tf_op jit(solution)/shard_map/all_to_all | solution.py:1056
  55.2 5.2 %mix.3 = (bf16[1024,512]{1,0:T(8,128)(2,1)S(1)}, bf16[1024,512]{1,0:T(8,128)(2,1)S(1)}, bf16[1024,512]{1,0:T(8,128)(2,1)S(1)}, bf16[1024,512]{1,0:T(8,128)(2,1)S...) custom-call(s32[4]{0:T(128)S(1)} %copy-done.8, ...), custom_call_target="tpu_custom_call" | custom-call | tf_op jit(solution)/shard_map/mix/pallas_call | solution.py:65
  60.4 3.4 %glu_back.2 = (bf16[1024,2560]{1,0:T(8,128)(2,1)S(1)}, f32[1,1024]{1,0:T(1,128)S(1)}, f32[1,512]{1,0:T(1,128)S(1)}, f32[4,32,128]{2,1,0:T(8,128)S(1)}, f32[8,4,5...) custom-call(s32[4]{0:T(128)S(1)} %copy-done.8, ...), custom_call_target="tpu_custom_call" | custom-call | tf_op jit(solution)/shard_map/glu_back/pallas_call | solution.py:65
  63.9 7.4 %all_to_all.44.refs_1_ = f32[8,4,512]{2,1,0:T(4,128)S(1)} all-to-all(f32[8,4,512]{2,1,0:T(4,128)S(1)} %get-tuple-element.145), channel_id=1, replica_groups=mesh['seq'=8,'batch'=4] {'seq'}, dimensions={0} | all-to-all | bytes 131072 | tf_op jit(solution)/shard_map/all_to_all | solution.py:1056
  71.3 4.0 %lift_back.2 = (bf16[1024,2048]{1,0:T(8,128)(2,1)S(1)}, f32[32,2,512]{2,1,0:T(2,128)}, f32[1,512]{1,0:T(1,128)S(1)}, f32[1,256]{1,0:T(1,128)S(1)}, f32[8,128]{1,0:T(8,128)}) custom-call(s32[4]{0:T(128)S(1)} %copy-done.8, f32[8,4,512]{2,1,0:T(4,128)S(1)} %all_to_all.44.refs_1_, f32[8,512]{1,0:T(8,128)S(1)} %get-tuple-element.146.refs_2_.refs_4_, ...), custom_call_target="tpu_custom_call" | custom-call | tf_op jit(solution)/shard_map/lift_back/pallas_call | solution.py:65
  75.2 3.9 %halves1.1 = (bf16[1088,512]{1,0:T(8,128)(2,1)S(1)}, bf16[1088,512]{1,0:T(8,128)(2,1)}, f32[8,128]{1,0:T(8,128)}) custom-call(s32[4]{0:T(128)S(1)} %copy-done.8, f32[1,512]{1,0:T(1,128)S(1)} %get-tuple-element.143.refs_1_, f32[1,1024]{1,0:T(1,128)S(1)} %get-tuple-element.144.refs_2_, f32[1,512]{1,0:T(1,128)S(1)} %get-tuple-element.151.refs_3_, ...), custom_call_target="tpu_custom_call" | custom-call | tf_op jit(solution)/shard_map/halves1/pallas_call | solution.py:65
  79.2 2.8 %all-to-all-start.5 = ((f32[32,2,512]{2,1,0:T(2,128)}), f32[32,2,512]{2,1,0:T(2,128)S(1)}, u32[]{:S(2)}, u32[]{:S(2)}) async-start(f32[32,2,512]{2,1,0:T(2,128)} %get-tuple-element.157), calls=%async_computation.5 | async-start | bytes 262144 | tf_op jit(solution)/shard_map/all_to_all | solution.py:1056
  92.4 6.5 %glu_back.3 = (bf16[1024,2560]{1,0:T(8,128)(2,1)S(1)}, f32[1,1024]{1,0:T(1,128)S(1)}, f32[1,512]{1,0:T(1,128)S(1)}, f32[4,32,128]{2,1,0:T(8,128)S(1)}, f32[8,4,5...) custom-call(s32[4]{0:T(128)S(1)} %copy-done.8, ...), custom_call_target="tpu_custom_call" | custom-call | tf_op jit(solution)/shard_map/glu_back/pallas_call | solution.py:65
  98.9 7.8 %all_to_all.45.refs_1_ = f32[8,4,512]{2,1,0:T(4,128)S(1)} all-to-all(f32[8,4,512]{2,1,0:T(4,128)S(1)} %get-tuple-element.160), channel_id=1, replica_groups=mesh['seq'=8,'batch'=4] {'seq'}, dimensions={0} | all-to-all | bytes 131072 | tf_op jit(solution)/shard_map/all_to_all | solution.py:1056
  107.3 4.5 %lift_back.3 = (bf16[1024,512]{1,0:T(8,128)(2,1)S(1)}, f32[32,2,512]{2,1,0:T(2,128)}, f32[1,512]{1,0:T(1,128)S(1)}, f32[1,256]{1,0:T(1,128)S(1)}, bf16[1024,512]...) custom-call(s32[4]{0:T(128)S(1)} %copy-done.8, f32[8,4,512]{2,1,0:T(4,128)S(1)} %get-tuple-element.168.refs_1_, ...), custom_call_target="tpu_custom_call" | custom-call | tf_op jit(solution)/shard_map/lift_back/pallas_call | solution.py:65
  111.7 2.9 %halves0.1 = (bf16[1088,512]{1,0:T(8,128)(2,1)S(1)}, bf16[1088,512]{1,0:T(8,128)(2,1)S(1)}, f32[8,128]{1,0:T(8,128)}) custom-call(s32[4]{0:T(128)S(1)} %copy-done.8, f32[1,512]{1,0:T(1,128)S(1)} %get-tuple-element.179.refs_1_, f32[1,1024]{1,0:T(1,128)S(1)} %get-tuple-element.180.refs_2_, f32[1,512]{1,0:T(1,128)S(1)} %get-tuple-element.181.refs_3_, ...), custom_call_target="tpu_custom_call" | custom-call | tf_op jit(solution)/shard_map/halves0/pallas_call | solution.py:65
  117.1 2.5 %collective-permute-start.5 = (bf16[80,512]{1,0:T(8,128)(2,1)S(1)}, bf16[80,512]{1,0:T(8,128)(2,1)S(1)}, u32[]{:S(2)}, u32[]{:S(2)}) collective-permute-start(bf16[80,512]{1,0:T(8,128)(2,1)S(1)} %get-tuple-element.188), channel_id=1, source_target_pairs={{0,2},{1,3},{2,0},{3,1},{4,6},{5,7},{6,4},{7,5},{8,10},{9,11},{10,... | collective-permute-start | bytes 245768 | tf_op jit(solution)/shard_map/ppermute | solution.py:890
  127.2 2.6 %collective-permute-start.13 = (bf16[80,512]{1,0:T(8,128)(2,1)S(1)}, bf16[80,512]{1,0:T(8,128)(2,1)S(1)}, u32[]{:S(2)}, u32[]{:S(2)}) collective-permute-start(bf16[80,512]{1,0:T(8,128)(2,1)S(1)} %get-tuple-element.200.refs_1_), channel_id=1, source_target_pairs={{0,3},{1,2},{2,1},{3,0},{4,7},{5,6},{6,5},{7,4},{8,11},{9,10},{10,... | collective-permute-start | bytes 245768 | tf_op jit(solution)/shard_map/ppermute | solution.py:890
  130.5 4.1 %collective-permute-done.13.refs_4_ = bf16[80,512]{1,0:T(8,128)(2,1)S(1)} collective-permute-done((bf16[80,512]{1,0:T(8,128)(2,1)S(1)}, bf16[80,512]{1,0:T(8,128)(2,1)S(1)}, u32[]{:S(2)}, u32[]{:S(2)}) %collective-permute-start.13) | collective-permute-done | bytes 81952 | tf_op jit(solution)/shard_map/ppermute | solution.py:890
  147.4 4.5 %collective-permute-done.15.refs_3_ = bf16[80,512]{1,0:T(8,128)(2,1)S(1)} collective-permute-done((bf16[80,512]{1,0:T(8,128)(2,1)S(1)}, bf16[80,512]{1,0:T(8,128)(2,1)S(1)}, u32[]{:S(2)}, u32[]{:S(2)}) %collective-permute-start.15) | collective-permute-done | bytes 81952 | tf_op jit(solution)/shard_map/ppermute | solution.py:890
  155.9 2.5 %collective-permute-start.17 = (bf16[80,512]{1,0:T(8,128)(2,1)S(1)}, bf16[80,512]{1,0:T(8,128)(2,1)S(1)}, u32[]{:S(2)}, u32[]{:S(2)}) collective-permute-start(bf16[80,512]{1,0:T(8,128)(2,1)S(1)} %get-tuple-element.206.refs_1_), channel_id=1, source_target_pairs={{0,1},{1,0},{2,3},{3,2},{4,5},{5,4},{6,7},{7,6},{8,9},{9,8},{10,11... | collective-permute-start | bytes 245768 | tf_op jit(solution)/shard_map/ppermute | solution.py:890
  166.8 2.6 %all-to-all-start.7 = ((f32[32,2,512]{2,1,0:T(2,128)}), f32[32,2,512]{2,1,0:T(2,128)S(1)}, u32[]{:S(2)}, u32[]{:S(2)}) async-start(f32[32,2,512]{2,1,0:T(2,128)} %get-tuple-element.195), calls=%async_computation.7 | async-start | bytes 262144 | tf_op jit(solution)/shard_map/all_to_all | solution.py:1056
  170.0 3.2 %collective-permute-done.22.refs_12_ = bf16[272,512]{1,0:T(8,128)(2,1)S(1)} collective-permute-done((bf16[272,512]{1,0:T(8,128)(2,1)S(1)}, bf16[272,512]{1,0:T(8,128)(2,1)S(1)}, u32[]{:S(2)}, u32[]{:S(2)}) %collective-permute-start.22) | collective-permute-done | bytes 278560 | tf_op jit(solution)/shard_map/ppermute | solution.py:890
  173.2 6.0 %collective-permute-done.21.refs_11_ = bf16[272,512]{1,0:T(8,128)(2,1)S(1)} collective-permute-done((bf16[272,512]{1,0:T(8,128)(2,1)S(1)}, bf16[272,512]{1,0:T(8,128)(2,1)S(1)}, u32[]{:S(2)}, u32[]{:S(2)}) %collective-permute-start.21) | collective-permute-done | bytes 278560 | tf_op jit(solution)/shard_map/ppermute | solution.py:890
  181.3 7.3 %results.1 = (f32[2,512,1024]{2,1,0:T(8,128)}, f32[2,512,512]{2,1,0:T(8,128)}, f32[2,512,512]{2,1,0:T(8,128)}, bf16[4,256,512]{2,1,0:T(8,128)(2,1)}, f32[2,512]{...) custom-call(s32[4]{0:T(128)S(1)} %copy-done.8, ...), custom_call_target="tpu_custom_call" | custom-call | flops 7699999744 | bytes 21000000 | tf_op jit(solution)/shard_map/results/pallas_call | solution.py:65
  (102 shorter events, 56.7 us)
Async XLA Ops:
  79.2 11.1 %all-to-all-start.5 = ((f32[32,2,512]{2,1,0:T(2,128)}), f32[32,2,512]{2,1,0:T(2,128)S(1)}, u32[]{:S(2)}, u32[]{:S(2)}) async-start(f32[32,2,512]{2,1,0:T(2,128)} %get-tuple-element.157), calls=%async_computation.5 | async-start | bytes 262144 | tf_op jit(solution)/shard_map/all_to_all | solution.py:1056
  86.1 20.6 %collective-permute-start.1 = (bf16[272,512]{1,0:T(8,128)(2,1)}, bf16[272,512]{1,0:T(8,128)(2,1)S(1)}, u32[]{:S(2)}, u32[]{:S(2)}) collective-permute-start(bf16[272,512]{1,0:T(8,128)(2,1)} %get-tuple-element.165), channel_id=1, source_target_pairs={{0,8},{4,12},{8,0},{12,4},{16,24},{20,28},{24,16},{28,20},{1,9},{5... | collective-permute-start | bytes 835592 | tf_op jit(solution)/shard_map/ppermute | solution.py:890
  87.5 19.2 %collective-permute-start.2 = (bf16[272,512]{1,0:T(8,128)(2,1)S(1)}, bf16[272,512]{1,0:T(8,128)(2,1)S(1)}, u32[]{:S(2)}, u32[]{:S(2)}) collective-permute-start(bf16[272,512]{1,0:T(8,128)(2,1)S(1)} %get-tuple-element.166), channel_id=1, source_target_pairs={{0,16},{4,20},{8,24},{12,28},{16,0},{20,4},{24,8},{28,12},{1,17},{... | collective-permute-start | bytes 835592 | tf_op jit(solution)/shard_map/ppermute | solution.py:890
  89.0 17.7 %collective-permute-start.3 = (bf16[272,512]{1,0:T(8,128)(2,1)S(1)}, bf16[272,512]{1,0:T(8,128)(2,1)S(1)}, u32[]{:S(2)}, u32[]{:S(2)}) collective-permute-start(bf16[272,512]{1,0:T(8,128)(2,1)S(1)} %get-tuple-element.167), channel_id=1, source_target_pairs={{0,24},{4,28},{8,16},{12,20},{16,8},{20,12},{24,0},{28,4},{1,25},{... | collective-permute-start | bytes 835592 | tf_op jit(solution)/shard_map/ppermute | solution.py:890
  117.1 9.5 %collective-permute-start.5 = (bf16[80,512]{1,0:T(8,128)(2,1)S(1)}, bf16[80,512]{1,0:T(8,128)(2,1)S(1)}, u32[]{:S(2)}, u32[]{:S(2)}) collective-permute-start(bf16[80,512]{1,0:T(8,128)(2,1)S(1)} %get-tuple-element.188), channel_id=1, source_target_pairs={{0,2},{1,3},{2,0},{3,1},{4,6},{5,7},{6,4},{7,5},{8,10},{9,11},{10,... | collective-permute-start | bytes 245768 | tf_op jit(solution)/shard_map/ppermute | solution.py:890
  120.8 21.3 %collective-permute-start.8 = (bf16[272,512]{1,0:T(8,128)(2,1)S(1)}, bf16[272,512]{1,0:T(8,128)(2,1)S(1)}, u32[]{:S(2)}, u32[]{:S(2)}) collective-permute-start(bf16[272,512]{1,0:T(8,128)(2,1)S(1)} %get-tuple-element.197), channel_id=1, source_target_pairs={{0,8},{4,12},{8,0},{12,4},{16,24},{20,28},{24,16},{28,20},{1,9},{5... | collective-permute-start | bytes 835592 | tf_op jit(solution)/shard_map/ppermute | solution.py:890
  121.4 20.6 %collective-permute-start.9 = (bf16[272,512]{1,0:T(8,128)(2,1)S(1)}, bf16[272,512]{1,0:T(8,128)(2,1)S(1)}, u32[]{:S(2)}, u32[]{:S(2)}) collective-permute-start(bf16[272,512]{1,0:T(8,128)(2,1)S(1)} %get-tuple-element.198), channel_id=1, source_target_pairs={{0,16},{4,20},{8,24},{12,28},{16,0},{20,4},{24,8},{28,12},{1,17},{... | collective-permute-start | bytes 835592 | tf_op jit(solution)/shard_map/ppermute | solution.py:890
  122.0 20.1 %collective-permute-start.10 = (bf16[272,512]{1,0:T(8,128)(2,1)S(1)}, bf16[272,512]{1,0:T(8,128)(2,1)S(1)}, u32[]{:S(2)}, u32[]{:S(2)}) collective-permute-start(bf16[272,512]{1,0:T(8,128)(2,1)S(1)} %get-tuple-element.199), channel_id=1, source_target_pairs={{0,24},{4,28},{8,16},{12,20},{16,8},{20,12},{24,0},{28,4},{1,25},{... | collective-permute-start | bytes 835592 | tf_op jit(solution)/shard_map/ppermute | solution.py:890
  127.2 7.3 %collective-permute-start.13 = (bf16[80,512]{1,0:T(8,128)(2,1)S(1)}, bf16[80,512]{1,0:T(8,128)(2,1)S(1)}, u32[]{:S(2)}, u32[]{:S(2)}) collective-permute-start(bf16[80,512]{1,0:T(8,128)(2,1)S(1)} %get-tuple-element.200.refs_1_), channel_id=1, source_target_pairs={{0,3},{1,2},{2,1},{3,0},{4,7},{5,6},{6,5},{7,4},{8,11},{9,10},{10,... | collective-permute-start | bytes 245768 | tf_op jit(solution)/shard_map/ppermute | solution.py:890
  129.9 7.4 %collective-permute-start.12 = (bf16[80,512]{1,0:T(8,128)(2,1)S(1)}, bf16[80,512]{1,0:T(8,128)(2,1)S(1)}, u32[]{:S(2)}, u32[]{:S(2)}) collective-permute-start(bf16[80,512]{1,0:T(8,128)(2,1)S(1)} %get-tuple-element.200.refs_1_), channel_id=1, source_target_pairs={{0,2},{1,3},{2,0},{3,1},{4,6},{5,7},{6,4},{7,5},{8,10},{9,11},{10,... | collective-permute-start | bytes 245768 | tf_op jit(solution)/shard_map/ppermute | solution.py:890
  140.0 15.9 %collective-permute-start.29 = (bf16[272,512]{1,0:T(8,128)(2,1)S(1)}, bf16[272,512]{1,0:T(8,128)(2,1)S(1)}, u32[]{:S(2)}, u32[]{:S(2)}) collective-permute-start(bf16[272,512]{1,0:T(8,128)(2,1)S(1)} %get-tuple-element.212.refs_17_), channel_id=1, source_target_pairs={{0,24},{4,28},{8,16},{12,20},{16,8},{20,12},{24,0},{28,4},{1,25},{... | collective-permute-start | bytes 835592 | tf_op jit(solution)/shard_map/ppermute | solution.py:890
  140.6 15.3 %collective-permute-start.28 = (bf16[272,512]{1,0:T(8,128)(2,1)S(1)}, bf16[272,512]{1,0:T(8,128)(2,1)S(1)}, u32[]{:S(2)}, u32[]{:S(2)}) collective-permute-start(bf16[272,512]{1,0:T(8,128)(2,1)S(1)} %get-tuple-element.212.refs_17_), channel_id=1, source_target_pairs={{0,16},{4,20},{8,24},{12,28},{16,0},{20,4},{24,8},{28,12},{1,17},{... | collective-permute-start | bytes 835592 | tf_op jit(solution)/shard_map/ppermute | solution.py:890
  145.5 7.9 %collective-permute-start.16 = (bf16[80,512]{1,0:T(8,128)(2,1)S(1)}, bf16[80,512]{1,0:T(8,128)(2,1)S(1)}, u32[]{:S(2)}, u32[]{:S(2)}) collective-permute-start(bf16[80,512]{1,0:T(8,128)(2,1)S(1)} %get-tuple-element.205), channel_id=1, source_target_pairs={{0,3},{1,2},{2,1},{3,0},{4,7},{5,6},{6,5},{7,4},{8,11},{9,10},{10,... | collective-permute-start | bytes 245768 | tf_op jit(solution)/shard_map/ppermute | solution.py:890
  147.4 15.9 %collective-permute-start.30 = (bf16[272,512]{1,0:T(8,128)(2,1)S(1)}, bf16[272,512]{1,0:T(8,128)(2,1)S(1)}, u32[]{:S(2)}, u32[]{:S(2)}) collective-permute-start(bf16[272,512]{1,0:T(8,128)(2,1)S(1)} %get-tuple-element.212.refs_17_), channel_id=1, source_target_pairs={{0,4},{4,0},{8,12},{12,8},{16,20},{20,16},{24,28},{28,24},{1,5},{5... | collective-permute-start | bytes 835592 | tf_op jit(solution)/shard_map/ppermute | solution.py:890
  151.9 12.8 %collective-permute-start.27 = (bf16[272,512]{1,0:T(8,128)(2,1)S(1)}, bf16[272,512]{1,0:T(8,128)(2,1)S(1)}, u32[]{:S(2)}, u32[]{:S(2)}) collective-permute-start(bf16[272,512]{1,0:T(8,128)(2,1)S(1)} %get-tuple-element.212.refs_17_), channel_id=1, source_target_pairs={{0,8},{4,12},{8,0},{12,4},{16,24},{20,28},{24,16},{28,20},{1,9},{5... | collective-permute-start | bytes 835592 | tf_op jit(solution)/shard_map/ppermute | solution.py:890
  160.3 9.1 %collective-permute-start.33 = (bf16[272,512]{1,0:T(8,128)(2,1)S(1)}, bf16[272,512]{1,0:T(8,128)(2,1)S(1)}, u32[]{:S(2)}, u32[]{:S(2)}) collective-permute-start(bf16[272,512]{1,0:T(8,128)(2,1)S(1)} %collective-permute-done.29.refs_20_), channel_id=1, source_target_pairs={{0,4},{4,0},{8,12},{12,8},{16,20},{20,16},{24,28},{28,24},{1,5},{5... | collective-permute-start | bytes 835592 | tf_op jit(solution)/shard_map/ppermute | solution.py:890
  162.0 7.5 %collective-permute-start.32 = (bf16[272,512]{1,0:T(8,128)(2,1)S(1)}, bf16[272,512]{1,0:T(8,128)(2,1)S(1)}, u32[]{:S(2)}, u32[]{:S(2)}) collective-permute-start(bf16[272,512]{1,0:T(8,128)(2,1)S(1)} %collective-permute-done.28.refs_19_), channel_id=1, source_target_pairs={{0,4},{4,0},{8,12},{12,8},{16,20},{20,16},{24,28},{28,24},{1,5},{5... | collective-permute-start | bytes 835592 | tf_op jit(solution)/shard_map/ppermute | solution.py:890
  162.7 10.5 %collective-permute-start.22 = (bf16[272,512]{1,0:T(8,128)(2,1)S(1)}, bf16[272,512]{1,0:T(8,128)(2,1)S(1)}, u32[]{:S(2)}, u32[]{:S(2)}) collective-permute-start(bf16[272,512]{1,0:T(8,128)(2,1)S(1)} %get-tuple-element.211.refs_9_), channel_id=1, source_target_pairs={{0,24},{4,28},{8,16},{12,20},{16,8},{20,12},{24,0},{28,4},{1,25},{... | collective-permute-start | bytes 835592 | tf_op jit(solution)/shard_map/ppermute | solution.py:890
  163.3 15.9 %collective-permute-start.21 = (bf16[272,512]{1,0:T(8,128)(2,1)S(1)}, bf16[272,512]{1,0:T(8,128)(2,1)S(1)}, u32[]{:S(2)}, u32[]{:S(2)}) collective-permute-start(bf16[272,512]{1,0:T(8,128)(2,1)S(1)} %get-tuple-element.211.refs_9_), channel_id=1, source_target_pairs={{0,16},{4,20},{8,24},{12,28},{16,0},{20,4},{24,8},{28,12},{1,17},{... | collective-permute-start | bytes 835592 | tf_op jit(solution)/shard_map/ppermute | solution.py:890
  164.8 14.4 %collective-permute-start.20 = (bf16[272,512]{1,0:T(8,128)(2,1)S(1)}, bf16[272,512]{1,0:T(8,128)(2,1)S(1)}, u32[]{:S(2)}, u32[]{:S(2)}) collective-permute-start(bf16[272,512]{1,0:T(8,128)(2,1)S(1)} %get-tuple-element.211.refs_9_), channel_id=1, source_target_pairs={{0,8},{4,12},{8,0},{12,4},{16,24},{20,28},{24,16},{28,20},{1,9},{5... | collective-permute-start | bytes 835592 | tf_op jit(solution)/shard_map/ppermute | solution.py:890
  166.8 13.3 %all-to-all-start.7 = ((f32[32,2,512]{2,1,0:T(2,128)}), f32[32,2,512]{2,1,0:T(2,128)S(1)}, u32[]{:S(2)}, u32[]{:S(2)}) async-start(f32[32,2,512]{2,1,0:T(2,128)} %get-tuple-element.195), calls=%async_computation.7 | async-start | bytes 262144 | tf_op jit(solution)/shard_map/all_to_all | solution.py:1056
  169.4 11.3 %collective-permute-start.31 = (bf16[272,512]{1,0:T(8,128)(2,1)S(1)}, bf16[272,512]{1,0:T(8,128)(2,1)}, u32[]{:S(2)}, u32[]{:S(2)}) collective-permute-start(bf16[272,512]{1,0:T(8,128)(2,1)S(1)} %collective-permute-done.27.refs_18_), channel_id=1, source_target_pairs={{0,4},{4,0},{8,12},{12,8},{16,20},{20,16},{24,28},{28,24},{1,5},{5... | collective-permute-start | bytes 835592 | tf_op jit(solution)/shard_map/ppermute | solution.py:890
  169.6 11.2 %collective-permute-start.23 = (bf16[272,512]{1,0:T(8,128)(2,1)S(1)}, bf16[272,512]{1,0:T(8,128)(2,1)}, u32[]{:S(2)}, u32[]{:S(2)}) collective-permute-start(bf16[272,512]{1,0:T(8,128)(2,1)S(1)} %get-tuple-element.211.refs_9_), channel_id=1, source_target_pairs={{0,4},{4,0},{8,12},{12,8},{16,20},{20,16},{24,28},{28,24},{1,5},{5... | collective-permute-start | bytes 835592 | tf_op jit(solution)/shard_map/ppermute | solution.py:890
  173.2 7.6 %collective-permute-start.26 = (bf16[272,512]{1,0:T(8,128)(2,1)S(1)}, bf16[272,512]{1,0:T(8,128)(2,1)}, u32[]{:S(2)}, u32[]{:S(2)}) collective-permute-start(bf16[272,512]{1,0:T(8,128)(2,1)S(1)} %collective-permute-done.22.refs_12_), channel_id=1, source_target_pairs={{0,4},{4,0},{8,12},{12,8},{16,20},{20,16},{24,28},{28,24},{1,5},{5... | collective-permute-start | bytes 835592 | tf_op jit(solution)/shard_map/ppermute | solution.py:890
  (24 other events, 192.1 us)

commit v6 on v5

--- a/solution.py
+++ b/solution.py
@@ -86,7 +86,7 @@
     return pltpu.with_memory_space_constraint(x, pltpu.HBM)
 
 
-def call(kernel, info, inputs, arrays, away, outs, scratch, name, after=(), fetch=(), spill=(), us=None):
+def call(kernel, info, inputs, arrays, away, outs, scratch, name, after=(), fetch=(), spill=(), us=None, late=False):
     first = 1 + len(inputs) + len(arrays) + len(away)
     n_copies = len(fetch) + len(spill)
     fetched = [jax.eval_shape(lambda x, at=at: x if at is None else x[at], a) for a, at in fetch]
@@ -105,8 +105,12 @@
         copies = []
         for i, (x, y) in enumerate(zip(sources, targets)):
             copies += copy_parts(x, y, rest[-1].at[i])
-        begin(copies)
-        kernel(*ins[:first], *(rest[:-1] if copies else rest))
+        own = (*ins[:first], *(rest[:-1] if copies else rest))
+        if late:
+            kernel(*own, begin_others=lambda: begin(copies))
+        else:
+            begin(copies)
+            kernel(*own)
         finished(copies)
 
     given = [*inputs, *map(here, arrays), *map(there, away), *(there(a) for a, _ in fetch), *map(here, spill)]
@@ -509,7 +513,7 @@
     )
 
 
-def glu_back_kernel(k, seqs, info_ref, decay_ref, phase_ref, *refs):
+def glu_back_kernel(k, seqs, info_ref, decay_ref, phase_ref, *refs, begin_others):
     reverse = k == 0
     if k == 0:
         sums_ref, stats_ref, gain_ref, shift_ref, lift_pack_ref, kept_ref, normed_in, glu_in, mix_in = refs[:9]
@@ -536,6 +540,7 @@
     where = Where(info_ref, seqs, rows // seqs)
     if k == 1:
         (wide_ref,) = refs
+        begin_others()
         shuffle_rows(wide_ref, start_ref)
     else:
         copies = {}
@@ -549,6 +554,7 @@
             begin(copies[block])
             if n == 0:
                 begin(weights)
+        begin_others()
         sums = jnp.sum(sums_ref[...], axis=0)
         total_ref[...] = sums
         root, count = stats_ref[1:2, :], stats_ref[2:3, 0:1]
@@ -622,7 +628,8 @@
         ]
     scratch += Powers.scratch(seqs, seq_devices, states, False)
     return call(
-        partial(glu_back_kernel, k, seqs), info, inputs, arrays, away, outs, scratch, "glu_back", after, fetch, spill
+        partial(glu_back_kernel, k, seqs), info, inputs, arrays, away, outs, scratch, "glu_back", after, fetch, spill,
+        late=True,
     )
 
 

time: 189 us -> 189 us (level)
  transfers between devices with their start and end apart: 36 -> 36, of which waited for: 13 -> 13; matrix products, arithmetic and copies ran while one was open for 0% -> 0% of each run, Pallas kernels for 9% -> 8%
where the time goes in v6:
time: 189 us; the launch traced here: 188 us
  Pallas kernels  60.4 us (32%)
  blocking collectives  56.1 us (30%)
  starting transfers between devices  39.8 us (21%)
  waiting for transfers between devices  27.8 us (15%)
  local copies, waits for them, and re-layouts  2.9 us (2%)
    pallas_call x24, Pallas kernels, run(): pl.pallas_call(ticking, in_specs=[in_smem] + specs + [in_hbm] * len(after...  60.4 us
    all_to_all x6, blocking collectives, to_all(): return lax.all_to_all(x, axes, split_axis=0, concat_axis=0, tiled=True)  56.1 us
    ppermute x34, starting transfers between devices, trade(): return lax.ppermute(x, axis, [(i, i ^ mask) for i in range(size)])  34.4 us
    ppermute x34, waiting for transfers between devices, trade(): return lax.ppermute(x, axis, [(i, i ^ mask) for i in range(size)])  26.7 us
    all_to_all x2, starting transfers between devices, to_all(): return lax.all_to_all(x, axes, split_axis=0, concat_axis=0, tiled=True)  5.39 us
  transfers between devices with their start and end apart: 36, of which 13 were waited for; matrix products, arithmetic and copies ran while one was open for 0% of the time, Pallas kernels for 8%

profile of v6, /device:TPU:0, one launch (start us, length us, event | category | flops | bytes accessed | tf_op | source)
XLA Modules:
  0.0 188.1 jit_solution(8613889433250935044)
XLA Ops:
  3.6 16.0 %all_to_all.40.refs_1_ = f32[32,2,640]{2,1,0:T(2,128)S(1)} all-to-all(f32[32,2,640]{2,1,0:T(2,128)S(1)} %get-tuple-element.117), channel_id=1, replica_groups=mesh['seq'=8,'batch'=4] {'seq','batch'}, dimensions={0} | all-to-all | bytes 327680 | tf_op jit(solution)/shard_map/all_to_all | solution.py:1063
  22.0 7.4 %all_to_all.41.refs_1_ = f32[8,4,512]{2,1,0:T(4,128)S(1)} all-to-all(f32[8,4,512]{2,1,0:T(4,128)S(1)} %get-tuple-element.120), channel_id=1, replica_groups=mesh['seq'=8,'batch'=4] {'seq'}, dimensions={0} | all-to-all | bytes 131072 | tf_op jit(solution)/shard_map/all_to_all | solution.py:1063
  29.4 6.3 %mix.2 = (f32[1024,512]{1,0:T(8,128)S(1)}, f32[32,2,512]{2,1,0:T(2,128)S(1)}, bf16[1024,2560]{1,0:T(8,128)(2,1)}, bf16[512,512]{1,0:T(8,128)(2,1)S(1)}, bf16[1024,512]{1,0:T(8,128)(2,1)}, /*index=5*/f32[8,128]{1,0:T(8,128)}) custom-call(s32[4]{0:T(128)S(1)} %copy-done.8, f32[8,4,512]{2,1,0:T(4,128)S(1)} %all_to_all.41.refs_1_, f32[2,512]{1,0:T(2,128)S(1)} %copy-done.9, ...), custom_call_target="tpu_custom_call" | custom-call | tf_op jit(solution)/shard_map/mix/pallas_call | solution.py:65
  35.7 10.1 %all_to_all.42.refs_1_ = f32[32,2,512]{2,1,0:T(2,128)S(1)} all-to-all(f32[32,2,512]{2,1,0:T(2,128)S(1)} %get-tuple-element.127), channel_id=1, replica_groups=mesh['seq'=8,'batch'=4] {'seq','batch'}, dimensions={0} | all-to-all | bytes 262144 | tf_op jit(solution)/shard_map/all_to_all | solution.py:1063
  47.8 7.4 %all_to_all.43.refs_1_ = f32[8,4,512]{2,1,0:T(4,128)S(1)} all-to-all(f32[8,4,512]{2,1,0:T(4,128)S(1)} %get-tuple-element.131), channel_id=1, replica_groups=mesh['seq'=8,'batch'=4] {'seq'}, dimensions={0} | all-to-all | bytes 131072 | tf_op jit(solution)/shard_map/all_to_all | solution.py:1063
  55.2 5.2 %mix.3 = (bf16[1024,512]{1,0:T(8,128)(2,1)S(1)}, bf16[1024,512]{1,0:T(8,128)(2,1)S(1)}, bf16[1024,512]{1,0:T(8,128)(2,1)S(1)}, bf16[1024,512]{1,0:T(8,128)(2,1)S...) custom-call(s32[4]{0:T(128)S(1)} %copy-done.8, ...), custom_call_target="tpu_custom_call" | custom-call | tf_op jit(solution)/shard_map/mix/pallas_call | solution.py:65
  60.4 3.4 %glu_back.2 = (bf16[1024,2560]{1,0:T(8,128)(2,1)S(1)}, f32[1,1024]{1,0:T(1,128)S(1)}, f32[1,512]{1,0:T(1,128)S(1)}, f32[4,32,128]{2,1,0:T(8,128)S(1)}, f32[8,4,5...) custom-call(s32[4]{0:T(128)S(1)} %copy-done.8, ...), custom_call_target="tpu_custom_call" | custom-call | tf_op jit(solution)/shard_map/glu_back/pallas_call | solution.py:65
  63.9 7.4 %all_to_all.44.refs_1_ = f32[8,4,512]{2,1,0:T(4,128)S(1)} all-to-all(f32[8,4,512]{2,1,0:T(4,128)S(1)} %get-tuple-element.145), channel_id=1, replica_groups=mesh['seq'=8,'batch'=4] {'seq'}, dimensions={0} | all-to-all | bytes 131072 | tf_op jit(solution)/shard_map/all_to_all | solution.py:1063
  71.3 4.0 %lift_back.2 = (bf16[1024,2048]{1,0:T(8,128)(2,1)S(1)}, f32[32,2,512]{2,1,0:T(2,128)}, f32[1,512]{1,0:T(1,128)S(1)}, f32[1,256]{1,0:T(1,128)S(1)}, f32[8,128]{1,0:T(8,128)}) custom-call(s32[4]{0:T(128)S(1)} %copy-done.8, f32[8,4,512]{2,1,0:T(4,128)S(1)} %all_to_all.44.refs_1_, f32[8,512]{1,0:T(8,128)S(1)} %get-tuple-element.146.refs_2_.refs_4_, ...), custom_call_target="tpu_custom_call" | custom-call | tf_op jit(solution)/shard_map/lift_back/pallas_call | solution.py:65
  75.2 3.9 %halves1.1 = (bf16[1088,512]{1,0:T(8,128)(2,1)S(1)}, bf16[1088,512]{1,0:T(8,128)(2,1)}, f32[8,128]{1,0:T(8,128)}) custom-call(s32[4]{0:T(128)S(1)} %copy-done.8, f32[1,512]{1,0:T(1,128)S(1)} %get-tuple-element.143.refs_1_, f32[1,1024]{1,0:T(1,128)S(1)} %get-tuple-element.144.refs_2_, f32[1,512]{1,0:T(1,128)S(1)} %get-tuple-element.151.refs_3_, ...), custom_call_target="tpu_custom_call" | custom-call | tf_op jit(solution)/shard_map/halves1/pallas_call | solution.py:65
  79.2 2.8 %all-to-all-start.5 = ((f32[32,2,512]{2,1,0:T(2,128)}), f32[32,2,512]{2,1,0:T(2,128)S(1)}, u32[]{:S(2)}, u32[]{:S(2)}) async-start(f32[32,2,512]{2,1,0:T(2,128)} %get-tuple-element.157), calls=%async_computation.5 | async-start | bytes 262144 | tf_op jit(solution)/shard_map/all_to_all | solution.py:1063
  92.4 5.8 %glu_back.3 = (bf16[1024,2560]{1,0:T(8,128)(2,1)S(1)}, f32[1,1024]{1,0:T(1,128)S(1)}, f32[1,512]{1,0:T(1,128)S(1)}, f32[4,32,128]{2,1,0:T(8,128)S(1)}, f32[8,4,5...) custom-call(s32[4]{0:T(128)S(1)} %copy-done.8, ...), custom_call_target="tpu_custom_call" | custom-call | tf_op jit(solution)/shard_map/glu_back/pallas_call | solution.py:65
  98.2 7.8 %all_to_all.45.refs_1_ = f32[8,4,512]{2,1,0:T(4,128)S(1)} all-to-all(f32[8,4,512]{2,1,0:T(4,128)S(1)} %get-tuple-element.160), channel_id=1, replica_groups=mesh['seq'=8,'batch'=4] {'seq'}, dimensions={0} | all-to-all | bytes 131072 | tf_op jit(solution)/shard_map/all_to_all | solution.py:1063
  106.6 4.5 %lift_back.3 = (bf16[1024,512]{1,0:T(8,128)(2,1)S(1)}, f32[32,2,512]{2,1,0:T(2,128)}, f32[1,512]{1,0:T(1,128)S(1)}, f32[1,256]{1,0:T(1,128)S(1)}, bf16[1024,512]...) custom-call(s32[4]{0:T(128)S(1)} %copy-done.8, f32[8,4,512]{2,1,0:T(4,128)S(1)} %get-tuple-element.168.refs_1_, ...), custom_call_target="tpu_custom_call" | custom-call | tf_op jit(solution)/shard_map/lift_back/pallas_call | solution.py:65
  111.0 2.9 %halves0.1 = (bf16[1088,512]{1,0:T(8,128)(2,1)S(1)}, bf16[1088,512]{1,0:T(8,128)(2,1)S(1)}, f32[8,128]{1,0:T(8,128)}) custom-call(s32[4]{0:T(128)S(1)} %copy-done.8, f32[1,512]{1,0:T(1,128)S(1)} %get-tuple-element.179.refs_1_, f32[1,1024]{1,0:T(1,128)S(1)} %get-tuple-element.180.refs_2_, f32[1,512]{1,0:T(1,128)S(1)} %get-tuple-element.181.refs_3_, ...), custom_call_target="tpu_custom_call" | custom-call | tf_op jit(solution)/shard_map/halves0/pallas_call | solution.py:65
  116.4 2.5 %collective-permute-start.5 = (bf16[80,512]{1,0:T(8,128)(2,1)S(1)}, bf16[80,512]{1,0:T(8,128)(2,1)S(1)}, u32[]{:S(2)}, u32[]{:S(2)}) collective-permute-start(bf16[80,512]{1,0:T(8,128)(2,1)S(1)} %get-tuple-element.188), channel_id=1, source_target_pairs={{0,2},{1,3},{2,0},{3,1},{4,6},{5,7},{6,4},{7,5},{8,10},{9,11},{10,... | collective-permute-start | bytes 245768 | tf_op jit(solution)/shard_map/ppermute | solution.py:897
  126.5 2.6 %collective-permute-start.13 = (bf16[80,512]{1,0:T(8,128)(2,1)S(1)}, bf16[80,512]{1,0:T(8,128)(2,1)S(1)}, u32[]{:S(2)}, u32[]{:S(2)}) collective-permute-start(bf16[80,512]{1,0:T(8,128)(2,1)S(1)} %get-tuple-element.200.refs_1_), channel_id=1, source_target_pairs={{0,3},{1,2},{2,1},{3,0},{4,7},{5,6},{6,5},{7,4},{8,11},{9,10},{10,... | collective-permute-start | bytes 245768 | tf_op jit(solution)/shard_map/ppermute | solution.py:897
  129.8 4.1 %collective-permute-done.13.refs_4_ = bf16[80,512]{1,0:T(8,128)(2,1)S(1)} collective-permute-done((bf16[80,512]{1,0:T(8,128)(2,1)S(1)}, bf16[80,512]{1,0:T(8,128)(2,1)S(1)}, u32[]{:S(2)}, u32[]{:S(2)}) %collective-permute-start.13) | collective-permute-done | bytes 81952 | tf_op jit(solution)/shard_map/ppermute | solution.py:897
  146.7 4.5 %collective-permute-done.15.refs_3_ = bf16[80,512]{1,0:T(8,128)(2,1)S(1)} collective-permute-done((bf16[80,512]{1,0:T(8,128)(2,1)S(1)}, bf16[80,512]{1,0:T(8,128)(2,1)S(1)}, u32[]{:S(2)}, u32[]{:S(2)}) %collective-permute-start.15) | collective-permute-done | bytes 81952 | tf_op jit(solution)/shard_map/ppermute | solution.py:897
  155.2 2.5 %collective-permute-start.17 = (bf16[80,512]{1,0:T(8,128)(2,1)S(1)}, bf16[80,512]{1,0:T(8,128)(2,1)S(1)}, u32[]{:S(2)}, u32[]{:S(2)}) collective-permute-start(bf16[80,512]{1,0:T(8,128)(2,1)S(1)} %get-tuple-element.206.refs_1_), channel_id=1, source_target_pairs={{0,1},{1,0},{2,3},{3,2},{4,5},{5,4},{6,7},{7,6},{8,9},{9,8},{10,11... | collective-permute-start | bytes 245768 | tf_op jit(solution)/shard_map/ppermute | solution.py:897
  166.1 2.6 %all-to-all-start.7 = ((f32[32,2,512]{2,1,0:T(2,128)}), f32[32,2,512]{2,1,0:T(2,128)S(1)}, u32[]{:S(2)}, u32[]{:S(2)}) async-start(f32[32,2,512]{2,1,0:T(2,128)} %get-tuple-element.195), calls=%async_computation.7 | async-start | bytes 262144 | tf_op jit(solution)/shard_map/all_to_all | solution.py:1063
  169.3 3.2 %collective-permute-done.22.refs_12_ = bf16[272,512]{1,0:T(8,128)(2,1)S(1)} collective-permute-done((bf16[272,512]{1,0:T(8,128)(2,1)S(1)}, bf16[272,512]{1,0:T(8,128)(2,1)S(1)}, u32[]{:S(2)}, u32[]{:S(2)}) %collective-permute-start.22) | collective-permute-done | bytes 278560 | tf_op jit(solution)/shard_map/ppermute | solution.py:897
  172.5 6.0 %collective-permute-done.21.refs_11_ = bf16[272,512]{1,0:T(8,128)(2,1)S(1)} collective-permute-done((bf16[272,512]{1,0:T(8,128)(2,1)S(1)}, bf16[272,512]{1,0:T(8,128)(2,1)S(1)}, u32[]{:S(2)}, u32[]{:S(2)}) %collective-permute-start.21) | collective-permute-done | bytes 278560 | tf_op jit(solution)/shard_map/ppermute | solution.py:897
  180.6 7.3 %results.1 = (f32[2,512,1024]{2,1,0:T(8,128)}, f32[2,512,512]{2,1,0:T(8,128)}, f32[2,512,512]{2,1,0:T(8,128)}, bf16[4,256,512]{2,1,0:T(8,128)(2,1)}, f32[2,512]{...) custom-call(s32[4]{0:T(128)S(1)} %copy-done.8, ...), custom_call_target="tpu_custom_call" | custom-call | flops 7699999744 | bytes 21000000 | tf_op jit(solution)/shard_map/results/pallas_call | solution.py:65
  (102 shorter events, 56.7 us)
Async XLA Ops:
  79.2 11.1 %all-to-all-start.5 = ((f32[32,2,512]{2,1,0:T(2,128)}), f32[32,2,512]{2,1,0:T(2,128)S(1)}, u32[]{:S(2)}, u32[]{:S(2)}) async-start(f32[32,2,512]{2,1,0:T(2,128)} %get-tuple-element.157), calls=%async_computation.5 | async-start | bytes 262144 | tf_op jit(solution)/shard_map/all_to_all | solution.py:1063
  86.1 19.9 %collective-permute-start.1 = (bf16[272,512]{1,0:T(8,128)(2,1)}, bf16[272,512]{1,0:T(8,128)(2,1)S(1)}, u32[]{:S(2)}, u32[]{:S(2)}) collective-permute-start(bf16[272,512]{1,0:T(8,128)(2,1)} %get-tuple-element.165), channel_id=1, source_target_pairs={{0,8},{4,12},{8,0},{12,4},{16,24},{20,28},{24,16},{28,20},{1,9},{5... | collective-permute-start | bytes 835592 | tf_op jit(solution)/shard_map/ppermute | solution.py:897
  87.5 18.5 %collective-permute-start.2 = (bf16[272,512]{1,0:T(8,128)(2,1)S(1)}, bf16[272,512]{1,0:T(8,128)(2,1)S(1)}, u32[]{:S(2)}, u32[]{:S(2)}) collective-permute-start(bf16[272,512]{1,0:T(8,128)(2,1)S(1)} %get-tuple-element.166), channel_id=1, source_target_pairs={{0,16},{4,20},{8,24},{12,28},{16,0},{20,4},{24,8},{28,12},{1,17},{... | collective-permute-start | bytes 835592 | tf_op jit(solution)/shard_map/ppermute | solution.py:897
  89.0 17.0 %collective-permute-start.3 = (bf16[272,512]{1,0:T(8,128)(2,1)S(1)}, bf16[272,512]{1,0:T(8,128)(2,1)S(1)}, u32[]{:S(2)}, u32[]{:S(2)}) collective-permute-start(bf16[272,512]{1,0:T(8,128)(2,1)S(1)} %get-tuple-element.167), channel_id=1, source_target_pairs={{0,24},{4,28},{8,16},{12,20},{16,8},{20,12},{24,0},{28,4},{1,25},{... | collective-permute-start | bytes 835592 | tf_op jit(solution)/shard_map/ppermute | solution.py:897
  116.4 9.5 %collective-permute-start.5 = (bf16[80,512]{1,0:T(8,128)(2,1)S(1)}, bf16[80,512]{1,0:T(8,128)(2,1)S(1)}, u32[]{:S(2)}, u32[]{:S(2)}) collective-permute-start(bf16[80,512]{1,0:T(8,128)(2,1)S(1)} %get-tuple-element.188), channel_id=1, source_target_pairs={{0,2},{1,3},{2,0},{3,1},{4,6},{5,7},{6,4},{7,5},{8,10},{9,11},{10,... | collective-permute-start | bytes 245768 | tf_op jit(solution)/shard_map/ppermute | solution.py:897
  120.1 21.3 %collective-permute-start.8 = (bf16[272,512]{1,0:T(8,128)(2,1)S(1)}, bf16[272,512]{1,0:T(8,128)(2,1)S(1)}, u32[]{:S(2)}, u32[]{:S(2)}) collective-permute-start(bf16[272,512]{1,0:T(8,128)(2,1)S(1)} %get-tuple-element.197), channel_id=1, source_target_pairs={{0,8},{4,12},{8,0},{12,4},{16,24},{20,28},{24,16},{28,20},{1,9},{5... | collective-permute-start | bytes 835592 | tf_op jit(solution)/shard_map/ppermute | solution.py:897
  120.7 20.6 %collective-permute-start.9 = (bf16[272,512]{1,0:T(8,128)(2,1)S(1)}, bf16[272,512]{1,0:T(8,128)(2,1)S(1)}, u32[]{:S(2)}, u32[]{:S(2)}) collective-permute-start(bf16[272,512]{1,0:T(8,128)(2,1)S(1)} %get-tuple-element.198), channel_id=1, source_target_pairs={{0,16},{4,20},{8,24},{12,28},{16,0},{20,4},{24,8},{28,12},{1,17},{... | collective-permute-start | bytes 835592 | tf_op jit(solution)/shard_map/ppermute | solution.py:897
  121.3 20.1 %collective-permute-start.10 = (bf16[272,512]{1,0:T(8,128)(2,1)S(1)}, bf16[272,512]{1,0:T(8,128)(2,1)S(1)}, u32[]{:S(2)}, u32[]{:S(2)}) collective-permute-start(bf16[272,512]{1,0:T(8,128)(2,1)S(1)} %get-tuple-element.199), channel_id=1, source_target_pairs={{0,24},{4,28},{8,16},{12,20},{16,8},{20,12},{24,0},{28,4},{1,25},{... | collective-permute-start | bytes 835592 | tf_op jit(solution)/shard_map/ppermute | solution.py:897
  126.5 7.3 %collective-permute-start.13 = (bf16[80,512]{1,0:T(8,128)(2,1)S(1)}, bf16[80,512]{1,0:T(8,128)(2,1)S(1)}, u32[]{:S(2)}, u32[]{:S(2)}) collective-permute-start(bf16[80,512]{1,0:T(8,128)(2,1)S(1)} %get-tuple-element.200.refs_1_), channel_id=1, source_target_pairs={{0,3},{1,2},{2,1},{3,0},{4,7},{5,6},{6,5},{7,4},{8,11},{9,10},{10,... | collective-permute-start | bytes 245768 | tf_op jit(solution)/shard_map/ppermute | solution.py:897
  129.2 7.4 %collective-permute-start.12 = (bf16[80,512]{1,0:T(8,128)(2,1)S(1)}, bf16[80,512]{1,0:T(8,128)(2,1)S(1)}, u32[]{:S(2)}, u32[]{:S(2)}) collective-permute-start(bf16[80,512]{1,0:T(8,128)(2,1)S(1)} %get-tuple-element.200.refs_1_), channel_id=1, source_target_pairs={{0,2},{1,3},{2,0},{3,1},{4,6},{5,7},{6,4},{7,5},{8,10},{9,11},{10,... | collective-permute-start | bytes 245768 | tf_op jit(solution)/shard_map/ppermute | solution.py:897
  139.3 15.9 %collective-permute-start.29 = (bf16[272,512]{1,0:T(8,128)(2,1)S(1)}, bf16[272,512]{1,0:T(8,128)(2,1)S(1)}, u32[]{:S(2)}, u32[]{:S(2)}) collective-permute-start(bf16[272,512]{1,0:T(8,128)(2,1)S(1)} %get-tuple-element.212.refs_17_), channel_id=1, source_target_pairs={{0,24},{4,28},{8,16},{12,20},{16,8},{20,12},{24,0},{28,4},{1,25},{... | collective-permute-start | bytes 835592 | tf_op jit(solution)/shard_map/ppermute | solution.py:897
  139.9 15.3 %collective-permute-start.28 = (bf16[272,512]{1,0:T(8,128)(2,1)S(1)}, bf16[272,512]{1,0:T(8,128)(2,1)S(1)}, u32[]{:S(2)}, u32[]{:S(2)}) collective-permute-start(bf16[272,512]{1,0:T(8,128)(2,1)S(1)} %get-tuple-element.212.refs_17_), channel_id=1, source_target_pairs={{0,16},{4,20},{8,24},{12,28},{16,0},{20,4},{24,8},{28,12},{1,17},{... | collective-permute-start | bytes 835592 | tf_op jit(solution)/shard_map/ppermute | solution.py:897
  144.8 7.9 %collective-permute-start.16 = (bf16[80,512]{1,0:T(8,128)(2,1)S(1)}, bf16[80,512]{1,0:T(8,128)(2,1)S(1)}, u32[]{:S(2)}, u32[]{:S(2)}) collective-permute-start(bf16[80,512]{1,0:T(8,128)(2,1)S(1)} %get-tuple-element.205), channel_id=1, source_target_pairs={{0,3},{1,2},{2,1},{3,0},{4,7},{5,6},{6,5},{7,4},{8,11},{9,10},{10,... | collective-permute-start | bytes 245768 | tf_op jit(solution)/shard_map/ppermute | solution.py:897
  146.7 15.9 %collective-permute-start.30 = (bf16[272,512]{1,0:T(8,128)(2,1)S(1)}, bf16[272,512]{1,0:T(8,128)(2,1)S(1)}, u32[]{:S(2)}, u32[]{:S(2)}) collective-permute-start(bf16[272,512]{1,0:T(8,128)(2,1)S(1)} %get-tuple-element.212.refs_17_), channel_id=1, source_target_pairs={{0,4},{4,0},{8,12},{12,8},{16,20},{20,16},{24,28},{28,24},{1,5},{5... | collective-permute-start | bytes 835592 | tf_op jit(solution)/shard_map/ppermute | solution.py:897
  151.2 12.8 %collective-permute-start.27 = (bf16[272,512]{1,0:T(8,128)(2,1)S(1)}, bf16[272,512]{1,0:T(8,128)(2,1)S(1)}, u32[]{:S(2)}, u32[]{:S(2)}) collective-permute-start(bf16[272,512]{1,0:T(8,128)(2,1)S(1)} %get-tuple-element.212.refs_17_), channel_id=1, source_target_pairs={{0,8},{4,12},{8,0},{12,4},{16,24},{20,28},{24,16},{28,20},{1,9},{5... | collective-permute-start | bytes 835592 | tf_op jit(solution)/shard_map/ppermute | solution.py:897
  159.6 9.1 %collective-permute-start.33 = (bf16[272,512]{1,0:T(8,128)(2,1)S(1)}, bf16[272,512]{1,0:T(8,128)(2,1)S(1)}, u32[]{:S(2)}, u32[]{:S(2)}) collective-permute-start(bf16[272,512]{1,0:T(8,128)(2,1)S(1)} %collective-permute-done.29.refs_20_), channel_id=1, source_target_pairs={{0,4},{4,0},{8,12},{12,8},{16,20},{20,16},{24,28},{28,24},{1,5},{5... | collective-permute-start | bytes 835592 | tf_op jit(solution)/shard_map/ppermute | solution.py:897
  161.3 7.5 %collective-permute-start.32 = (bf16[272,512]{1,0:T(8,128)(2,1)S(1)}, bf16[272,512]{1,0:T(8,128)(2,1)S(1)}, u32[]{:S(2)}, u32[]{:S(2)}) collective-permute-start(bf16[272,512]{1,0:T(8,128)(2,1)S(1)} %collective-permute-done.28.refs_19_), channel_id=1, source_target_pairs={{0,4},{4,0},{8,12},{12,8},{16,20},{20,16},{24,28},{28,24},{1,5},{5... | collective-permute-start | bytes 835592 | tf_op jit(solution)/shard_map/ppermute | solution.py:897
  162.0 10.5 %collective-permute-start.22 = (bf16[272,512]{1,0:T(8,128)(2,1)S(1)}, bf16[272,512]{1,0:T(8,128)(2,1)S(1)}, u32[]{:S(2)}, u32[]{:S(2)}) collective-permute-start(bf16[272,512]{1,0:T(8,128)(2,1)S(1)} %get-tuple-element.211.refs_9_), channel_id=1, source_target_pairs={{0,24},{4,28},{8,16},{12,20},{16,8},{20,12},{24,0},{28,4},{1,25},{... | collective-permute-start | bytes 835592 | tf_op jit(solution)/shard_map/ppermute | solution.py:897
  162.6 15.9 %collective-permute-start.21 = (bf16[272,512]{1,0:T(8,128)(2,1)S(1)}, bf16[272,512]{1,0:T(8,128)(2,1)S(1)}, u32[]{:S(2)}, u32[]{:S(2)}) collective-permute-start(bf16[272,512]{1,0:T(8,128)(2,1)S(1)} %get-tuple-element.211.refs_9_), channel_id=1, source_target_pairs={{0,16},{4,20},{8,24},{12,28},{16,0},{20,4},{24,8},{28,12},{1,17},{... | collective-permute-start | bytes 835592 | tf_op jit(solution)/shard_map/ppermute | solution.py:897
  164.1 14.4 %collective-permute-start.20 = (bf16[272,512]{1,0:T(8,128)(2,1)S(1)}, bf16[272,512]{1,0:T(8,128)(2,1)S(1)}, u32[]{:S(2)}, u32[]{:S(2)}) collective-permute-start(bf16[272,512]{1,0:T(8,128)(2,1)S(1)} %get-tuple-element.211.refs_9_), channel_id=1, source_target_pairs={{0,8},{4,12},{8,0},{12,4},{16,24},{20,28},{24,16},{28,20},{1,9},{5... | collective-permute-start | bytes 835592 | tf_op jit(solution)/shard_map/ppermute | solution.py:897
  166.1 13.3 %all-to-all-start.7 = ((f32[32,2,512]{2,1,0:T(2,128)}), f32[32,2,512]{2,1,0:T(2,128)S(1)}, u32[]{:S(2)}, u32[]{:S(2)}) async-start(f32[32,2,512]{2,1,0:T(2,128)} %get-tuple-element.195), calls=%async_computation.7 | async-start | bytes 262144 | tf_op jit(solution)/shard_map/all_to_all | solution.py:1063
  168.7 11.3 %collective-permute-start.31 = (bf16[272,512]{1,0:T(8,128)(2,1)S(1)}, bf16[272,512]{1,0:T(8,128)(2,1)}, u32[]{:S(2)}, u32[]{:S(2)}) collective-permute-start(bf16[272,512]{1,0:T(8,128)(2,1)S(1)} %collective-permute-done.27.refs_18_), channel_id=1, source_target_pairs={{0,4},{4,0},{8,12},{12,8},{16,20},{20,16},{24,28},{28,24},{1,5},{5... | collective-permute-start | bytes 835592 | tf_op jit(solution)/shard_map/ppermute | solution.py:897
  168.9 11.2 %collective-permute-start.23 = (bf16[272,512]{1,0:T(8,128)(2,1)S(1)}, bf16[272,512]{1,0:T(8,128)(2,1)}, u32[]{:S(2)}, u32[]{:S(2)}) collective-permute-start(bf16[272,512]{1,0:T(8,128)(2,1)S(1)} %get-tuple-element.211.refs_9_), channel_id=1, source_target_pairs={{0,4},{4,0},{8,12},{12,8},{16,20},{20,16},{24,28},{28,24},{1,5},{5... | collective-permute-start | bytes 835592 | tf_op jit(solution)/shard_map/ppermute | solution.py:897
  172.5 7.6 %collective-permute-start.26 = (bf16[272,512]{1,0:T(8,128)(2,1)S(1)}, bf16[272,512]{1,0:T(8,128)(2,1)}, u32[]{:S(2)}, u32[]{:S(2)}) collective-permute-start(bf16[272,512]{1,0:T(8,128)(2,1)S(1)} %collective-permute-done.22.refs_12_), channel_id=1, source_target_pairs={{0,4},{4,0},{8,12},{12,8},{16,20},{20,16},{24,28},{28,24},{1,5},{5... | collective-permute-start | bytes 835592 | tf_op jit(solution)/shard_map/ppermute | solution.py:897
  (24 other events, 192.1 us)
